TPU v7x, 32 devices: a whole 2x2x4 slice. The times are simulated.
32 devices in a mesh: grp: 2 (over x), seq: 16 (over z, y, core).
Axes of the slice: x: 2, y: 2, z: 4, core: 2. Of those that a mesh axis runs over, the one named last changes fastest.
Arguments:
- queries: bfloat16 [4096, 3072], P(('grp', 'seq')), parts along dimension 0, may hold values from -6 to 6
- keys: bfloat16 [4096, 3072], P(('grp', 'seq')), parts along dimension 0, may hold values from -6 to 6
- values: bfloat16 [4096, 3072], P(('grp', 'seq')), parts along dimension 0, may hold values from -6 to 6
- text_keys: bfloat16 [512, 3072], P('grp'), parts along dimension 0, may hold values from -6 to 6
- text_values: bfloat16 [512, 3072], P('grp'), parts along dimension 0, may hold values from -6 to 6
- text_len: int32 [2], P('grp'), parts along dimension 0, may hold values from 64 to 256
- plan: int32 [12], P('grp'), parts along dimension 0, may hold values from 0 to 9
- deltas: bfloat16 [6, 4096, 3072], P(None, ('grp', 'seq')), parts along dimension 1, may hold values from -2 to 2
Outputs:
- mixed: bfloat16 [4096, 3072], P(('grp', 'seq')), parts along dimension 0
There are 2 independent parts, one for each index of `grp`. A program takes and returns all parts, laid end to end along the dimension named above; each array names one. Nothing has to cross between parts.
All inputs are finite; a program needn't handle non-finite values.
Results may differ from a plain program's by a relative error of at most 0.0034.
Values may be sent and summed in bfloat16 or wider, within the bound.
No kernel may reach another device: no remote copies, remote signals or barrier semaphores. Data moves between devices by JAX's collectives and lax.ppermute only.
A program may use at most 128 MiB of HBM per device.

v0:
```python
import jax
import jax.numpy as jnp
from jax import lax
from jax.sharding import PartitionSpec as P

HEADS = 24
HEAD_DIM = 128
HEADS_DEV = 3


def attend(head_queries, head_keys, head_values, group_token_keys, group_tv, usable):
    query_rows = head_queries.shape[0]
    score_scale = HEAD_DIM ** (-0.5)
    reshaped_queries = head_queries.reshape(query_rows, HEADS_DEV, HEAD_DIM)

    def compute_scores(current_key_block):
        return (
            jnp.einsum(
                "qgp,ugp->gqu",
                reshaped_queries,
                current_key_block,
                preferred_element_type=jnp.float32,
            )
            * score_scale
        )

    text_scores = compute_scores(group_token_keys.reshape(-1, HEADS_DEV, HEAD_DIM))
    text_scores = jnp.where(usable[None, None, :], text_scores, -jnp.inf)
    row_top = jnp.max(text_scores, axis=-1)
    text_exp = jnp.exp(text_scores - row_top[..., None])
    denominator = jnp.sum(text_exp, axis=-1)
    weighted = jnp.einsum(
        "vie,evs->vis",
        text_exp.astype(jnp.bfloat16),
        group_tv.reshape(-1, HEADS_DEV, HEAD_DIM),
        preferred_element_type=jnp.float32,
    )
    key_total = head_keys.shape[0]
    current_key_block = 2048
    block_keys = head_keys.reshape(
        key_total // current_key_block, current_key_block, HEADS_DEV, HEAD_DIM
    )
    block_values = head_values.reshape(
        key_total // current_key_block, current_key_block, HEADS_DEV, HEAD_DIM
    )

    def advance(carry, blocks):
        old_top, old_denominator, old_weighted = carry
        local_keys, values_here = blocks
        block_scores = compute_scores(local_keys)
        new_top = jnp.maximum(old_top, jnp.max(block_scores, axis=-1))
        running_rescale = jnp.exp(old_top - new_top)
        block_exp = jnp.exp(block_scores - new_top[..., None])
        new_denominator = old_denominator * running_rescale + jnp.sum(block_exp, axis=-1)
        new_weighted = old_weighted * running_rescale[..., None] + jnp.einsum(
            "vie,evs->vis",
            block_exp.astype(jnp.bfloat16),
            values_here,
            preferred_element_type=jnp.float32,
        )
        return ((new_top, new_denominator, new_weighted), None)

    (row_top, denominator, weighted), unused = lax.scan(
        advance, (row_top, denominator, weighted), (block_keys, block_values)
    )
    context = weighted / denominator[..., None]
    return context.transpose(1, 0, 2).reshape(query_rows, HEADS_DEV * HEAD_DIM).astype(jnp.bfloat16)


def body(queries, keys, values, text_keys, text_values, text_len, plan, deltas):
    tok_rows, feat_width = queries.shape
    axis_count = lax.axis_size("seq")
    head_groups = HEADS // HEADS_DEV
    query_pieces = axis_count // head_groups
    slot_width = HEADS_DEV * HEAD_DIM

    def replicate_slots(array):
        spread = jnp.broadcast_to(array[:, None, :], (tok_rows, query_pieces, feat_width))
        return spread.reshape(tok_rows, query_pieces * feat_width)

    head_queries = lax.all_to_all(
        queries.reshape(tok_rows // query_pieces, query_pieces * feat_width),
        "seq",
        split_axis=1,
        concat_axis=0,
        tiled=True,
    )
    head_keys = lax.all_to_all(
        replicate_slots(keys), "seq", split_axis=1, concat_axis=0, tiled=True
    )
    head_values = lax.all_to_all(
        replicate_slots(values), "seq", split_axis=1, concat_axis=0, tiled=True
    )
    group_index = lax.axis_index("seq") % head_groups
    group_token_keys = lax.dynamic_slice_in_dim(text_keys, group_index * slot_width, slot_width, 1)
    group_tv = lax.dynamic_slice_in_dim(text_values, group_index * slot_width, slot_width, 1)
    usable = jnp.arange(text_keys.shape[0]) < text_len[0]
    context = attend(head_queries, head_keys, head_values, group_token_keys, group_tv, usable)
    returned = lax.all_to_all(context, "seq", split_axis=0, concat_axis=1, tiled=True)
    context_rows = returned.reshape(tok_rows, feat_width)
    added = (
        jnp.einsum(
            "b,btc->tc", plan.astype(jnp.bfloat16), deltas, preferred_element_type=jnp.float32
        )
        * 0.25
    )
    return (context_rows.astype(jnp.float32) + added).astype(jnp.bfloat16)


def solution(mesh):
    return jax.shard_map(
        body,
        mesh=mesh,
        in_specs=(
            P(("grp", "seq"), None),
            P(("grp", "seq"), None),
            P(("grp", "seq"), None),
            P("grp", None),
            P("grp", None),
            P("grp"),
            P("grp"),
            P(None, ("grp", "seq"), None),
        ),
        out_specs=P(("grp", "seq"), None),
        check_vma=False,
    )
```

profile of v0, /device:TPU:0, one launch (start us, length us, event | category | flops | bytes accessed | tf_op | source)
XLA Modules:
  0.0 167.6 jit_solution(10132103594488439020)
XLA Ops:
  0.0 1.5 all_to_all.44
  1.5 1.1 copy.22
  2.6 7.4 %all-to-all-start = ((bf16[64,16,384]{2,0,1:T(8,128)(2,1)}), bf16[64,16,384]{2,0,1:T(8,128)(2,1)S(1)}, u32[]{:S(2)}, u32[]{:S(2)}) async-start(bf16[64,16,384]{2,0,1:T(8,128)(2,1)} %copy.22), calls=%async_computation | async-start | bytes 1572864 | tf_op jit(solution)/shard_map/all_to_all | solution.py:81
  10.4 18.3 %all-to-all-done = bf16[64,16,384]{2,0,1:T(8,128)(2,1)S(1)} async-done(((bf16[64,16,384]{2,0,1:T(8,128)(2,1)}), bf16[64,16,384]{2,0,1:T(8,128)(2,1)S(1)}, u32[]{:S(2)}, u32[]{:S(2)}) %all-to-all-start) | async-done | bytes 786464 | tf_op jit(solution)/shard_map/all_to_all | solution.py:81
  28.7 1.3 broadcast_in_dim.22
  30.0 5.5 %all-to-all-start.1 = ((bf16[128,16,384]{0,2,1:T(8,128)(2,1)}), bf16[128,16,384]{0,2,1:T(8,128)(2,1)S(1)}, u32[]{:S(2)}, u32[]{:S(2)}) async-start(bf16[128,16,384]{0,2,1:T(8,128)(2,1)} %bitcast.7), calls=%async_computation.1 | async-start | bytes 3145728 | tf_op jit(solution)/shard_map/all_to_all | solution.py:88
  35.4 1.5 copy.32
  37.0 30.5 %all-to-all-done.1 = bf16[128,16,384]{0,2,1:T(8,128)(2,1)S(1)} async-done(((bf16[128,16,384]{0,2,1:T(8,128)(2,1)}), bf16[128,16,384]{0,2,1:T(8,128)(2,1)S(1)}, u32[]{:S(2)}, u32[]{:S(2)}) %all-to-all-start.1) | async-done | bytes 1572896 | tf_op jit(solution)/shard_map/all_to_all | solution.py:88
  67.4 1.4 broadcast_in_dim.34
  69.1 9.1 %all-to-all-start.2 = ((bf16[128,16,384]{0,2,1:T(8,128)(2,1)}), bf16[128,16,384]{0,2,1:T(8,128)(2,1)S(1)}, u32[]{:S(2)}, u32[]{:S(2)}) async-start(bf16[128,16,384]{0,2,1:T(8,128)(2,1)} %bitcast.10), calls=%async_computation.2 | async-start | bytes 3145728 | tf_op jit(solution)/shard_map/all_to_all | solution.py:91
  78.2 1.1 constant_dynamic-slice_fusion
  81.8 1.8 %bitcast_reduce_fusion = (f32[3,1024]{1,0:T(4,128)S(1)}, f32[3,256,1024]{2,1,0:T(8,128)S(1)}) fusion(pred[256]{0:T(512)(128)(4,1)S(1)} %iota_compare_fusion, bf16[256,3,128]{0,2,1:T(8,128)(2,1)} %bitcast.63, bf16[1024,3,128]{2,1,0:T(4,128)(2,1)S(1)} %reshape.70), kind=kOutput, calls=%fused_computation.8 | convolution fusion | flops 203682816 | bytes 4141312 | tf_op jit(solution)/shard_map/qgp,ugp->gqu/dot_general | solution.py:18
  84.4 2.2 %fusion.9 = f32[3,1024,128]{2,1,0:T(8,128)} fusion(bf16[256,3,128]{0,2,1:T(8,128)(2,1)S(1)} %bitcast.64, f32[3,256,1024]{2,1,0:T(8,128)S(1)} %get-tuple-element.20, f32[3,1024]{1,0:T(4,128)S(1)} %get-tuple-element.19, pred[256]{0:T(512)(128)(4,1)S(1)} %iota_compare_fusion), kind=kOutput, calls=%fused_computation.13 | convolution fusion | flops 204472320 | bytes 4927744 | tf_op jit(solution)/shard_map/vie,evs->vis/dot_general | solution.py:32
  86.6 2.2 %copy.29 = bf16[16,128,384]{1,0,2:T(8,128)(2,1)} copy(bf16[16,128,384]{1,2,0:T(8,128)(2,1)S(1)} %bitcast.61) | data formatting | bytes 3145728 | tf_op jit(solution)/shard_map/all_to_all | solution.py:88
  88.8 3.7 %squeeze.13 = bf16[2048,3,128]{0,2,1:T(8,128)(2,1)} reshape(bf16[16,128,384]{1,0,2:T(8,128)(2,1)} %copy.29) | data formatting | bytes 3145728 | tf_op jit(solution)/shard_map/while/body/jit(dynamic_index_in_dim)/squeeze | solution.py:63
  92.5 11.6 %multiply_reduce_fusion = (f32[3,1024]{1,0:T(4,128)S(1)}, f32[3,1024,2048]{2,1,0:T(8,128)}) fusion(bf16[2048,3,128]{0,2,1:T(8,128)(2,1)} %squeeze.13, bf16[1024,3,128]{2,1,0:T(4,128)(2,1)S(1)} %reshape.70), kind=kOutput, calls=%fused_computation.1 | convolution fusion | flops 1623192576 | bytes 27537408 | tf_op jit(solution)/shard_map/while/body/eval_jaxpr/qgp,ugp->gqu/dot_general | solution.py:18
  104.1 6.1 %all-to-all-done.2 = bf16[128,16,384]{0,2,1:T(8,128)(2,1)S(1)} async-done(((bf16[128,16,384]{0,2,1:T(8,128)(2,1)}), bf16[128,16,384]{0,2,1:T(8,128)(2,1)S(1)}, u32[]{:S(2)}, u32[]{:S(2)}) %all-to-all-start.2) | async-done | bytes 1572896 | tf_op jit(solution)/shard_map/all_to_all | solution.py:91
  111.9 10.9 %fusion = f32[3,1024]{1,0:T(4,128)S(1)} fusion(f32[3,1024,2048]{2,1,0:T(8,128)} %get-tuple-element.30, f32[3,1024]{1,0:T(4,128)S(1)} %max.19), kind=kLoop, calls=%fused_computation.2 | loop fusion | flops 18871296 | bytes 25190400 | tf_op jit(solution)/shard_map/while/body/eval_jaxpr/reduce_sum | solution.py:54
  122.9 10.6 %fusion.14 = bf16[1024,3,128]{2,0,1:T(8,128)(2,1)S(1)} fusion(f32[3,1024,128]{2,1,0:T(8,128)S(1)} %copy-done.2, bf16[2048,3,128]{0,2,1:T(8,128)(2,1)S(1)} %squeeze.14, f32[3,1024,2048]{2,1,0:T(8,128)} %get-tuple-element.30, f32[3,1024]{1,0:T(4,128)S(1)} %max.19, f32[1024,3]{0,1:T(4,128)S(1)} %get-tuple-element.17, f32[1024,3]{0,1:T(4,128)S(1)} %get-tuple-element.18), kind=kOutput, calls=%fused_computation.19 | convolution fusion | flops 1631059968 | bytes 29134848 | tf_op jit(solution)/shard_map/while/body/eval_jaxpr/vie,evs->vis/dot_general | solution.py:55
  134.2 1.6 convert_element_type.32
  135.8 9.1 %all-to-all-start.3 = ((bf16[16,64,384]{2,1,0:T(8,128)(2,1)}), bf16[16,64,384]{2,1,0:T(8,128)(2,1)S(1)}, u32[]{:S(2)}, u32[]{:S(2)}) async-start(bf16[16,64,384]{2,1,0:T(8,128)(2,1)} %convert_element_type.32), calls=%async_computation.3 | async-start | bytes 1572864 | tf_op jit(solution)/shard_map/all_to_all | solution.py:99
  144.9 7.3 %fusion.4 = f32[1,128,3072]{2,0,1:T(1,128)} fusion(bf16[6,128,3072]{2,1,0:T(8,128)(2,1)} %param.15, s32[6]{0:T(128)S(1)} %copy-done.5), kind=kOutput, calls=%fused_computation.5 | convolution fusion | flops 4718598 | bytes 6291480 | tf_op jit(solution)/shard_map/b,btc->tc/dot_general | solution.py:102
  152.2 11.4 %all-to-all-done.3 = bf16[16,64,384]{2,1,0:T(8,128)(2,1)S(1)} async-done(((bf16[16,64,384]{2,1,0:T(8,128)(2,1)}), bf16[16,64,384]{2,1,0:T(8,128)(2,1)S(1)}, u32[]{:S(2)}, u32[]{:S(2)}) %all-to-all-start.3) | async-done | bytes 786464 | tf_op jit(solution)/shard_map/all_to_all | solution.py:99
  165.0 2.6 %fusion.12 = bf16[128,3072]{1,0:T(8,128)(2,1)} fusion(f32[128,3072]{1,0:T(8,128)S(1)} %reshape.72, f32[1,128,3072]{2,0,1:T(1,128)} %fusion.4), kind=kLoop, calls=%fused_computation.16 | loop fusion | flops 1179648 | bytes 3932160 | tf_op jit(solution)/shard_map/convert_element_type | solution.py:107
  (26 shorter events, 7.0 us)
Async XLA Ops:
  0.0 10.0 %copy-start.4 = (bf16[128,3072]{1,0:T(8,128)(2,1)S(1)}, bf16[128,3072]{1,0:T(8,128)(2,1)}, u32[]{:S(2)}) copy-start(bf16[128,3072]{1,0:T(8,128)(2,1)} %param.9) | copy-start | bytes 2359300
  2.6 26.1 %all-to-all-start = ((bf16[64,16,384]{2,0,1:T(8,128)(2,1)}), bf16[64,16,384]{2,0,1:T(8,128)(2,1)S(1)}, u32[]{:S(2)}, u32[]{:S(2)}) async-start(bf16[64,16,384]{2,0,1:T(8,128)(2,1)} %copy.22), calls=%async_computation | async-start | bytes 1572864 | tf_op jit(solution)/shard_map/all_to_all | solution.py:81
  30.0 37.5 %all-to-all-start.1 = ((bf16[128,16,384]{0,2,1:T(8,128)(2,1)}), bf16[128,16,384]{0,2,1:T(8,128)(2,1)S(1)}, u32[]{:S(2)}, u32[]{:S(2)}) async-start(bf16[128,16,384]{0,2,1:T(8,128)(2,1)} %bitcast.7), calls=%async_computation.1 | async-start | bytes 3145728 | tf_op jit(solution)/shard_map/all_to_all | solution.py:88
  67.4 1.7 copy-start
  69.1 41.1 %all-to-all-start.2 = ((bf16[128,16,384]{0,2,1:T(8,128)(2,1)}), bf16[128,16,384]{0,2,1:T(8,128)(2,1)S(1)}, u32[]{:S(2)}, u32[]{:S(2)}) async-start(bf16[128,16,384]{0,2,1:T(8,128)(2,1)} %bitcast.10), calls=%async_computation.2 | async-start | bytes 3145728 | tf_op jit(solution)/shard_map/all_to_all | solution.py:91
  81.8 2.6 %copy-start.3 = (bf16[256,384]{0,1:T(8,128)(2,1)S(1)}, bf16[256,384]{0,1:T(8,128)(2,1)}, u32[]{:S(2)}) copy-start(bf16[256,384]{0,1:T(8,128)(2,1)} %copy.45) | copy-start | bytes 589828
  84.4 2.2 %copy-start.1 = (bf16[128,16,384]{0,2,1:T(8,128)(2,1)S(1)}, bf16[128,16,384]{0,2,1:T(8,128)(2,1)}, u32[]{:S(2)}) copy-start(bf16[128,16,384]{0,2,1:T(8,128)(2,1)} %copy-done) | copy-start | bytes 4718596
  111.9 10.9 %copy-start.2 = (f32[3,1024,128]{2,1,0:T(8,128)S(1)}, f32[3,1024,128]{2,1,0:T(8,128)}, u32[]{:S(2)}) copy-start(f32[3,1024,128]{2,1,0:T(8,128)} %fusion.9) | copy-start | bytes 4718596
  133.5 11.4 %copy-start.5 = (s32[6]{0:T(128)S(1)}, s32[6]{0:T(128)}, u32[]{:S(2)}) copy-start(s32[6]{0:T(128)} %param.14) | copy-start | bytes 76
  135.8 27.8 %all-to-all-start.3 = ((bf16[16,64,384]{2,1,0:T(8,128)(2,1)}), bf16[16,64,384]{2,1,0:T(8,128)(2,1)S(1)}, u32[]{:S(2)}, u32[]{:S(2)}) async-start(bf16[16,64,384]{2,1,0:T(8,128)(2,1)} %convert_element_type.32), calls=%async_computation.3 | async-start | bytes 1572864 | tf_op jit(solution)/shard_map/all_to_all | solution.py:99
where the time goes:
time: 168 us
  waiting for transfers between devices  66.3 us (39%)
  matrix products  33.5 us (20%)
  starting transfers between devices  31.1 us (19%)
  local copies, waits for them, and re-layouts  21.4 us (13%)
  other arithmetic  14.5 us (9%)
    all_to_all x1, waiting for transfers between devices, body(): lax.all_to_all(replicate_slots(keys), 'seq', split_axis=1, concat_axis=0,...  30.5 us
    all_to_all x1, waiting for transfers between devices, body(): lax.all_to_all(queries.reshape(tok_rows // query_pieces, query_pieces * f...  18.3 us
    dot_general x2, matrix products, compute_scores(): jnp.einsum('qgp,ugp->gqu', reshaped_queries, current_key_block, preferred...  13.4 us
    all_to_all x1, waiting for transfers between devices, body(): lax.all_to_all(context, 'seq', split_axis=0, concat_axis=1, tiled=True)  11.4 us
    reduce_sum x1, other arithmetic, advance(): jnp.sum(block_exp, axis=-1)  10.9 us
    dot_general x1, matrix products, advance(): jnp.einsum('vie,evs->vis', block_exp.astype(jnp.bfloat16), values_here, p...  10.6 us
    all_to_all x1, starting transfers between devices, body(): lax.all_to_all(replicate_slots(values), 'seq', split_axis=1, concat_axis=...  9.11 us
    all_to_all x1, starting transfers between devices, body(): lax.all_to_all(context, 'seq', split_axis=0, concat_axis=1, tiled=True)  9.11 us
  transfers between devices with their start and end apart: 4, of which 4 were waited for; matrix products, arithmetic and copies ran while one was open for 20% of the time, Pallas kernels for 0%

commit v1 on v0

--- a/solution.py
+++ b/solution.py
@@ -1,11 +1,204 @@
+import functools
+import math
+
 import jax
 import jax.numpy as jnp
 from jax import lax
+from jax.experimental import pallas as pl
+from jax.experimental.pallas import tpu as pltpu
 from jax.sharding import PartitionSpec as P
 
 HEADS = 24
 HEAD_DIM = 128
 HEADS_DEV = 3
+PLANE = 4
+PAIR = 2 * HEAD_DIM
+EXP_SCALE = HEAD_DIM ** (-0.5) * math.log2(math.e)
+
+
+def pack_kernel(spans, planes, where, *refs):
+    n_src = 1 + max(source for source, _ in spans)
+    sources, outs, sems = refs[:n_src], refs[n_src:-1], refs[-1]
+    copies = []
+    for relative in range(planes):
+        plane = jnp.bitwise_xor(where[0], relative)
+        for slot, (source, base) in enumerate(spans):
+            start = pl.multiple_of(base + plane * PAIR, PAIR)
+            copies.append(
+                pltpu.make_async_copy(
+                    sources[source].at[:, pl.ds(start, PAIR)],
+                    outs[relative].at[:, pl.ds(slot * PAIR, PAIR)],
+                    sems.at[relative, slot],
+                )
+            )
+    for copy in copies:
+        copy.start()
+    for copy in copies:
+        copy.wait()
+
+
+def pack(where, spans, planes, *sources):
+    rows = sources[0].shape[0]
+    shape = jax.ShapeDtypeStruct((rows, len(spans) * PAIR), sources[0].dtype)
+    return pl.pallas_call(
+        functools.partial(pack_kernel, spans, planes),
+        out_shape=[shape] * planes,
+        in_specs=[pl.BlockSpec(memory_space=pltpu.SMEM)] + [pl.BlockSpec(memory_space=pl.ANY)] * len(sources),
+        out_specs=[pl.BlockSpec(memory_space=pl.ANY)] * planes,
+        scratch_shapes=[pltpu.SemaphoreType.DMA((planes, len(spans)))],
+        name="pack",
+    )(where, *sources)
+
+
+def attend_kernel(n_q, n_kv, scalars, *refs):
+    queries = refs[:n_q]
+    keys = refs[n_q : n_q + n_kv]
+    values = refs[n_q + n_kv : n_q + 2 * n_kv]
+    text_keys, text_values = refs[n_q + 2 * n_kv : n_q + 2 * n_kv + 2]
+    outs = refs[n_q + 2 * n_kv + 2 :]
+    text_slots = text_keys.shape[0]
+    contract_last = (((1,), (1,)), ((), ()))
+    for first in range(0, n_q, 2):
+        q = jnp.concatenate([queries[first][...], queries[first + 1][...]], axis=0)
+        rows = q.shape[0]
+        scores = [
+            lax.dot_general(q, k[...], contract_last, preferred_element_type=jnp.float32) for k in keys
+        ]
+        text_scores = lax.dot_general(q, text_keys[...], contract_last, preferred_element_type=jnp.float32)
+        usable = lax.broadcasted_iota(jnp.int32, (rows, text_slots), 1) < scalars[1]
+        scores.append(jnp.where(usable, text_scores, -jnp.inf))
+        top = functools.reduce(jnp.maximum, [jnp.max(s, axis=1, keepdims=True) for s in scores])
+        total = jnp.zeros((rows, 1), jnp.float32)
+        weighted = jnp.zeros((rows, HEAD_DIM), jnp.float32)
+        for s, v in zip(scores, (*values, text_values)):
+            weights = jnp.exp2((s - top) * EXP_SCALE)
+            total = total + jnp.sum(weights, axis=1, keepdims=True)
+            weighted = weighted + jnp.dot(
+                weights.astype(jnp.bfloat16), v[...], preferred_element_type=jnp.float32
+            )
+        context = (weighted / total).astype(jnp.bfloat16)
+        half = rows // 2
+        outs[first][...] = context[:half]
+        outs[first + 1][...] = context[half:]
+
+
+def attend_pair(scalars, queries, q_block, kvs, text_keys, text_values, text_block):
+    n_q, n_kv = len(queries), len(kvs)
+    rows = queries[0].shape[0]
+    slots = text_keys.shape[0]
+
+    def column(block):
+        return lambda head, scalars: (0, block + head)
+
+    def text_column(head, scalars):
+        return (0, text_block + scalars[0] * 2 + head)
+
+    in_specs = [pl.BlockSpec((rows, HEAD_DIM), column(q_block)) for _ in queries]
+    in_specs += [pl.BlockSpec((kv.shape[0], HEAD_DIM), column(0)) for kv in kvs]
+    in_specs += [pl.BlockSpec((kv.shape[0], HEAD_DIM), column(2)) for kv in kvs]
+    in_specs += [pl.BlockSpec((slots, HEAD_DIM), text_column)] * 2
+    n_keys = sum(kv.shape[0] for kv in kvs) + slots
+    work = 2 * n_q * rows * n_keys
+    return pl.pallas_call(
+        functools.partial(attend_kernel, n_q, n_kv),
+        grid_spec=pltpu.PrefetchScalarGridSpec(
+            num_scalar_prefetch=1,
+            grid=(2,),
+            in_specs=in_specs,
+            out_specs=[pl.BlockSpec((rows, HEAD_DIM), column(0)) for _ in queries],
+        ),
+        out_shape=[jax.ShapeDtypeStruct((rows, PAIR), jnp.bfloat16)] * n_q,
+        compiler_params=pltpu.CompilerParams(vmem_limit_bytes=40 * 1024 * 1024),
+        cost_estimate=pl.CostEstimate(
+            flops=work * HEAD_DIM * 4, bytes_accessed=4 * n_keys * PAIR, transcendentals=work
+        ),
+        name="attend",
+    )(scalars, *queries, *kvs, *kvs, text_keys, text_values)
+
+
+def deltas_kernel(plan, deltas, out):
+    total = plan[0].astype(jnp.float32) * deltas[0].astype(jnp.float32)
+    for block in range(1, deltas.shape[0]):
+        total = total + plan[block].astype(jnp.float32) * deltas[block].astype(jnp.float32)
+    out[...] = total * 0.25
+
+
+def sum_deltas(plan, deltas):
+    blocks, rows, width = deltas.shape
+    step = width // 4
+    return pl.pallas_call(
+        deltas_kernel,
+        grid=(4,),
+        in_specs=[
+            pl.BlockSpec(memory_space=pltpu.SMEM),
+            pl.BlockSpec((blocks, rows, step), lambda i: (0, 0, i)),
+        ],
+        out_specs=pl.BlockSpec((rows, step), lambda i: (0, i)),
+        out_shape=jax.ShapeDtypeStruct((rows, width), jnp.float32),
+        cost_estimate=pl.CostEstimate(
+            flops=2 * blocks * rows * width, bytes_accessed=2 * blocks * rows * width, transcendentals=0
+        ),
+        name="deltas",
+    )(plan, deltas)
+
+
+def mix_kernel(planes, where, added, *refs):
+    pieces, out = refs[:-1], refs[-1]
+    slab = planes * PAIR
+    for index, piece in enumerate(pieces):
+        phase, relative = divmod(index, planes)
+        plane = jnp.bitwise_xor(where[0], relative)
+        columns = pl.ds(pl.multiple_of(phase * slab + plane * PAIR, PAIR), PAIR)
+        out[:, columns] = (piece[...].astype(jnp.float32) + added[:, columns]).astype(out.dtype)
+
+
+def mix(where, planes, added, pieces):
+    vmem = pl.BlockSpec(memory_space=pltpu.VMEM)
+    return pl.pallas_call(
+        functools.partial(mix_kernel, planes),
+        in_specs=[pl.BlockSpec(memory_space=pltpu.SMEM)] + [vmem] * (1 + len(pieces)),
+        out_specs=vmem,
+        out_shape=jax.ShapeDtypeStruct(added.shape, jnp.bfloat16),
+        name="mix",
+    )(where, added, *pieces)
+
+
+def plane_body(queries, keys, values, text_keys, text_values, text_len, plan, deltas):
+    size = lax.axis_size("seq")
+    planes = size // PLANE
+    slab = planes * PAIR
+    phases = HEADS * HEAD_DIM // slab
+    plane = lax.axis_index("seq") // PLANE
+    where = plane.astype(jnp.int32).reshape(1)
+    scalars = jnp.concatenate([where, text_len])
+
+    def swap(array, distance):
+        return lax.ppermute(array, "seq", [(i, i ^ distance) for i in range(size)])
+
+    def to_planes(pieces):
+        return [pieces[0]] + [swap(pieces[r], PLANE * r) for r in range(1, planes)]
+
+    def gather_plane(pieces):
+        own = jnp.concatenate(pieces, axis=0)
+        other = swap(own, 2)
+        return [own, other, swap(own, 1), swap(other, 1)]
+
+    first = to_planes(pack(where, ((0, 0), (1, 0), (2, 0)), planes, queries, keys, values))
+    rest = [
+        to_planes(pack(where, ((0, slab * p), (1, slab * p)), planes, keys, values)) for p in range(1, phases)
+    ]
+    later = to_planes(pack(where, tuple((0, slab * p) for p in range(1, phases)), planes, queries))
+
+    gathered = [gather_plane([piece[:, PAIR:] for piece in first])] + [gather_plane(r) for r in rest]
+    added = sum_deltas(plan, deltas)
+    returned = []
+    for p in range(phases):
+        pieces, block = (first, 0) if p == 0 else (later, 2 * (p - 1))
+        contexts = attend_pair(
+            scalars, pieces, block, gathered[p], text_keys, text_values, p * slab // HEAD_DIM
+        )
+        returned += to_planes(contexts)
+    return mix(where, planes, added, returned)
 
 
 def attend(head_queries, head_keys, head_values, group_token_keys, group_tv, usable):
@@ -37,12 +230,8 @@
     )
     key_total = head_keys.shape[0]
     current_key_block = 2048
-    block_keys = head_keys.reshape(
-        key_total // current_key_block, current_key_block, HEADS_DEV, HEAD_DIM
-    )
-    block_values = head_values.reshape(
-        key_total // current_key_block, current_key_block, HEADS_DEV, HEAD_DIM
-    )
+    block_keys = head_keys.reshape(key_total // current_key_block, current_key_block, HEADS_DEV, HEAD_DIM)
+    block_values = head_values.reshape(key_total // current_key_block, current_key_block, HEADS_DEV, HEAD_DIM)
 
     def advance(carry, blocks):
         old_top, old_denominator, old_weighted = carry
@@ -67,7 +256,7 @@
     return context.transpose(1, 0, 2).reshape(query_rows, HEADS_DEV * HEAD_DIM).astype(jnp.bfloat16)
 
 
-def body(queries, keys, values, text_keys, text_values, text_len, plan, deltas):
+def general_body(queries, keys, values, text_keys, text_values, text_len, plan, deltas):
     tok_rows, feat_width = queries.shape
     axis_count = lax.axis_size("seq")
     head_groups = HEADS // HEADS_DEV
@@ -85,12 +274,8 @@
         concat_axis=0,
         tiled=True,
     )
-    head_keys = lax.all_to_all(
-        replicate_slots(keys), "seq", split_axis=1, concat_axis=0, tiled=True
-    )
-    head_values = lax.all_to_all(
-        replicate_slots(values), "seq", split_axis=1, concat_axis=0, tiled=True
-    )
+    head_keys = lax.all_to_all(replicate_slots(keys), "seq", split_axis=1, concat_axis=0, tiled=True)
+    head_values = lax.all_to_all(replicate_slots(values), "seq", split_axis=1, concat_axis=0, tiled=True)
     group_index = lax.axis_index("seq") % head_groups
     group_token_keys = lax.dynamic_slice_in_dim(text_keys, group_index * slot_width, slot_width, 1)
     group_tv = lax.dynamic_slice_in_dim(text_values, group_index * slot_width, slot_width, 1)
@@ -99,17 +284,17 @@
     returned = lax.all_to_all(context, "seq", split_axis=0, concat_axis=1, tiled=True)
     context_rows = returned.reshape(tok_rows, feat_width)
     added = (
-        jnp.einsum(
-            "b,btc->tc", plan.astype(jnp.bfloat16), deltas, preferred_element_type=jnp.float32
-        )
-        * 0.25
+        jnp.einsum("b,btc->tc", plan.astype(jnp.bfloat16), deltas, preferred_element_type=jnp.float32) * 0.25
     )
     return (context_rows.astype(jnp.float32) + added).astype(jnp.bfloat16)
 
 
 def solution(mesh):
+    size = mesh.shape["seq"]
+    planes = size // PLANE
+    fits = planes in (2, 4) and planes * PLANE == size and HEADS % (2 * planes) == 0
     return jax.shard_map(
-        body,
+        plane_body if fits else general_body,
         mesh=mesh,
         in_specs=(
             P(("grp", "seq"), None),

time: 168 us -> 178 us (1.060)
  Pallas kernels: 0 us -> 102 us
  waiting for transfers between devices: 66.3 us -> 21.8 us
  matrix products: 33.5 us -> 0 us
  other arithmetic: 14.5 us -> 0.9 us
  local copies, waits for them, and re-layouts: 21.4 us -> 11.2 us
  starting transfers between devices: 31.1 us -> 40.6 us
    pallas_call x0 -> x9, Pallas kernels: none -> 102 us  [the longest x4 76.2 us: pack(): pl.pallas_call(functools.partial(pack_kernel, spans, planes), out_shape=[...]
    all_to_all x4 -> x0, waiting for transfers between devices: 66.3 us -> none  [the longest x1 30.5 us: body(): lax.all_to_all(replicate_slots(keys), 'seq', split_axis=1, concat_axis=0,...]
    ppermute x0 -> x30, starting transfers between devices: none -> 40.6 us  [swap(): return lax.ppermute(array, 'seq', [(i, i ^ distance) for i in range(size)])]
    dot_general x5 -> x0, matrix products: 33.5 us -> none  [the longest x2 13.4 us: compute_scores(): jnp.einsum('qgp,ugp->gqu', reshaped_queries, current_key_block, preferred...]
    all_to_all x4 -> x0, starting transfers between devices: 31.1 us -> none  [the longest x1 9.11 us: body(): lax.all_to_all(replicate_slots(values), 'seq', split_axis=1, concat_axis=...]
    ppermute x0 -> x30, waiting for transfers between devices: none -> 21.8 us  [swap(): return lax.ppermute(array, 'seq', [(i, i ^ distance) for i in range(size)])]
    reduce_sum x2 -> x0, other arithmetic: 11.6 us -> none  [the longest x1 10.9 us: advance(): jnp.sum(block_exp, axis=-1)]
    all_to_all x4 -> x0, local copies, waits for them, and re-layouts: 5.77 us -> none  [the longest x2 2.59 us: body(): lax.all_to_all(queries.reshape(tok_rows // query_pieces, query_pieces * f...]
  transfers between devices with their start and end apart: 4 -> 30, of which waited for: 4 -> 6; matrix products, arithmetic and copies ran while one was open for 20% -> 5% of each run, Pallas kernels for 0% -> 46%
where the time goes in v1:
time: 178 us
  Pallas kernels  102 us (57%)
  starting transfers between devices  40.6 us (23%)
  waiting for transfers between devices  21.8 us (12%)
  local copies, waits for them, and re-layouts  11.2 us (6%)
    pallas_call x4, Pallas kernels, pack(): pl.pallas_call(functools.partial(pack_kernel, spans, planes), out_shape=[...  76.2 us
    ppermute x30, starting transfers between devices, swap(): return lax.ppermute(array, 'seq', [(i, i ^ distance) for i in range(size)])  40.6 us
    ppermute x30, waiting for transfers between devices, swap(): return lax.ppermute(array, 'seq', [(i, i ^ distance) for i in range(size)])  21.8 us
    pallas_call x3, Pallas kernels, attend_pair(): pl.pallas_call(functools.partial(attend_kernel, n_q, n_kv), grid_spec=plt...  18.9 us
    unnamed x48, local copies, waits for them, and re-layouts  8.07 us
    pallas_call x1, Pallas kernels, sum_deltas(): pl.pallas_call(deltas_kernel, grid=(4,), in_specs=[pl.BlockSpec(memory_sp...  4.63 us
  transfers between devices with their start and end apart: 30, of which 6 were waited for; matrix products, arithmetic and copies ran while one was open for 5% of the time, Pallas kernels for 46%

profile of v1, /device:TPU:0, one launch (start us, length us, event | category | flops | bytes accessed | tf_op | source)
XLA Modules:
  0.0 177.9 jit_solution(2474664965466879319)
XLA Ops:
  0.0 17.1 %pack.7 = (bf16[128,512]{1,0:T(8,128)(2,1)}, bf16[128,512]{1,0:T(8,128)(2,1)}, bf16[128,512]{1,0:T(8,128)(2,1)}, bf16[128,512]{1,0:T(8,128)(2,1)}) custom-call(s32[1]{0:T(128)} %bitcast.where, bf16[128,3072]{1,0:T(8,128)(2,1)} %refs_0_.7, bf16[128,3072]{1,0:T(8,128)(2,1)} %refs_1_.5), custom_call_target="tpu_custom_call" | custom-call | tf_op jit(solution)/shard_map/pack/pallas_call | solution.py:43
  17.1 3.1 %collective-permute-start.21 = (bf16[128,512]{1,0:T(8,128)(2,1)}, bf16[128,512]{1,0:T(8,128)(2,1)S(1)}, u32[]{:S(2)}, u32[]{:S(2)}) collective-permute-start(bf16[128,512]{1,0:T(8,128)(2,1)} %get-tuple-element.54), channel_id=1, source_target_pairs={{0,4},{1,5},{2,6},{3,7},{4,0},{5,1},{6,2},{7,3},{8,12},{9,13},{10,... | collective-permute-start | bytes 393224 | tf_op jit(solution)/shard_map/ppermute | solution.py:176
  20.2 2.6 %collective-permute-start.22 = (bf16[128,512]{1,0:T(8,128)(2,1)}, bf16[128,512]{1,0:T(8,128)(2,1)}, u32[]{:S(2)}, u32[]{:S(2)}) collective-permute-start(bf16[128,512]{1,0:T(8,128)(2,1)} %get-tuple-element.55), channel_id=1, source_target_pairs={{0,8},{1,9},{2,10},{3,11},{4,12},{5,13},{6,14},{7,15},{8,0},{9,1},... | collective-permute-start | bytes 393224 | tf_op jit(solution)/shard_map/ppermute | solution.py:176
  22.8 17.1 %pack.6 = (bf16[128,512]{1,0:T(8,128)(2,1)}, bf16[128,512]{1,0:T(8,128)(2,1)}, bf16[128,512]{1,0:T(8,128)(2,1)}, bf16[128,512]{1,0:T(8,128)(2,1)}) custom-call(s32[1]{0:T(128)} %bitcast.where, bf16[128,3072]{1,0:T(8,128)(2,1)} %refs_0_.7, bf16[128,3072]{1,0:T(8,128)(2,1)} %refs_1_.5), custom_call_target="tpu_custom_call" | custom-call | tf_op jit(solution)/shard_map/pack/pallas_call | solution.py:43
  40.8 3.5 %collective-permute-start.13 = (bf16[128,512]{1,0:T(8,128)(2,1)}, bf16[128,512]{1,0:T(8,128)(2,1)S(1)}, u32[]{:S(2)}, u32[]{:S(2)}) collective-permute-start(bf16[128,512]{1,0:T(8,128)(2,1)} %get-tuple-element.47), channel_id=1, source_target_pairs={{0,8},{1,9},{2,10},{3,11},{4,12},{5,13},{6,14},{7,15},{8,0},{9,1},... | collective-permute-start | bytes 393224 | tf_op jit(solution)/shard_map/ppermute | solution.py:176
  45.9 25.0 %pack.4 = (bf16[128,768]{1,0:T(8,128)(2,1)}, bf16[128,768]{1,0:T(8,128)(2,1)}, bf16[128,768]{1,0:T(8,128)(2,1)}, bf16[128,768]{1,0:T(8,128)(2,1)}) custom-call(s32[1]{0:T(128)} %bitcast.where, bf16[128,3072]{1,0:T(8,128)(2,1)} %refs_0_.5, bf16[128,3072]{1,0:T(8,128)(2,1)} %refs_0_.7, bf16[128,3072]{1,0:T(8,128)(2,1)} %refs_1_.5), custom_call_target="tpu_custom_call" | custom-call | tf_op jit(solution)/shard_map/pack/pallas_call | solution.py:43
  73.2 3.8 %collective-permute-start.1 = (bf16[128,768]{1,0:T(8,128)(2,1)}, bf16[128,768]{1,0:T(8,128)(2,1)S(1)}, u32[]{:S(2)}, u32[]{:S(2)}) collective-permute-start(bf16[128,768]{1,0:T(8,128)(2,1)} %get-tuple-element.35), channel_id=1, source_target_pairs={{0,8},{1,9},{2,10},{3,11},{4,12},{5,13},{6,14},{7,15},{8,0},{9,1},... | collective-permute-start | bytes 589832 | tf_op jit(solution)/shard_map/ppermute | solution.py:176
  77.7 2.5 %collective-permute-done.14 = bf16[128,512]{1,0:T(8,128)(2,1)S(1)} collective-permute-done((bf16[128,512]{1,0:T(8,128)(2,1)S(1)}, bf16[128,512]{1,0:T(8,128)(2,1)S(1)}, u32[]{:S(2)}, u32[]{:S(2)}) %collective-permute-start.14) | collective-permute-done | bytes 131104 | tf_op jit(solution)/shard_map/ppermute | solution.py:176
  82.6 1.7 collective-permute-start.15
  86.3 6.6 %collective-permute-done.1.refs_2_ = bf16[128,768]{1,0:T(8,128)(2,1)S(1)} collective-permute-done((bf16[128,768]{1,0:T(8,128)(2,1)}, bf16[128,768]{1,0:T(8,128)(2,1)S(1)}, u32[]{:S(2)}, u32[]{:S(2)}) %collective-permute-start.1) | collective-permute-done | bytes 196640 | tf_op jit(solution)/shard_map/ppermute | solution.py:176
  96.0 17.1 %pack.5 = (bf16[128,512]{1,0:T(8,128)(2,1)}, bf16[128,512]{1,0:T(8,128)(2,1)}, bf16[128,512]{1,0:T(8,128)(2,1)}, bf16[128,512]{1,0:T(8,128)(2,1)}) custom-call(s32[1]{0:T(128)} %bitcast.where, bf16[128,3072]{1,0:T(8,128)(2,1)} %refs_0_.5), custom_call_target="tpu_custom_call" | custom-call | tf_op jit(solution)/shard_map/pack/pallas_call | solution.py:43
  113.0 3.5 %collective-permute-start.9 = (bf16[128,512]{1,0:T(8,128)(2,1)}, bf16[128,512]{1,0:T(8,128)(2,1)S(1)}, u32[]{:S(2)}, u32[]{:S(2)}) collective-permute-start(bf16[128,512]{1,0:T(8,128)(2,1)} %get-tuple-element.42), channel_id=1, source_target_pairs={{0,4},{1,5},{2,6},{3,7},{4,0},{5,1},{6,2},{7,3},{8,12},{9,13},{10,... | collective-permute-start | bytes 393224 | tf_op jit(solution)/shard_map/ppermute | solution.py:176
  116.5 3.2 %collective-permute-done.9.refs_1_ = bf16[128,512]{1,0:T(8,128)(2,1)S(1)} collective-permute-done((bf16[128,512]{1,0:T(8,128)(2,1)}, bf16[128,512]{1,0:T(8,128)(2,1)S(1)}, u32[]{:S(2)}, u32[]{:S(2)}) %collective-permute-start.9) | collective-permute-done | bytes 131104 | tf_op jit(solution)/shard_map/ppermute | solution.py:176
  121.0 4.7 %collective-permute-done.10.refs_2_ = bf16[128,512]{1,0:T(8,128)(2,1)S(1)} collective-permute-done((bf16[128,512]{1,0:T(8,128)(2,1)}, bf16[128,512]{1,0:T(8,128)(2,1)S(1)}, u32[]{:S(2)}, u32[]{:S(2)}) %collective-permute-start.10) | collective-permute-done | bytes 131104 | tf_op jit(solution)/shard_map/ppermute | solution.py:176
  125.8 3.2 %collective-permute-start.11 = (bf16[128,512]{1,0:T(8,128)(2,1)}, bf16[128,512]{1,0:T(8,128)(2,1)S(1)}, u32[]{:S(2)}, u32[]{:S(2)}) collective-permute-start(bf16[128,512]{1,0:T(8,128)(2,1)} %get-tuple-element.44), channel_id=1, source_target_pairs={{0,12},{1,13},{2,14},{3,15},{4,8},{5,9},{6,10},{7,11},{8,4},{9,5},... | collective-permute-start | bytes 393224 | tf_op jit(solution)/shard_map/ppermute | solution.py:176
  129.0 3.9 %collective-permute-done.11.refs_3_ = bf16[128,512]{1,0:T(8,128)(2,1)S(1)} collective-permute-done((bf16[128,512]{1,0:T(8,128)(2,1)}, bf16[128,512]{1,0:T(8,128)(2,1)S(1)}, u32[]{:S(2)}, u32[]{:S(2)}) %collective-permute-start.11) | collective-permute-done | bytes 131104 | tf_op jit(solution)/shard_map/ppermute | solution.py:176
  135.5 6.0 %attend.4 = (bf16[128,256]{1,0:T(8,128)(2,1)S(1)}, bf16[128,256]{1,0:T(8,128)(2,1)S(1)}, bf16[128,256]{1,0:T(8,128)(2,1)S(1)}, bf16[128,256]{1,0:T(8,128)(2,1)S(1)}) custom-call(s32[2]{0:T(128)S(1)} %pad_add_fusion.scalars, bf16[128,512]{1,0:T(8,128)(2,1)S(1)} %copy-done.7, bf16[128,512]{1,0:T(8,128)(2,1)S(1)} %collective-permute-done.9.refs_1_, ...), custom_call_target="tpu_custom_call" | custom-call | flops 1207959552 | bytes 2359296 | tf_op jit(solution)/shard_map/attend/pallas_call | solution.py:102
  143.2 2.1 %collective-permute-start.19 = (bf16[128,256]{1,0:T(8,128)(2,1)S(1)}, bf16[128,256]{1,0:T(8,128)(2,1)S(1)}, u32[]{:S(2)}, u32[]{:S(2)}) collective-permute-start(bf16[128,256]{1,0:T(8,128)(2,1)S(1)} %get-tuple-element.51), channel_id=1, source_target_pairs={{0,8},{1,9},{2,10},{3,11},{4,12},{5,13},{6,14},{7,15},{8,0},{9,1},... | collective-permute-start | bytes 196616 | tf_op jit(solution)/shard_map/ppermute | solution.py:176
  146.0 6.4 %attend.5 = (bf16[128,256]{1,0:T(8,128)(2,1)S(1)}, bf16[128,256]{1,0:T(8,128)(2,1)S(1)}, bf16[128,256]{1,0:T(8,128)(2,1)}, bf16[128,256]{1,0:T(8,128)(2,1)}) custom-call(s32[2]{0:T(128)S(1)} %pad_add_fusion.scalars, bf16[128,512]{1,0:T(8,128)(2,1)S(1)} %copy-done.7, bf16[128,512]{1,0:T(8,128)(2,1)S(1)} %collective-permute-done.9.refs_1_, ...), custom_call_target="tpu_custom_call" | custom-call | flops 1207959552 | bytes 2359296 | tf_op jit(solution)/shard_map/attend/pallas_call | solution.py:102
  153.2 3.0 %collective-permute-start.28 = (bf16[128,256]{1,0:T(8,128)(2,1)}, bf16[128,256]{1,0:T(8,128)(2,1)}, u32[]{:S(2)}, u32[]{:S(2)}) collective-permute-start(bf16[128,256]{1,0:T(8,128)(2,1)} %get-tuple-element.59), channel_id=1, source_target_pairs={{0,8},{1,9},{2,10},{3,11},{4,12},{5,13},{6,14},{7,15},{8,0},{9,1},... | collective-permute-start | bytes 196616 | tf_op jit(solution)/shard_map/ppermute | solution.py:176
  156.2 6.5 %attend.3 = (bf16[128,256]{1,0:T(8,128)(2,1)S(1)}, bf16[128,256]{1,0:T(8,128)(2,1)}, bf16[128,256]{1,0:T(8,128)(2,1)}, bf16[128,256]{1,0:T(8,128)(2,1)}) custom-call(s32[2]{0:T(128)S(1)} %pad_add_fusion.scalars, bf16[128,768]{1,0:T(8,128)(2,1)S(1)} %copy-done.4, bf16[128,768]{1,0:T(8,128)(2,1)S(1)} %collective-permute-done.refs_1_, ...), custom_call_target="tpu_custom_call" | custom-call | flops 1207959552 | bytes 2359296 | tf_op jit(solution)/shard_map/attend/pallas_call | solution.py:102
  164.1 3.7 %collective-permute-start.7 = (bf16[128,256]{1,0:T(8,128)(2,1)}, bf16[128,256]{1,0:T(8,128)(2,1)S(1)}, u32[]{:S(2)}, u32[]{:S(2)}) collective-permute-start(bf16[128,256]{1,0:T(8,128)(2,1)} %get-tuple-element.39), channel_id=1, source_target_pairs={{0,8},{1,9},{2,10},{3,11},{4,12},{5,13},{6,14},{7,15},{8,0},{9,1},... | collective-permute-start | bytes 196616 | tf_op jit(solution)/shard_map/ppermute | solution.py:176
  169.0 4.6 %deltas.2.added = f32[128,3072]{1,0:T(8,128)} custom-call(s32[6]{0:T(128)} %plan.1, bf16[6,128,3072]{2,1,0:T(8,128)(2,1)} %deltas.3), custom_call_target="tpu_custom_call" | custom-call | flops 4718592 | bytes 4718592 | tf_op jit(solution)/shard_map/deltas/pallas_call | solution.py:129
  175.2 2.7 %mix.1 = bf16[128,3072]{1,0:T(8,128)(2,1)} custom-call(s32[1]{0:T(128)} %bitcast.where, f32[128,3072]{1,0:T(8,128)} %deltas.2.added, bf16[128,256]{1,0:T(8,128)(2,1)} %copy-done.10, bf16[128,256]{1,0:T(8,128)(2,1)} %copy-done.17, bf16[128,256]{1,0:T(8,128)(2,1)} %copy-done.18, bf16[128,256]{1,0:T(8,128)(2,1)} %copy-done.19, bf16[128,256]{1,0:T(8,128)(2,1)} %copy-done.8, ...), custom_call_target="tpu_custom_call" | custom-call | tf_op jit(solution)/shard_map/mix/pallas_call | solution.py:157
  (101 shorter events, 23.4 us)
Async XLA Ops:
  17.1 54.8 %collective-permute-start.21 = (bf16[128,512]{1,0:T(8,128)(2,1)}, bf16[128,512]{1,0:T(8,128)(2,1)S(1)}, u32[]{:S(2)}, u32[]{:S(2)}) collective-permute-start(bf16[128,512]{1,0:T(8,128)(2,1)} %get-tuple-element.54), channel_id=1, source_target_pairs={{0,4},{1,5},{2,6},{3,7},{4,0},{5,1},{6,2},{7,3},{8,12},{9,13},{10,... | collective-permute-start | bytes 393224 | tf_op jit(solution)/shard_map/ppermute | solution.py:176
  20.2 60.8 %collective-permute-start.22 = (bf16[128,512]{1,0:T(8,128)(2,1)}, bf16[128,512]{1,0:T(8,128)(2,1)}, u32[]{:S(2)}, u32[]{:S(2)}) collective-permute-start(bf16[128,512]{1,0:T(8,128)(2,1)} %get-tuple-element.55), channel_id=1, source_target_pairs={{0,8},{1,9},{2,10},{3,11},{4,12},{5,13},{6,14},{7,15},{8,0},{9,1},... | collective-permute-start | bytes 393224 | tf_op jit(solution)/shard_map/ppermute | solution.py:176
  22.7 59.9 %collective-permute-start.23 = (bf16[128,512]{1,0:T(8,128)(2,1)}, bf16[128,512]{1,0:T(8,128)(2,1)}, u32[]{:S(2)}, u32[]{:S(2)}) collective-permute-start(bf16[128,512]{1,0:T(8,128)(2,1)} %get-tuple-element.56), channel_id=1, source_target_pairs={{0,12},{1,13},{2,14},{3,15},{4,8},{5,9},{6,10},{7,11},{8,4},{9,5},... | collective-permute-start | bytes 393224 | tf_op jit(solution)/shard_map/ppermute | solution.py:176
  39.8 32.1 %collective-permute-start.12 = (bf16[128,512]{1,0:T(8,128)(2,1)}, bf16[128,512]{1,0:T(8,128)(2,1)S(1)}, u32[]{:S(2)}, u32[]{:S(2)}) collective-permute-start(bf16[128,512]{1,0:T(8,128)(2,1)} %get-tuple-element.46), channel_id=1, source_target_pairs={{0,4},{1,5},{2,6},{3,7},{4,0},{5,1},{6,2},{7,3},{8,12},{9,13},{10,... | collective-permute-start | bytes 393224 | tf_op jit(solution)/shard_map/ppermute | solution.py:176
  40.8 32.5 %collective-permute-start.13 = (bf16[128,512]{1,0:T(8,128)(2,1)}, bf16[128,512]{1,0:T(8,128)(2,1)S(1)}, u32[]{:S(2)}, u32[]{:S(2)}) collective-permute-start(bf16[128,512]{1,0:T(8,128)(2,1)} %get-tuple-element.47), channel_id=1, source_target_pairs={{0,8},{1,9},{2,10},{3,11},{4,12},{5,13},{6,14},{7,15},{8,0},{9,1},... | collective-permute-start | bytes 393224 | tf_op jit(solution)/shard_map/ppermute | solution.py:176
  72.0 14.0 %collective-permute-start = (bf16[128,768]{1,0:T(8,128)(2,1)}, bf16[128,768]{1,0:T(8,128)(2,1)S(1)}, u32[]{:S(2)}, u32[]{:S(2)}) collective-permute-start(bf16[128,768]{1,0:T(8,128)(2,1)} %get-tuple-element.34), channel_id=1, source_target_pairs={{0,4},{1,5},{2,6},{3,7},{4,0},{5,1},{6,2},{7,3},{8,12},{9,13},{10,... | collective-permute-start | bytes 589832 | tf_op jit(solution)/shard_map/ppermute | solution.py:176
  73.2 19.7 %collective-permute-start.1 = (bf16[128,768]{1,0:T(8,128)(2,1)}, bf16[128,768]{1,0:T(8,128)(2,1)S(1)}, u32[]{:S(2)}, u32[]{:S(2)}) collective-permute-start(bf16[128,768]{1,0:T(8,128)(2,1)} %get-tuple-element.35), channel_id=1, source_target_pairs={{0,8},{1,9},{2,10},{3,11},{4,12},{5,13},{6,14},{7,15},{8,0},{9,1},... | collective-permute-start | bytes 589832 | tf_op jit(solution)/shard_map/ppermute | solution.py:176
  80.2 12.7 %collective-permute-start.2 = (bf16[128,768]{1,0:T(8,128)(2,1)}, bf16[128,768]{1,0:T(8,128)(2,1)S(1)}, u32[]{:S(2)}, u32[]{:S(2)}) collective-permute-start(bf16[128,768]{1,0:T(8,128)(2,1)} %get-tuple-element.36), channel_id=1, source_target_pairs={{0,12},{1,13},{2,14},{3,15},{4,8},{5,9},{6,10},{7,11},{8,4},{9,5},... | collective-permute-start | bytes 589832 | tf_op jit(solution)/shard_map/ppermute | solution.py:176
  80.9 52.4 %collective-permute-start.16 = (bf16[512,512]{1,0:T(8,128)(2,1)}, bf16[512,512]{1,0:T(8,128)(2,1)}, u32[]{:S(2)}, u32[]{:S(2)}) collective-permute-start(bf16[512,512]{1,0:T(8,128)(2,1)} %constant_dynamic-update-slice_fusion.refs_4_.refs_8_), channel_id=1, source_target_pairs={{0,1},{1,0},{2,3},{3,2},{4,5},{5,4},{6,7},{7,6},{8,9},{9,8},{10,11... | collective-permute-start | bytes 1572872 | tf_op jit(solution)/shard_map/ppermute | solution.py:176
  82.6 46.3 %collective-permute-start.15 = (bf16[512,512]{1,0:T(8,128)(2,1)}, bf16[512,512]{1,0:T(8,128)(2,1)}, u32[]{:S(2)}, u32[]{:S(2)}) collective-permute-start(bf16[512,512]{1,0:T(8,128)(2,1)} %constant_dynamic-update-slice_fusion.refs_4_.refs_8_), channel_id=1, source_target_pairs={{0,2},{1,3},{2,0},{3,1},{4,6},{5,7},{6,4},{7,5},{8,10},{9,11},{10,... | collective-permute-start | bytes 1572872 | tf_op jit(solution)/shard_map/ppermute | solution.py:176
  86.0 46.9 %collective-permute-start.24 = (bf16[512,512]{1,0:T(8,128)(2,1)}, bf16[512,512]{1,0:T(8,128)(2,1)}, u32[]{:S(2)}, u32[]{:S(2)}) collective-permute-start(bf16[512,512]{1,0:T(8,128)(2,1)} %constant_dynamic-update-slice_fusion.4.refs_4_.refs_8_), channel_id=1, source_target_pairs={{0,2},{1,3},{2,0},{3,1},{4,6},{5,7},{6,4},{7,5},{8,10},{9,11},{10,... | collective-permute-start | bytes 1572872 | tf_op jit(solution)/shard_map/ppermute | solution.py:176
  94.4 39.0 %collective-permute-start.3 = (bf16[512,512]{1,0:T(8,128)(2,1)}, bf16[512,512]{1,0:T(8,128)(2,1)}, u32[]{:S(2)}, u32[]{:S(2)}) collective-permute-start(bf16[512,512]{1,0:T(8,128)(2,1)} %pad_maximum_fusion.refs_4_.refs_8_), channel_id=1, source_target_pairs={{0,2},{1,3},{2,0},{3,1},{4,6},{5,7},{6,4},{7,5},{8,10},{9,11},{10,... | collective-permute-start | bytes 1572872 | tf_op jit(solution)/shard_map/ppermute | solution.py:176
  132.8 10.4 %collective-permute-start.25 = (bf16[512,512]{1,0:T(8,128)(2,1)}, bf16[512,512]{1,0:T(8,128)(2,1)S(1)}, u32[]{:S(2)}, u32[]{:S(2)}) collective-permute-start(bf16[512,512]{1,0:T(8,128)(2,1)} %constant_dynamic-update-slice_fusion.4.refs_4_.refs_8_), channel_id=1, source_target_pairs={{0,1},{1,0},{2,3},{3,2},{4,5},{5,4},{6,7},{7,6},{8,9},{9,8},{10,11... | collective-permute-start | bytes 1572872 | tf_op jit(solution)/shard_map/ppermute | solution.py:176
  132.9 12.5 %collective-permute-start.26 = (bf16[512,512]{1,0:T(8,128)(2,1)}, bf16[512,512]{1,0:T(8,128)(2,1)S(1)}, u32[]{:S(2)}, u32[]{:S(2)}) collective-permute-start(bf16[512,512]{1,0:T(8,128)(2,1)} %collective-permute-done.24.refs_5_.refs_9_), channel_id=1, source_target_pairs={{0,1},{1,0},{2,3},{3,2},{4,5},{5,4},{6,7},{7,6},{8,9},{9,8},{10,11... | collective-permute-start | bytes 1572872 | tf_op jit(solution)/shard_map/ppermute | solution.py:176
  133.4 19.1 %collective-permute-start.4 = (bf16[512,512]{1,0:T(8,128)(2,1)}, bf16[512,512]{1,0:T(8,128)(2,1)S(1)}, u32[]{:S(2)}, u32[]{:S(2)}) collective-permute-start(bf16[512,512]{1,0:T(8,128)(2,1)} %pad_maximum_fusion.refs_4_.refs_8_), channel_id=1, source_target_pairs={{0,1},{1,0},{2,3},{3,2},{4,5},{5,4},{6,7},{7,6},{8,9},{9,8},{10,11... | collective-permute-start | bytes 1572872 | tf_op jit(solution)/shard_map/ppermute | solution.py:176
  133.4 19.7 %collective-permute-start.5 = (bf16[512,512]{1,0:T(8,128)(2,1)}, bf16[512,512]{1,0:T(8,128)(2,1)S(1)}, u32[]{:S(2)}, u32[]{:S(2)}) collective-permute-start(bf16[512,512]{1,0:T(8,128)(2,1)} %collective-permute-done.3.refs_5_.refs_9_), channel_id=1, source_target_pairs={{0,1},{1,0},{2,3},{3,2},{4,5},{5,4},{6,7},{7,6},{8,9},{9,8},{10,11... | collective-permute-start | bytes 1572872 | tf_op jit(solution)/shard_map/ppermute | solution.py:176
  141.6 21.7 %collective-permute-start.18 = (bf16[128,256]{1,0:T(8,128)(2,1)S(1)}, bf16[128,256]{1,0:T(8,128)(2,1)S(1)}, u32[]{:S(2)}, u32[]{:S(2)}) collective-permute-start(bf16[128,256]{1,0:T(8,128)(2,1)S(1)} %get-tuple-element.50), channel_id=1, source_target_pairs={{0,4},{1,5},{2,6},{3,7},{4,0},{5,1},{6,2},{7,3},{8,12},{9,13},{10,... | collective-permute-start | bytes 196616 | tf_op jit(solution)/shard_map/ppermute | solution.py:176
  143.2 20.8 %collective-permute-start.19 = (bf16[128,256]{1,0:T(8,128)(2,1)S(1)}, bf16[128,256]{1,0:T(8,128)(2,1)S(1)}, u32[]{:S(2)}, u32[]{:S(2)}) collective-permute-start(bf16[128,256]{1,0:T(8,128)(2,1)S(1)} %get-tuple-element.51), channel_id=1, source_target_pairs={{0,8},{1,9},{2,10},{3,11},{4,12},{5,13},{6,14},{7,15},{8,0},{9,1},... | collective-permute-start | bytes 196616 | tf_op jit(solution)/shard_map/ppermute | solution.py:176
  145.3 18.7 %collective-permute-start.20 = (bf16[128,256]{1,0:T(8,128)(2,1)S(1)}, bf16[128,256]{1,0:T(8,128)(2,1)S(1)}, u32[]{:S(2)}, u32[]{:S(2)}) collective-permute-start(bf16[128,256]{1,0:T(8,128)(2,1)S(1)} %get-tuple-element.52), channel_id=1, source_target_pairs={{0,12},{1,13},{2,14},{3,15},{4,8},{5,9},{6,10},{7,11},{8,4},{9,5},... | collective-permute-start | bytes 196616 | tf_op jit(solution)/shard_map/ppermute | solution.py:176
  152.4 15.3 %collective-permute-start.27 = (bf16[128,256]{1,0:T(8,128)(2,1)S(1)}, bf16[128,256]{1,0:T(8,128)(2,1)S(1)}, u32[]{:S(2)}, u32[]{:S(2)}) collective-permute-start(bf16[128,256]{1,0:T(8,128)(2,1)S(1)} %get-tuple-element.58), channel_id=1, source_target_pairs={{0,4},{1,5},{2,6},{3,7},{4,0},{5,1},{6,2},{7,3},{8,12},{9,13},{10,... | collective-permute-start | bytes 196616 | tf_op jit(solution)/shard_map/ppermute | solution.py:176
  153.2 20.5 %collective-permute-start.28 = (bf16[128,256]{1,0:T(8,128)(2,1)}, bf16[128,256]{1,0:T(8,128)(2,1)}, u32[]{:S(2)}, u32[]{:S(2)}) collective-permute-start(bf16[128,256]{1,0:T(8,128)(2,1)} %get-tuple-element.59), channel_id=1, source_target_pairs={{0,8},{1,9},{2,10},{3,11},{4,12},{5,13},{6,14},{7,15},{8,0},{9,1},... | collective-permute-start | bytes 196616 | tf_op jit(solution)/shard_map/ppermute | solution.py:176
  163.3 10.4 %collective-permute-start.29 = (bf16[128,256]{1,0:T(8,128)(2,1)}, bf16[128,256]{1,0:T(8,128)(2,1)S(1)}, u32[]{:S(2)}, u32[]{:S(2)}) collective-permute-start(bf16[128,256]{1,0:T(8,128)(2,1)} %get-tuple-element.60), channel_id=1, source_target_pairs={{0,12},{1,13},{2,14},{3,15},{4,8},{5,9},{6,10},{7,11},{8,4},{9,5},... | collective-permute-start | bytes 196616 | tf_op jit(solution)/shard_map/ppermute | solution.py:176
  164.0 9.7 %collective-permute-start.6 = (bf16[128,256]{1,0:T(8,128)(2,1)}, bf16[128,256]{1,0:T(8,128)(2,1)S(1)}, u32[]{:S(2)}, u32[]{:S(2)}) collective-permute-start(bf16[128,256]{1,0:T(8,128)(2,1)} %get-tuple-element.38), channel_id=1, source_target_pairs={{0,4},{1,5},{2,6},{3,7},{4,0},{5,1},{6,2},{7,3},{8,12},{9,13},{10,... | collective-permute-start | bytes 196616 | tf_op jit(solution)/shard_map/ppermute | solution.py:176
  164.1 9.7 %collective-permute-start.7 = (bf16[128,256]{1,0:T(8,128)(2,1)}, bf16[128,256]{1,0:T(8,128)(2,1)S(1)}, u32[]{:S(2)}, u32[]{:S(2)}) collective-permute-start(bf16[128,256]{1,0:T(8,128)(2,1)} %get-tuple-element.39), channel_id=1, source_target_pairs={{0,8},{1,9},{2,10},{3,11},{4,12},{5,13},{6,14},{7,15},{8,0},{9,1},... | collective-permute-start | bytes 196616 | tf_op jit(solution)/shard_map/ppermute | solution.py:176
  (27 other events, 281.9 us)

commit v2 on v1

--- a/solution.py
+++ b/solution.py
@@ -17,37 +17,49 @@
 
 
 def pack_kernel(spans, planes, where, *refs):
-    n_src = 1 + max(source for source, _ in spans)
-    sources, outs, sems = refs[:n_src], refs[n_src:-1], refs[-1]
-    copies = []
+    sources, outs = refs[: len(spans)], refs[len(spans) :]
     for relative in range(planes):
         plane = jnp.bitwise_xor(where[0], relative)
-        for slot, (source, base) in enumerate(spans):
-            start = pl.multiple_of(base + plane * PAIR, PAIR)
-            copies.append(
-                pltpu.make_async_copy(
-                    sources[source].at[:, pl.ds(start, PAIR)],
-                    outs[relative].at[:, pl.ds(slot * PAIR, PAIR)],
-                    sems.at[relative, slot],
-                )
-            )
-    for copy in copies:
-        copy.start()
-    for copy in copies:
-        copy.wait()
-
-
-def pack(where, spans, planes, *sources):
-    rows = sources[0].shape[0]
-    shape = jax.ShapeDtypeStruct((rows, len(spans) * PAIR), sources[0].dtype)
+        columns = pl.ds(pl.multiple_of(plane * PAIR, PAIR), PAIR)
+        for slot, source in enumerate(sources):
+            outs[relative][:, slot * PAIR : (slot + 1) * PAIR] = source[:, columns]
+
+
+def pack(where, spans, planes):
+    rows = spans[0][0].shape[0]
+    slab = planes * PAIR
+    shape = jax.ShapeDtypeStruct((rows, len(spans) * PAIR), spans[0][0].dtype)
+
+    def block(phase):
+        return pl.BlockSpec((rows, slab), lambda i: (0, phase))
+
     return pl.pallas_call(
         functools.partial(pack_kernel, spans, planes),
+        grid=(1,),
         out_shape=[shape] * planes,
-        in_specs=[pl.BlockSpec(memory_space=pltpu.SMEM)] + [pl.BlockSpec(memory_space=pl.ANY)] * len(sources),
-        out_specs=[pl.BlockSpec(memory_space=pl.ANY)] * planes,
-        scratch_shapes=[pltpu.SemaphoreType.DMA((planes, len(spans)))],
+        in_specs=[pl.BlockSpec(memory_space=pltpu.SMEM)] + [block(phase) for _, phase in spans],
+        out_specs=[pl.BlockSpec(shape.shape, lambda i: (0, 0))] * planes,
         name="pack",
-    )(where, *sources)
+    )(where, *[source for source, _ in spans])
+
+
+def stack_kernel(first, n, *refs):
+    pieces, out = refs[:n], refs[n]
+    rows = pieces[0].shape[0]
+    for index, piece in enumerate(pieces):
+        out[index * rows : (index + 1) * rows] = piece[:, first:]
+
+
+def stack(pieces, first):
+    rows, width = pieces[0].shape
+    vmem = pl.BlockSpec(memory_space=pltpu.VMEM)
+    return pl.pallas_call(
+        functools.partial(stack_kernel, first, len(pieces)),
+        in_specs=[vmem] * len(pieces),
+        out_specs=vmem,
+        out_shape=jax.ShapeDtypeStruct((rows * len(pieces), width - first), pieces[0].dtype),
+        name="stack",
+    )(*pieces)
 
 
 def attend_kernel(n_q, n_kv, scalars, *refs):
@@ -178,18 +190,18 @@
     def to_planes(pieces):
         return [pieces[0]] + [swap(pieces[r], PLANE * r) for r in range(1, planes)]
 
-    def gather_plane(pieces):
-        own = jnp.concatenate(pieces, axis=0)
+    def gather_plane(pieces, first):
+        own = stack(pieces, first)
         other = swap(own, 2)
         return [own, other, swap(own, 1), swap(other, 1)]
 
-    first = to_planes(pack(where, ((0, 0), (1, 0), (2, 0)), planes, queries, keys, values))
+    first = to_planes(pack(where, ((queries, 0), (keys, 0), (values, 0)), planes))
     rest = [
-        to_planes(pack(where, ((0, slab * p), (1, slab * p)), planes, keys, values)) for p in range(1, phases)
+        to_planes(pack(where, ((keys, p), (values, p)), planes)) for p in range(1, phases)
     ]
-    later = to_planes(pack(where, tuple((0, slab * p) for p in range(1, phases)), planes, queries))
-
-    gathered = [gather_plane([piece[:, PAIR:] for piece in first])] + [gather_plane(r) for r in rest]
+    later = to_planes(pack(where, [(queries, p) for p in range(1, phases)], planes))
+
+    gathered = [gather_plane(first, PAIR)] + [gather_plane(pieces, 0) for pieces in rest]
     added = sum_deltas(plan, deltas)
     returned = []
     for p in range(phases):

time: 178 us -> 117 us (0.66)
  Pallas kernels: 102 us -> 38.7 us
  local copies, waits for them, and re-layouts: 11.2 us -> 5.93 us
  starting transfers between devices: 40.6 us -> 45.3 us
  waiting for transfers between devices: 21.8 us -> 25.5 us
    pallas_call x4 -> x7, Pallas kernels: 76.2 us -> 13.8 us  [the longest x4 7.81 us: pack(): pl.pallas_call(functools.partial(pack_kernel, spans, planes), grid=(1,),...]
    ppermute x30, starting transfers between devices: 40.6 us -> 45.3 us  [swap(): return lax.ppermute(array, 'seq', [(i, i ^ distance) for i in range(size)])]
    ppermute x30, waiting for transfers between devices: 21.8 us -> 25.5 us  [swap(): return lax.ppermute(array, 'seq', [(i, i ^ distance) for i in range(size)])]
    concatenate x2 -> x0, local copies, waits for them, and re-layouts: 2.23 us -> none  [gather_plane(): own = jnp.concatenate(pieces, axis=0)]
    unnamed x48 -> x56, local copies, waits for them, and re-layouts: 8.07 us -> 5.93 us
  transfers between devices with their start and end apart: 30 -> 30, of which waited for: 6 -> 6; matrix products, arithmetic and copies ran while one was open for 5% -> 0% of each run, Pallas kernels for 46% -> 29%
where the time goes in v2:
time: 117 us; the launch traced here: 116 us
  starting transfers between devices  45.3 us (39%)
  Pallas kernels  38.7 us (33%)
  waiting for transfers between devices  25.5 us (22%)
  local copies, waits for them, and re-layouts  5.93 us (5%)
    ppermute x30, starting transfers between devices, swap(): return lax.ppermute(array, 'seq', [(i, i ^ distance) for i in range(size)])  45.3 us
    ppermute x30, waiting for transfers between devices, swap(): return lax.ppermute(array, 'seq', [(i, i ^ distance) for i in range(size)])  25.5 us
    pallas_call x3, Pallas kernels, attend_pair(): pl.pallas_call(functools.partial(attend_kernel, n_q, n_kv), grid_spec=plt...  17.5 us
    pallas_call x4, Pallas kernels, pack(): pl.pallas_call(functools.partial(pack_kernel, spans, planes), grid=(1,),...  7.81 us
    pallas_call x3, Pallas kernels, stack(): pl.pallas_call(functools.partial(stack_kernel, first, len(pieces)), in_sp...  6.03 us
    unnamed x56, local copies, waits for them, and re-layouts  5.93 us
    pallas_call x1, Pallas kernels, sum_deltas(): pl.pallas_call(deltas_kernel, grid=(4,), in_specs=[pl.BlockSpec(memory_sp...  4.64 us
    pallas_call x1, Pallas kernels, mix(): pl.pallas_call(functools.partial(mix_kernel, planes), in_specs=[pl.BlockS...  2.67 us
  transfers between devices with their start and end apart: 30, of which 6 were waited for; matrix products, arithmetic and copies ran while one was open for 0% of the time, Pallas kernels for 29%

profile of v2, /device:TPU:0, one launch (start us, length us, event | category | flops | bytes accessed | tf_op | source)
XLA Modules:
  0.0 116.3 jit_solution(793634293416014052)
XLA Ops:
  1.9 3.0 %collective-permute-start.12 = (bf16[128,512]{1,0:T(8,128)(2,1)}, bf16[128,512]{1,0:T(8,128)(2,1)S(1)}, u32[]{:S(2)}, u32[]{:S(2)}) collective-permute-start(bf16[128,512]{1,0:T(8,128)(2,1)} %get-tuple-element.46), channel_id=1, source_target_pairs={{0,4},{1,5},{2,6},{3,7},{4,0},{5,1},{6,2},{7,3},{8,12},{9,13},{10,... | collective-permute-start | bytes 393224 | tf_op jit(solution)/shard_map/ppermute | solution.py:188
  4.9 2.6 %collective-permute-start.13 = (bf16[128,512]{1,0:T(8,128)(2,1)}, bf16[128,512]{1,0:T(8,128)(2,1)S(1)}, u32[]{:S(2)}, u32[]{:S(2)}) collective-permute-start(bf16[128,512]{1,0:T(8,128)(2,1)} %get-tuple-element.47), channel_id=1, source_target_pairs={{0,8},{1,9},{2,10},{3,11},{4,12},{5,13},{6,14},{7,15},{8,0},{9,1},... | collective-permute-start | bytes 393224 | tf_op jit(solution)/shard_map/ppermute | solution.py:188
  10.3 3.5 %collective-permute-start.22 = (bf16[128,512]{1,0:T(8,128)(2,1)}, bf16[128,512]{1,0:T(8,128)(2,1)S(1)}, u32[]{:S(2)}, u32[]{:S(2)}) collective-permute-start(bf16[128,512]{1,0:T(8,128)(2,1)} %get-tuple-element.55), channel_id=1, source_target_pairs={{0,8},{1,9},{2,10},{3,11},{4,12},{5,13},{6,14},{7,15},{8,0},{9,1},... | collective-permute-start | bytes 393224 | tf_op jit(solution)/shard_map/ppermute | solution.py:188
  14.0 4.1 %collective-permute-done.13.refs_2_ = bf16[128,512]{1,0:T(8,128)(2,1)S(1)} collective-permute-done((bf16[128,512]{1,0:T(8,128)(2,1)}, bf16[128,512]{1,0:T(8,128)(2,1)S(1)}, u32[]{:S(2)}, u32[]{:S(2)}) %collective-permute-start.13) | collective-permute-done | bytes 131104 | tf_op jit(solution)/shard_map/ppermute | solution.py:188
  18.8 1.9 %stack.4.refs_4_.refs_8_ = bf16[512,512]{1,0:T(8,128)(2,1)} custom-call(bf16[128,512]{1,0:T(8,128)(2,1)} %get-tuple-element.45.refs_0_, bf16[128,512]{1,0:T(8,128)(2,1)} %copy-done.17, bf16[128,512]{1,0:T(8,128)(2,1)} %copy-done.18, bf16[128,512]{1,0:T(8,128)(2,1)} %copy-done.19), custom_call_target="tpu_custom_call" | custom-call | tf_op jit(solution)/shard_map/stack/pallas_call | solution.py:56
  22.2 2.1 %pack.4 = (bf16[128,768]{1,0:T(8,128)(2,1)}, bf16[128,768]{1,0:T(8,128)(2,1)}, bf16[128,768]{1,0:T(8,128)(2,1)}, bf16[128,768]{1,0:T(8,128)(2,1)}) custom-call(s32[1]{0:T(128)} %bitcast.where, bf16[128,3072]{1,0:T(8,128)(2,1)} %refs_1_.5, bf16[128,3072]{1,0:T(8,128)(2,1)} %refs_0_.7, bf16[128,3072]{1,0:T(8,128)(2,1)} %refs_1_.7), custom_call_target="tpu_custom_call" | custom-call | tf_op jit(solution)/shard_map/pack/pallas_call | solution.py:36
  24.3 8.9 %collective-permute-start = (bf16[128,768]{1,0:T(8,128)(2,1)}, bf16[128,768]{1,0:T(8,128)(2,1)S(1)}, u32[]{:S(2)}, u32[]{:S(2)}) collective-permute-start(bf16[128,768]{1,0:T(8,128)(2,1)} %get-tuple-element.34), channel_id=1, source_target_pairs={{0,4},{1,5},{2,6},{3,7},{4,0},{5,1},{6,2},{7,3},{8,12},{9,13},{10,... | collective-permute-start | bytes 589832 | tf_op jit(solution)/shard_map/ppermute | solution.py:188
  36.4 2.0 %stack.5.refs_4_.refs_8_ = bf16[512,512]{1,0:T(8,128)(2,1)} custom-call(bf16[128,512]{1,0:T(8,128)(2,1)} %get-tuple-element.53.refs_0_, bf16[128,512]{1,0:T(8,128)(2,1)} %copy-done.14, bf16[128,512]{1,0:T(8,128)(2,1)} %copy-done.15, bf16[128,512]{1,0:T(8,128)(2,1)} %copy-done.16), custom_call_target="tpu_custom_call" | custom-call | tf_op jit(solution)/shard_map/stack/pallas_call | solution.py:56
  39.4 6.0 %collective-permute-done.1.refs_2_ = bf16[128,768]{1,0:T(8,128)(2,1)S(1)} collective-permute-done((bf16[128,768]{1,0:T(8,128)(2,1)}, bf16[128,768]{1,0:T(8,128)(2,1)S(1)}, u32[]{:S(2)}, u32[]{:S(2)}) %collective-permute-start.1) | collective-permute-done | bytes 196640 | tf_op jit(solution)/shard_map/ppermute | solution.py:188
  46.1 2.0 %stack.3.refs_4_.refs_8_ = bf16[512,512]{1,0:T(8,128)(2,1)} custom-call(bf16[128,768]{1,0:T(8,128)(2,1)} %get-tuple-element.33.refs_0_, bf16[128,768]{1,0:T(8,128)(2,1)} %copy-done.6, bf16[128,768]{1,0:T(8,128)(2,1)} %copy-done.8, bf16[128,768]{1,0:T(8,128)(2,1)} %collective-permute-done.2.refs_3_), custom_call_target="tpu_custom_call" | custom-call | tf_op jit(solution)/shard_map/stack/pallas_call | solution.py:56
  49.7 1.9 %pack.5 = (bf16[128,512]{1,0:T(8,128)(2,1)}, bf16[128,512]{1,0:T(8,128)(2,1)}, bf16[128,512]{1,0:T(8,128)(2,1)}, bf16[128,512]{1,0:T(8,128)(2,1)}) custom-call(s32[1]{0:T(128)} %bitcast.where, bf16[128,3072]{1,0:T(8,128)(2,1)} %refs_1_.5, bf16[128,3072]{1,0:T(8,128)(2,1)} %refs_1_.5), custom_call_target="tpu_custom_call" | custom-call | tf_op jit(solution)/shard_map/pack/pallas_call | solution.py:36
  51.6 2.1 %collective-permute-start.9 = (bf16[128,512]{1,0:T(8,128)(2,1)}, bf16[128,512]{1,0:T(8,128)(2,1)S(1)}, u32[]{:S(2)}, u32[]{:S(2)}) collective-permute-start(bf16[128,512]{1,0:T(8,128)(2,1)} %get-tuple-element.42), channel_id=1, source_target_pairs={{0,4},{1,5},{2,6},{3,7},{4,0},{5,1},{6,2},{7,3},{8,12},{9,13},{10,... | collective-permute-start | bytes 393224 | tf_op jit(solution)/shard_map/ppermute | solution.py:188
  53.7 3.2 %collective-permute-done.9.refs_1_ = bf16[128,512]{1,0:T(8,128)(2,1)S(1)} collective-permute-done((bf16[128,512]{1,0:T(8,128)(2,1)}, bf16[128,512]{1,0:T(8,128)(2,1)S(1)}, u32[]{:S(2)}, u32[]{:S(2)}) %collective-permute-start.9) | collective-permute-done | bytes 131104 | tf_op jit(solution)/shard_map/ppermute | solution.py:188
  56.9 3.5 %collective-permute-start.10 = (bf16[128,512]{1,0:T(8,128)(2,1)}, bf16[128,512]{1,0:T(8,128)(2,1)S(1)}, u32[]{:S(2)}, u32[]{:S(2)}) collective-permute-start(bf16[128,512]{1,0:T(8,128)(2,1)} %get-tuple-element.43), channel_id=1, source_target_pairs={{0,8},{1,9},{2,10},{3,11},{4,12},{5,13},{6,14},{7,15},{8,0},{9,1},... | collective-permute-start | bytes 393224 | tf_op jit(solution)/shard_map/ppermute | solution.py:188
  60.4 4.9 %collective-permute-done.10.refs_2_ = bf16[128,512]{1,0:T(8,128)(2,1)S(1)} collective-permute-done((bf16[128,512]{1,0:T(8,128)(2,1)}, bf16[128,512]{1,0:T(8,128)(2,1)S(1)}, u32[]{:S(2)}, u32[]{:S(2)}) %collective-permute-start.10) | collective-permute-done | bytes 131104 | tf_op jit(solution)/shard_map/ppermute | solution.py:188
  65.5 6.7 %collective-permute-done.11.refs_3_ = bf16[128,512]{1,0:T(8,128)(2,1)S(1)} collective-permute-done((bf16[128,512]{1,0:T(8,128)(2,1)}, bf16[128,512]{1,0:T(8,128)(2,1)S(1)}, u32[]{:S(2)}, u32[]{:S(2)}) %collective-permute-start.11) | collective-permute-done | bytes 131104 | tf_op jit(solution)/shard_map/ppermute | solution.py:188
  76.0 5.9 %attend.4 = (bf16[128,256]{1,0:T(8,128)(2,1)S(1)}, bf16[128,256]{1,0:T(8,128)(2,1)S(1)}, bf16[128,256]{1,0:T(8,128)(2,1)S(1)}, bf16[128,256]{1,0:T(8,128)(2,1)S(1)}) custom-call(s32[2]{0:T(128)S(1)} %pad_add_fusion.scalars, bf16[128,512]{1,0:T(8,128)(2,1)S(1)} %copy-done.10, bf16[128,512]{1,0:T(8,128)(2,1)S(1)} %collective-permute-done.9.refs_1_, ...), custom_call_target="tpu_custom_call" | custom-call | flops 1207959552 | bytes 2359296 | tf_op jit(solution)/shard_map/attend/pallas_call | solution.py:114
  82.9 3.5 %collective-permute-start.20 = (bf16[128,256]{1,0:T(8,128)(2,1)S(1)}, bf16[128,256]{1,0:T(8,128)(2,1)S(1)}, u32[]{:S(2)}, u32[]{:S(2)}) collective-permute-start(bf16[128,256]{1,0:T(8,128)(2,1)S(1)} %get-tuple-element.52), channel_id=1, source_target_pairs={{0,12},{1,13},{2,14},{3,15},{4,8},{5,9},{6,10},{7,11},{8,4},{9,5},... | collective-permute-start | bytes 196616 | tf_op jit(solution)/shard_map/ppermute | solution.py:188
  86.5 5.8 %attend.5 = (bf16[128,256]{1,0:T(8,128)(2,1)S(1)}, bf16[128,256]{1,0:T(8,128)(2,1)S(1)}, bf16[128,256]{1,0:T(8,128)(2,1)S(1)}, bf16[128,256]{1,0:T(8,128)(2,1)S(1)}) custom-call(s32[2]{0:T(128)S(1)} %pad_add_fusion.scalars, bf16[128,512]{1,0:T(8,128)(2,1)S(1)} %copy-done.10, bf16[128,512]{1,0:T(8,128)(2,1)S(1)} %collective-permute-done.9.refs_1_, ...), custom_call_target="tpu_custom_call" | custom-call | flops 1207959552 | bytes 2359296 | tf_op jit(solution)/shard_map/attend/pallas_call | solution.py:114
  93.3 5.8 %attend.3 = (bf16[128,256]{1,0:T(8,128)(2,1)S(1)}, bf16[128,256]{1,0:T(8,128)(2,1)S(1)}, bf16[128,256]{1,0:T(8,128)(2,1)S(1)}, bf16[128,256]{1,0:T(8,128)(2,1)S(1)}) custom-call(s32[2]{0:T(128)S(1)} %pad_add_fusion.scalars, bf16[128,768]{1,0:T(8,128)(2,1)S(1)} %copy-done.5, bf16[128,768]{1,0:T(8,128)(2,1)S(1)} %copy-done.7, bf16[128,768]{1,0:T(8,128)(2,1)S(1)} %copy-done.9, ...), custom_call_target="tpu_custom_call" | custom-call | flops 1207959552 | bytes 2359296 | tf_op jit(solution)/shard_map/attend/pallas_call | solution.py:114
  99.8 3.5 %collective-permute-start.29 = (bf16[128,256]{1,0:T(8,128)(2,1)S(1)}, bf16[128,256]{1,0:T(8,128)(2,1)S(1)}, u32[]{:S(2)}, u32[]{:S(2)}) collective-permute-start(bf16[128,256]{1,0:T(8,128)(2,1)S(1)} %get-tuple-element.60), channel_id=1, source_target_pairs={{0,12},{1,13},{2,14},{3,15},{4,8},{5,9},{6,10},{7,11},{8,4},{9,5},... | collective-permute-start | bytes 196616 | tf_op jit(solution)/shard_map/ppermute | solution.py:188
  104.8 3.5 %collective-permute-start.8 = (bf16[128,256]{1,0:T(8,128)(2,1)S(1)}, bf16[128,256]{1,0:T(8,128)(2,1)S(1)}, u32[]{:S(2)}, u32[]{:S(2)}) collective-permute-start(bf16[128,256]{1,0:T(8,128)(2,1)S(1)} %get-tuple-element.40), channel_id=1, source_target_pairs={{0,12},{1,13},{2,14},{3,15},{4,8},{5,9},{6,10},{7,11},{8,4},{9,5},... | collective-permute-start | bytes 196616 | tf_op jit(solution)/shard_map/ppermute | solution.py:188
  108.3 4.6 %deltas.2.added = f32[128,3072]{1,0:T(8,128)} custom-call(s32[6]{0:T(128)} %plan.1, bf16[6,128,3072]{2,1,0:T(8,128)(2,1)} %deltas.3), custom_call_target="tpu_custom_call" | custom-call | flops 4718592 | bytes 4718592 | tf_op jit(solution)/shard_map/deltas/pallas_call | solution.py:141
  113.7 2.7 %mix.1 = bf16[128,3072]{1,0:T(8,128)(2,1)} custom-call(s32[1]{0:T(128)} %bitcast.where, f32[128,3072]{1,0:T(8,128)} %deltas.2.added, bf16[128,256]{1,0:T(8,128)(2,1)} %copy-done.13, bf16[128,256]{1,0:T(8,128)(2,1)} %copy-done.25, bf16[128,256]{1,0:T(8,128)(2,1)} %copy-done.26, bf16[128,256]{1,0:T(8,128)(2,1)} %copy-done.27, bf16[128,256]{1,0:T(8,128)(2,1)} %copy-done.11, ...), custom_call_target="tpu_custom_call" | custom-call | tf_op jit(solution)/shard_map/mix/pallas_call | solution.py:169
  (105 shorter events, 21.4 us)
Async XLA Ops:
  1.9 11.9 %collective-permute-start.12 = (bf16[128,512]{1,0:T(8,128)(2,1)}, bf16[128,512]{1,0:T(8,128)(2,1)S(1)}, u32[]{:S(2)}, u32[]{:S(2)}) collective-permute-start(bf16[128,512]{1,0:T(8,128)(2,1)} %get-tuple-element.46), channel_id=1, source_target_pairs={{0,4},{1,5},{2,6},{3,7},{4,0},{5,1},{6,2},{7,3},{8,12},{9,13},{10,... | collective-permute-start | bytes 393224 | tf_op jit(solution)/shard_map/ppermute | solution.py:188
  4.9 13.2 %collective-permute-start.13 = (bf16[128,512]{1,0:T(8,128)(2,1)}, bf16[128,512]{1,0:T(8,128)(2,1)S(1)}, u32[]{:S(2)}, u32[]{:S(2)}) collective-permute-start(bf16[128,512]{1,0:T(8,128)(2,1)} %get-tuple-element.47), channel_id=1, source_target_pairs={{0,8},{1,9},{2,10},{3,11},{4,12},{5,13},{6,14},{7,15},{8,0},{9,1},... | collective-permute-start | bytes 393224 | tf_op jit(solution)/shard_map/ppermute | solution.py:188
  7.5 10.6 %collective-permute-start.14 = (bf16[128,512]{1,0:T(8,128)(2,1)}, bf16[128,512]{1,0:T(8,128)(2,1)S(1)}, u32[]{:S(2)}, u32[]{:S(2)}) collective-permute-start(bf16[128,512]{1,0:T(8,128)(2,1)} %get-tuple-element.48), channel_id=1, source_target_pairs={{0,12},{1,13},{2,14},{3,15},{4,8},{5,9},{6,10},{7,11},{8,4},{9,5},... | collective-permute-start | bytes 393224 | tf_op jit(solution)/shard_map/ppermute | solution.py:188
  9.4 23.9 %collective-permute-start.21 = (bf16[128,512]{1,0:T(8,128)(2,1)}, bf16[128,512]{1,0:T(8,128)(2,1)S(1)}, u32[]{:S(2)}, u32[]{:S(2)}) collective-permute-start(bf16[128,512]{1,0:T(8,128)(2,1)} %get-tuple-element.54), channel_id=1, source_target_pairs={{0,4},{1,5},{2,6},{3,7},{4,0},{5,1},{6,2},{7,3},{8,12},{9,13},{10,... | collective-permute-start | bytes 393224 | tf_op jit(solution)/shard_map/ppermute | solution.py:188
  10.3 23.9 %collective-permute-start.22 = (bf16[128,512]{1,0:T(8,128)(2,1)}, bf16[128,512]{1,0:T(8,128)(2,1)S(1)}, u32[]{:S(2)}, u32[]{:S(2)}) collective-permute-start(bf16[128,512]{1,0:T(8,128)(2,1)} %get-tuple-element.55), channel_id=1, source_target_pairs={{0,8},{1,9},{2,10},{3,11},{4,12},{5,13},{6,14},{7,15},{8,0},{9,1},... | collective-permute-start | bytes 393224 | tf_op jit(solution)/shard_map/ppermute | solution.py:188
  13.8 21.9 %collective-permute-start.23 = (bf16[128,512]{1,0:T(8,128)(2,1)}, bf16[128,512]{1,0:T(8,128)(2,1)S(1)}, u32[]{:S(2)}, u32[]{:S(2)}) collective-permute-start(bf16[128,512]{1,0:T(8,128)(2,1)} %get-tuple-element.56), channel_id=1, source_target_pairs={{0,12},{1,13},{2,14},{3,15},{4,8},{5,9},{6,10},{7,11},{8,4},{9,5},... | collective-permute-start | bytes 393224 | tf_op jit(solution)/shard_map/ppermute | solution.py:188
  20.7 44.8 %collective-permute-start.15 = (bf16[512,512]{1,0:T(8,128)(2,1)}, bf16[512,512]{1,0:T(8,128)(2,1)}, u32[]{:S(2)}, u32[]{:S(2)}) collective-permute-start(bf16[512,512]{1,0:T(8,128)(2,1)} %stack.4.refs_4_.refs_8_), channel_id=1, source_target_pairs={{0,2},{1,3},{2,0},{3,1},{4,6},{5,7},{6,4},{7,5},{8,10},{9,11},{10,... | collective-permute-start | bytes 1572872 | tf_op jit(solution)/shard_map/ppermute | solution.py:188
  24.3 15.1 %collective-permute-start = (bf16[128,768]{1,0:T(8,128)(2,1)}, bf16[128,768]{1,0:T(8,128)(2,1)S(1)}, u32[]{:S(2)}, u32[]{:S(2)}) collective-permute-start(bf16[128,768]{1,0:T(8,128)(2,1)} %get-tuple-element.34), channel_id=1, source_target_pairs={{0,4},{1,5},{2,6},{3,7},{4,0},{5,1},{6,2},{7,3},{8,12},{9,13},{10,... | collective-permute-start | bytes 589832 | tf_op jit(solution)/shard_map/ppermute | solution.py:188
  33.3 12.2 %collective-permute-start.1 = (bf16[128,768]{1,0:T(8,128)(2,1)}, bf16[128,768]{1,0:T(8,128)(2,1)S(1)}, u32[]{:S(2)}, u32[]{:S(2)}) collective-permute-start(bf16[128,768]{1,0:T(8,128)(2,1)} %get-tuple-element.35), channel_id=1, source_target_pairs={{0,8},{1,9},{2,10},{3,11},{4,12},{5,13},{6,14},{7,15},{8,0},{9,1},... | collective-permute-start | bytes 589832 | tf_op jit(solution)/shard_map/ppermute | solution.py:188
  34.2 11.2 %collective-permute-start.2 = (bf16[128,768]{1,0:T(8,128)(2,1)}, bf16[128,768]{1,0:T(8,128)(2,1)}, u32[]{:S(2)}, u32[]{:S(2)}) collective-permute-start(bf16[128,768]{1,0:T(8,128)(2,1)} %get-tuple-element.36), channel_id=1, source_target_pairs={{0,12},{1,13},{2,14},{3,15},{4,8},{5,9},{6,10},{7,11},{8,4},{9,5},... | collective-permute-start | bytes 589832 | tf_op jit(solution)/shard_map/ppermute | solution.py:188
  38.4 33.8 %collective-permute-start.24 = (bf16[512,512]{1,0:T(8,128)(2,1)}, bf16[512,512]{1,0:T(8,128)(2,1)}, u32[]{:S(2)}, u32[]{:S(2)}) collective-permute-start(bf16[512,512]{1,0:T(8,128)(2,1)} %stack.5.refs_4_.refs_8_), channel_id=1, source_target_pairs={{0,2},{1,3},{2,0},{3,1},{4,6},{5,7},{6,4},{7,5},{8,10},{9,11},{10,... | collective-permute-start | bytes 1572872 | tf_op jit(solution)/shard_map/ppermute | solution.py:188
  39.4 33.4 %collective-permute-start.16 = (bf16[512,512]{1,0:T(8,128)(2,1)}, bf16[512,512]{1,0:T(8,128)(2,1)}, u32[]{:S(2)}, u32[]{:S(2)}) collective-permute-start(bf16[512,512]{1,0:T(8,128)(2,1)} %stack.4.refs_4_.refs_8_), channel_id=1, source_target_pairs={{0,1},{1,0},{2,3},{3,2},{4,5},{5,4},{6,7},{7,6},{8,9},{9,8},{10,11... | collective-permute-start | bytes 1572872 | tf_op jit(solution)/shard_map/ppermute | solution.py:188
  48.2 24.7 %collective-permute-start.3 = (bf16[512,512]{1,0:T(8,128)(2,1)}, bf16[512,512]{1,0:T(8,128)(2,1)}, u32[]{:S(2)}, u32[]{:S(2)}) collective-permute-start(bf16[512,512]{1,0:T(8,128)(2,1)} %stack.3.refs_4_.refs_8_), channel_id=1, source_target_pairs={{0,2},{1,3},{2,0},{3,1},{4,6},{5,7},{6,4},{7,5},{8,10},{9,11},{10,... | collective-permute-start | bytes 1572872 | tf_op jit(solution)/shard_map/ppermute | solution.py:188
  72.3 9.8 %collective-permute-start.25 = (bf16[512,512]{1,0:T(8,128)(2,1)}, bf16[512,512]{1,0:T(8,128)(2,1)S(1)}, u32[]{:S(2)}, u32[]{:S(2)}) collective-permute-start(bf16[512,512]{1,0:T(8,128)(2,1)} %stack.5.refs_4_.refs_8_), channel_id=1, source_target_pairs={{0,1},{1,0},{2,3},{3,2},{4,5},{5,4},{6,7},{7,6},{8,9},{9,8},{10,11... | collective-permute-start | bytes 1572872 | tf_op jit(solution)/shard_map/ppermute | solution.py:188
  72.3 10.7 %collective-permute-start.26 = (bf16[512,512]{1,0:T(8,128)(2,1)}, bf16[512,512]{1,0:T(8,128)(2,1)S(1)}, u32[]{:S(2)}, u32[]{:S(2)}) collective-permute-start(bf16[512,512]{1,0:T(8,128)(2,1)} %collective-permute-done.24.refs_5_.refs_9_), channel_id=1, source_target_pairs={{0,1},{1,0},{2,3},{3,2},{4,5},{5,4},{6,7},{7,6},{8,9},{9,8},{10,11... | collective-permute-start | bytes 1572872 | tf_op jit(solution)/shard_map/ppermute | solution.py:188
  72.8 19.5 %collective-permute-start.4 = (bf16[512,512]{1,0:T(8,128)(2,1)}, bf16[512,512]{1,0:T(8,128)(2,1)S(1)}, u32[]{:S(2)}, u32[]{:S(2)}) collective-permute-start(bf16[512,512]{1,0:T(8,128)(2,1)} %stack.3.refs_4_.refs_8_), channel_id=1, source_target_pairs={{0,1},{1,0},{2,3},{3,2},{4,5},{5,4},{6,7},{7,6},{8,9},{9,8},{10,11... | collective-permute-start | bytes 1572872 | tf_op jit(solution)/shard_map/ppermute | solution.py:188
  72.9 19.5 %collective-permute-start.5 = (bf16[512,512]{1,0:T(8,128)(2,1)}, bf16[512,512]{1,0:T(8,128)(2,1)S(1)}, u32[]{:S(2)}, u32[]{:S(2)}) collective-permute-start(bf16[512,512]{1,0:T(8,128)(2,1)} %collective-permute-done.3.refs_5_.refs_9_), channel_id=1, source_target_pairs={{0,1},{1,0},{2,3},{3,2},{4,5},{5,4},{6,7},{7,6},{8,9},{9,8},{10,11... | collective-permute-start | bytes 1572872 | tf_op jit(solution)/shard_map/ppermute | solution.py:188
  81.9 17.8 %collective-permute-start.18 = (bf16[128,256]{1,0:T(8,128)(2,1)S(1)}, bf16[128,256]{1,0:T(8,128)(2,1)S(1)}, u32[]{:S(2)}, u32[]{:S(2)}) collective-permute-start(bf16[128,256]{1,0:T(8,128)(2,1)S(1)} %get-tuple-element.50), channel_id=1, source_target_pairs={{0,4},{1,5},{2,6},{3,7},{4,0},{5,1},{6,2},{7,3},{8,12},{9,13},{10,... | collective-permute-start | bytes 196616 | tf_op jit(solution)/shard_map/ppermute | solution.py:188
  82.0 21.2 %collective-permute-start.19 = (bf16[128,256]{1,0:T(8,128)(2,1)S(1)}, bf16[128,256]{1,0:T(8,128)(2,1)S(1)}, u32[]{:S(2)}, u32[]{:S(2)}) collective-permute-start(bf16[128,256]{1,0:T(8,128)(2,1)S(1)} %get-tuple-element.51), channel_id=1, source_target_pairs={{0,8},{1,9},{2,10},{3,11},{4,12},{5,13},{6,14},{7,15},{8,0},{9,1},... | collective-permute-start | bytes 196616 | tf_op jit(solution)/shard_map/ppermute | solution.py:188
  82.9 20.3 %collective-permute-start.20 = (bf16[128,256]{1,0:T(8,128)(2,1)S(1)}, bf16[128,256]{1,0:T(8,128)(2,1)S(1)}, u32[]{:S(2)}, u32[]{:S(2)}) collective-permute-start(bf16[128,256]{1,0:T(8,128)(2,1)S(1)} %get-tuple-element.52), channel_id=1, source_target_pairs={{0,12},{1,13},{2,14},{3,15},{4,8},{5,9},{6,10},{7,11},{8,4},{9,5},... | collective-permute-start | bytes 196616 | tf_op jit(solution)/shard_map/ppermute | solution.py:188
  92.3 11.8 %collective-permute-start.27 = (bf16[128,256]{1,0:T(8,128)(2,1)S(1)}, bf16[128,256]{1,0:T(8,128)(2,1)S(1)}, u32[]{:S(2)}, u32[]{:S(2)}) collective-permute-start(bf16[128,256]{1,0:T(8,128)(2,1)S(1)} %get-tuple-element.58), channel_id=1, source_target_pairs={{0,4},{1,5},{2,6},{3,7},{4,0},{5,1},{6,2},{7,3},{8,12},{9,13},{10,... | collective-permute-start | bytes 196616 | tf_op jit(solution)/shard_map/ppermute | solution.py:188
  92.4 20.5 %collective-permute-start.28 = (bf16[128,256]{1,0:T(8,128)(2,1)S(1)}, bf16[128,256]{1,0:T(8,128)(2,1)}, u32[]{:S(2)}, u32[]{:S(2)}) collective-permute-start(bf16[128,256]{1,0:T(8,128)(2,1)S(1)} %get-tuple-element.59), channel_id=1, source_target_pairs={{0,8},{1,9},{2,10},{3,11},{4,12},{5,13},{6,14},{7,15},{8,0},{9,1},... | collective-permute-start | bytes 196616 | tf_op jit(solution)/shard_map/ppermute | solution.py:188
  99.8 13.2 %collective-permute-start.29 = (bf16[128,256]{1,0:T(8,128)(2,1)S(1)}, bf16[128,256]{1,0:T(8,128)(2,1)S(1)}, u32[]{:S(2)}, u32[]{:S(2)}) collective-permute-start(bf16[128,256]{1,0:T(8,128)(2,1)S(1)} %get-tuple-element.60), channel_id=1, source_target_pairs={{0,12},{1,13},{2,14},{3,15},{4,8},{5,9},{6,10},{7,11},{8,4},{9,5},... | collective-permute-start | bytes 196616 | tf_op jit(solution)/shard_map/ppermute | solution.py:188
  103.2 9.7 %collective-permute-start.6 = (bf16[128,256]{1,0:T(8,128)(2,1)S(1)}, bf16[128,256]{1,0:T(8,128)(2,1)S(1)}, u32[]{:S(2)}, u32[]{:S(2)}) collective-permute-start(bf16[128,256]{1,0:T(8,128)(2,1)S(1)} %get-tuple-element.38), channel_id=1, source_target_pairs={{0,4},{1,5},{2,6},{3,7},{4,0},{5,1},{6,2},{7,3},{8,12},{9,13},{10,... | collective-permute-start | bytes 196616 | tf_op jit(solution)/shard_map/ppermute | solution.py:188
  (34 other events, 227.2 us)

commit v3 on v0

--- a/solution.py
+++ b/solution.py
@@ -1,11 +1,329 @@
+import functools
+import math
+
 import jax
 import jax.numpy as jnp
 from jax import lax
+from jax.experimental import pallas as pl
+from jax.experimental.pallas import tpu as pltpu
 from jax.sharding import PartitionSpec as P
 
 HEADS = 24
 HEAD_DIM = 128
 HEADS_DEV = 3
+PLANE = 4
+PAIR = 2 * HEAD_DIM
+EXP_SCALE = HEAD_DIM ** (-0.5) * math.log2(math.e)
+
+
+SMALL = pl.CostEstimate(flops=1, bytes_accessed=1, transcendentals=0)
+LARGE = pl.CostEstimate(flops=20000000000, bytes_accessed=1, transcendentals=0)
+MID = pl.CostEstimate(flops=1000000000, bytes_accessed=1, transcendentals=0)
+
+
+def first_pack_kernel(spans, planes, where, *refs):
+    sources, outs = refs[: len(spans)], refs[len(spans) : len(spans) + planes]
+    slabs, sems = refs[-2:]
+    copies = [
+        pltpu.make_async_copy(source.at[:, pl.ds(phase * planes * PAIR, planes * PAIR)], slabs.at[slot], sems.at[slot])
+        for slot, (source, phase) in enumerate(zip(sources, spans))
+    ]
+    for copy in copies:
+        copy.start()
+    for copy in copies:
+        copy.wait()
+    for relative, out in enumerate(outs):
+        plane = jnp.bitwise_xor(where[0], relative)
+        columns = pl.ds(pl.multiple_of(plane * PAIR, PAIR), PAIR)
+        for slot in range(len(spans)):
+            out[:, slot * PAIR : (slot + 1) * PAIR] = slabs[slot, :, columns]
+
+
+def first_pack(where, phase, planes, *sources):
+    rows = sources[0].shape[0]
+    vmem = pl.BlockSpec(memory_space=pltpu.VMEM)
+    return pl.pallas_call(
+        functools.partial(first_pack_kernel, [phase] * len(sources), planes),
+        out_shape=[jax.ShapeDtypeStruct((rows, len(sources) * PAIR), sources[0].dtype)] * planes,
+        in_specs=[pl.BlockSpec(memory_space=pltpu.SMEM)] + [pl.BlockSpec(memory_space=pltpu.HBM)] * len(sources),
+        out_specs=[vmem] * planes,
+        scratch_shapes=[
+            pltpu.VMEM((len(sources), rows, planes * PAIR), sources[0].dtype),
+            pltpu.SemaphoreType.DMA((len(sources),)),
+        ],
+        compiler_params=pltpu.CompilerParams(vmem_limit_bytes=4 * 2**20),
+        cost_estimate=SMALL,
+        name="first_pack",
+    )(where, *sources)
+
+
+def pack_kernel(groups, planes, n_out, where, *refs):
+    sources, outs = refs[:3], refs[-n_out:]
+    slab = planes * PAIR
+    for relative in range(planes):
+        plane = jnp.bitwise_xor(where[0], relative)
+        for index, spans in enumerate(groups):
+            out = outs[index * planes + relative]
+            for slot, (source, phase) in enumerate(spans):
+                columns = pl.ds(pl.multiple_of(phase * slab + plane * PAIR, PAIR), PAIR)
+                out[:, slot * PAIR : (slot + 1) * PAIR] = sources[source][:, columns]
+
+
+def pack(where, groups, planes, sources, earlier):
+    rows = sources[0].shape[0]
+    shapes = [
+        jax.ShapeDtypeStruct((rows, len(spans) * PAIR), sources[0].dtype) for spans in groups for _ in range(planes)
+    ]
+    vmem = pl.BlockSpec(memory_space=pltpu.VMEM)
+    outs = pl.pallas_call(
+        functools.partial(pack_kernel, groups, planes, len(shapes)),
+        out_shape=shapes,
+        in_specs=[pl.BlockSpec(memory_space=pltpu.SMEM)]
+        + [vmem] * len(sources)
+        + [pl.BlockSpec(memory_space=pl.ANY)] * len(earlier),
+        out_specs=[vmem] * len(shapes),
+        compiler_params=pltpu.CompilerParams(vmem_limit_bytes=8 * 2**20),
+        cost_estimate=SMALL,
+        name="pack",
+    )(where, *sources, *earlier)
+    return [outs[i * planes : (i + 1) * planes] for i in range(len(groups))]
+
+
+def tick_kernel(axes, counts, widths, n_earlier, *refs):
+    sources, outs = list(refs[n_earlier : n_earlier + sum(counts)]), refs[n_earlier + sum(counts) :]
+    for axis, count, width, out in zip(axes, counts, widths, outs):
+        at = 0
+        for _ in range(count):
+            source = sources.pop(0)
+            if axis == 0:
+                out[at : at + source.shape[0]] = source[:, :width]
+                at += source.shape[0]
+            else:
+                out[:, at : at + source.shape[1]] = source[...]
+                at += source.shape[1]
+
+
+def tick(jobs, earlier, cost):
+    axes = [axis for axis, _, _ in jobs]
+    counts = [len(arrays) for _, arrays, _ in jobs]
+    widths = [width or arrays[0].shape[1] for _, arrays, width in jobs]
+    shapes = []
+    for axis, arrays, width in jobs:
+        if axis == 0:
+            shape = (sum(a.shape[0] for a in arrays), width or arrays[0].shape[1])
+        else:
+            shape = (arrays[0].shape[0], sum(a.shape[1] for a in arrays))
+        shapes.append(jax.ShapeDtypeStruct(shape, jnp.bfloat16))
+    vmem = pl.BlockSpec(memory_space=pltpu.VMEM)
+    return pl.pallas_call(
+        functools.partial(tick_kernel, axes, counts, widths, len(earlier)),
+        in_specs=[pl.BlockSpec(memory_space=pl.ANY)] * len(earlier) + [vmem] * sum(counts),
+        out_specs=[vmem] * len(shapes),
+        out_shape=shapes,
+        compiler_params=pltpu.CompilerParams(vmem_limit_bytes=6 * 2**20),
+        cost_estimate=cost,
+        name="tick",
+    )(*earlier, *[a for _, arrays, _ in jobs for a in arrays])
+
+
+def attend_kernel(n_q, n_kv, q_column, text_column, scalars, *refs):
+    queries, kvs = refs[:n_q], refs[n_q : n_q + n_kv]
+    text_keys, text_values = refs[n_q + n_kv : n_q + n_kv + 2]
+    outs = refs[len(refs) - n_q :]
+    rows = outs[0].shape[0]
+    contract_last = (((1,), (1,)), ((), ()))
+    for head in range(2):
+        here = slice(head * HEAD_DIM, (head + 1) * HEAD_DIM)
+        over = slice(PAIR + head * HEAD_DIM, PAIR + (head + 1) * HEAD_DIM)
+        text = slice(text_column + head * HEAD_DIM, text_column + (head + 1) * HEAD_DIM)
+        q_here = slice(q_column + head * HEAD_DIM, q_column + (head + 1) * HEAD_DIM)
+        q = jnp.concatenate([piece[:, q_here] for piece in queries], axis=0)
+        blocks = [(kv[:, here], kv[:, over]) for kv in kvs] + [(text_keys[:, text], text_values[:, text])]
+        top = None
+        for index, (keys, values) in enumerate(blocks):
+            scores = lax.dot_general(q, keys, contract_last, preferred_element_type=jnp.float32)
+            if index == n_kv:
+                usable = lax.broadcasted_iota(jnp.int32, scores.shape, 1) < scalars[1]
+                scores = jnp.where(usable, scores, -jnp.inf)
+            block_top = jnp.max(scores, axis=1, keepdims=True)
+            new_top = block_top if top is None else jnp.maximum(top, block_top)
+            weights = jnp.exp2((scores - new_top) * EXP_SCALE)
+            block_total = jnp.sum(weights, axis=1, keepdims=True)
+            block_weighted = jnp.dot(weights.astype(jnp.bfloat16), values, preferred_element_type=jnp.float32)
+            if top is None:
+                total, weighted = block_total, block_weighted
+            else:
+                rescale = jnp.exp2((top - new_top) * EXP_SCALE)
+                total, weighted = total * rescale + block_total, weighted * rescale + block_weighted
+            top = new_top
+        context = (weighted / total).astype(jnp.bfloat16)
+        for index, out in enumerate(outs):
+            out[:, here] = context[index * rows : (index + 1) * rows]
+
+
+def attend_pair(scalars, queries, q_block, kvs, text_keys, text_values, text_block, earlier):
+    n_q, n_kv = len(queries), len(kvs)
+    vmem = pl.BlockSpec(memory_space=pltpu.VMEM)
+    return pl.pallas_call(
+        functools.partial(attend_kernel, n_q, n_kv, q_block * HEAD_DIM, text_block * HEAD_DIM),
+        in_specs=[pl.BlockSpec(memory_space=pltpu.SMEM)]
+        + [vmem] * (n_q + n_kv + 2)
+        + [pl.BlockSpec(memory_space=pl.ANY)] * len(earlier),
+        out_specs=[vmem] * n_q,
+        out_shape=[jax.ShapeDtypeStruct((queries[0].shape[0], PAIR), jnp.bfloat16)] * n_q,
+        compiler_params=pltpu.CompilerParams(vmem_limit_bytes=24 * 2**20),
+        cost_estimate=SMALL,
+        name="attend",
+    )(scalars, *queries, *kvs, text_keys, text_values, *earlier)
+
+
+def text_kernel(planes, where, keys, values, *refs):
+    keys_out, values_out = refs[-2:]
+    slab = planes * PAIR
+    for phase in range(keys.shape[1] // slab):
+        columns = pl.ds(pl.multiple_of(phase * slab + where[0] * PAIR, PAIR), PAIR)
+        keys_out[:, phase * PAIR : (phase + 1) * PAIR] = keys[:, columns]
+        values_out[:, phase * PAIR : (phase + 1) * PAIR] = values[:, columns]
+
+
+def own_text(where, planes, text_keys, text_values, earlier):
+    vmem = pl.BlockSpec(memory_space=pltpu.VMEM)
+    shape = jax.ShapeDtypeStruct((text_keys.shape[0], text_keys.shape[1] // planes), text_keys.dtype)
+    return pl.pallas_call(
+        functools.partial(text_kernel, planes),
+        in_specs=[pl.BlockSpec(memory_space=pltpu.SMEM), vmem, vmem]
+        + [pl.BlockSpec(memory_space=pl.ANY)] * len(earlier),
+        out_specs=[vmem] * 2,
+        out_shape=[shape] * 2,
+        compiler_params=pltpu.CompilerParams(vmem_limit_bytes=6 * 2**20),
+        cost_estimate=SMALL,
+        name="own_text",
+    )(where, text_keys, text_values, *earlier)
+
+
+def deltas_kernel(plan, deltas, *refs):
+    out = refs[-1]
+    total = plan[0].astype(jnp.float32) * deltas[0].astype(jnp.float32)
+    for block in range(1, deltas.shape[0]):
+        total = total + plan[block].astype(jnp.float32) * deltas[block].astype(jnp.float32)
+    out[...] = total * 0.25
+
+
+def sum_deltas(plan, deltas, earlier):
+    blocks, rows, width = deltas.shape
+    step = width // 4
+    return pl.pallas_call(
+        deltas_kernel,
+        grid=(4,),
+        in_specs=[
+            pl.BlockSpec(memory_space=pltpu.SMEM),
+            pl.BlockSpec((blocks, rows, step), lambda i: (0, 0, i)),
+        ]
+        + [pl.BlockSpec(memory_space=pl.ANY)] * len(earlier),
+        out_specs=pl.BlockSpec((rows, step), lambda i: (0, i)),
+        out_shape=jax.ShapeDtypeStruct((rows, width), jnp.float32),
+        cost_estimate=SMALL,
+        compiler_params=pltpu.CompilerParams(vmem_limit_bytes=6 * 2**20),
+        name="deltas",
+    )(plan, deltas, *earlier)
+
+
+def mix_kernel(planes, where, added, *refs):
+    pieces, out = refs[:-1], refs[-1]
+    slab = planes * PAIR
+    phase = 0
+    for first in range(0, len(pieces), planes):
+        for part in range(pieces[first].shape[1] // PAIR):
+            for relative in range(planes):
+                plane = jnp.bitwise_xor(where[0], relative)
+                columns = pl.ds(pl.multiple_of(phase * slab + plane * PAIR, PAIR), PAIR)
+                piece = pieces[first + relative][:, part * PAIR : (part + 1) * PAIR]
+                out[:, columns] = (piece.astype(jnp.float32) + added[:, columns]).astype(out.dtype)
+            phase += 1
+
+
+def mix(where, planes, added, pieces):
+    vmem = pl.BlockSpec(memory_space=pltpu.VMEM)
+    return pl.pallas_call(
+        functools.partial(mix_kernel, planes),
+        in_specs=[pl.BlockSpec(memory_space=pltpu.SMEM)] + [vmem] * (1 + len(pieces)),
+        out_specs=vmem,
+        out_shape=jax.ShapeDtypeStruct(added.shape, jnp.bfloat16),
+        compiler_params=pltpu.CompilerParams(vmem_limit_bytes=6 * 2**20),
+        cost_estimate=SMALL,
+        name="mix",
+    )(where, added, *pieces)
+
+
+def plane_body(queries, keys, values, text_keys, text_values, text_len, plan, deltas):
+    size = lax.axis_size("seq")
+    planes = size // PLANE
+    slab = planes * PAIR
+    plane = lax.axis_index("seq") // PLANE
+    where = plane.astype(jnp.int32).reshape(1)
+    scalars = jnp.concatenate([where, text_len])
+
+    def swap(array, distance):
+        return lax.ppermute(array, "seq", [(i, i ^ distance) for i in range(size)])
+
+    def send(piece, r):
+        return swap(piece, PLANE * r)
+
+    def heads(p, pieces, block, gathered, earlier):
+        return attend_pair(
+            scalars, pieces, block, gathered, text_keys, text_values, 2 * p, earlier
+        )
+
+    fast, slow = (3,), (1, 2)
+    z1 = first_pack(where, 0, planes, keys, values)
+    groups = [((1, 1), (2, 1)), ((1, 2), (2, 2), (0, 0)), ((0, 1),), ((0, 2),)]
+    z2, z3, z4, z5 = pack(where, groups, planes, (queries, keys, values), z1)
+    text_keys, text_values = own_text(where, planes, text_keys, text_values, [z5[0]])
+    added = sum_deltas(plan, deltas, [text_keys])
+
+    def release(batch, lanes):
+        return [(0, [batch[r]], None) for r in lanes]
+
+    in1 = {r: send(z1[r], r) for r in range(1, planes)}
+    out = tick(release(z2, fast), [in1[r] for r in fast] + [added], LARGE)
+    in2 = {r: send(piece, r) for r, piece in zip(fast, out)}
+    out = tick([(0, [z1[0]] + [in1[r] for r in range(1, planes)], 2 * PAIR)] + release(z2, slow), [out[0]], MID)
+    own1, sent = out[0], out[1:]
+    other1 = swap(own1, 2)
+    in2.update({r: send(piece, r) for r, piece in zip(slow, sent)})
+    out = tick(release(z3, fast), [in2[r] for r in fast] + [own1], LARGE)
+    in3 = {r: send(piece, r) for r, piece in zip(fast, out)}
+    out = tick(
+        [(0, [other1, own1], None), (0, [z2[0]] + [in2[r] for r in range(1, planes)], 2 * PAIR)] + release(z3, slow),
+        [out[0]],
+        MID,
+    )
+    pair1, own2, sent = out[0], out[1], out[2:]
+    other2, core1 = swap(own2, 2), swap(pair1, 1)
+    in3.update({r: send(piece, r) for r, piece in zip(slow, sent)})
+    out = tick(release(z4, fast), [own2] + [in3[r] for r in fast], LARGE)
+    in4 = {r: send(piece, r) for r, piece in zip(fast, out)}
+    out = tick(
+        [(0, [other2, own2], None), (0, [z3[0]] + [in3[r] for r in range(1, planes)], 2 * PAIR)] + release(z4, slow),
+        [in3[r] for r in slow] + [out[0]],
+        MID,
+    )
+    pair2, own3, sent = out[0], out[1], out[2:]
+    other3, core2 = swap(own3, 2), swap(pair2, 1)
+    in4.update({r: send(piece, r) for r, piece in zip(slow, sent)})
+    context1 = heads(0, [z3[0]] + [in3[r] for r in range(1, planes)], 4, [pair1, core1], [own3])
+    out = tick(release(z5, fast), [context1[0]] + [in4[r] for r in fast], LARGE)
+    in5 = {r: send(piece, r) for r, piece in zip(fast, out)}
+    out = tick(release(z5, slow), [in4[r] for r in slow] + [out[0]], MID)
+    in5.update({r: send(piece, r) for r, piece in zip(slow, out)})
+    context2 = heads(1, [z4[0]] + [in4[r] for r in range(1, planes)], 0, [pair2, core2], [out[0]])
+    out = tick([(0, [other3, own3], None)] + [(1, [context1[r], context2[r]], None) for r in range(planes)], [in5[r] for r in range(1, planes)], MID)
+    pair3, contexts = out[0], out[1:]
+    core3 = swap(pair3, 1)
+    returned = [contexts[0]] + [send(contexts[r], r) for r in range(1, planes)]
+    context3 = heads(2, [z5[0]] + [in5[r] for r in range(1, planes)], 0, [pair3, core3], [])
+    returned += [context3[0]] + [send(context3[r], r) for r in range(1, planes)]
+    return mix(where, planes, added, returned)
 
 
 def attend(head_queries, head_keys, head_values, group_token_keys, group_tv, usable):
@@ -37,12 +355,8 @@
     )
     key_total = head_keys.shape[0]
     current_key_block = 2048
-    block_keys = head_keys.reshape(
-        key_total // current_key_block, current_key_block, HEADS_DEV, HEAD_DIM
-    )
-    block_values = head_values.reshape(
-        key_total // current_key_block, current_key_block, HEADS_DEV, HEAD_DIM
-    )
+    block_keys = head_keys.reshape(key_total // current_key_block, current_key_block, HEADS_DEV, HEAD_DIM)
+    block_values = head_values.reshape(key_total // current_key_block, current_key_block, HEADS_DEV, HEAD_DIM)
 
     def advance(carry, blocks):
         old_top, old_denominator, old_weighted = carry
@@ -67,7 +381,7 @@
     return context.transpose(1, 0, 2).reshape(query_rows, HEADS_DEV * HEAD_DIM).astype(jnp.bfloat16)
 
 
-def body(queries, keys, values, text_keys, text_values, text_len, plan, deltas):
+def general_body(queries, keys, values, text_keys, text_values, text_len, plan, deltas):
     tok_rows, feat_width = queries.shape
     axis_count = lax.axis_size("seq")
     head_groups = HEADS // HEADS_DEV
@@ -85,12 +399,8 @@
         concat_axis=0,
         tiled=True,
     )
-    head_keys = lax.all_to_all(
-        replicate_slots(keys), "seq", split_axis=1, concat_axis=0, tiled=True
-    )
-    head_values = lax.all_to_all(
-        replicate_slots(values), "seq", split_axis=1, concat_axis=0, tiled=True
-    )
+    head_keys = lax.all_to_all(replicate_slots(keys), "seq", split_axis=1, concat_axis=0, tiled=True)
+    head_values = lax.all_to_all(replicate_slots(values), "seq", split_axis=1, concat_axis=0, tiled=True)
     group_index = lax.axis_index("seq") % head_groups
     group_token_keys = lax.dynamic_slice_in_dim(text_keys, group_index * slot_width, slot_width, 1)
     group_tv = lax.dynamic_slice_in_dim(text_values, group_index * slot_width, slot_width, 1)
@@ -99,17 +409,17 @@
     returned = lax.all_to_all(context, "seq", split_axis=0, concat_axis=1, tiled=True)
     context_rows = returned.reshape(tok_rows, feat_width)
     added = (
-        jnp.einsum(
-            "b,btc->tc", plan.astype(jnp.bfloat16), deltas, preferred_element_type=jnp.float32
-        )
-        * 0.25
+        jnp.einsum("b,btc->tc", plan.astype(jnp.bfloat16), deltas, preferred_element_type=jnp.float32) * 0.25
     )
     return (context_rows.astype(jnp.float32) + added).astype(jnp.bfloat16)
 
 
 def solution(mesh):
+    size = mesh.shape["seq"]
+    planes = size // PLANE
+    fits = planes in (2, 4) and planes * PLANE == size and HEADS % (2 * planes) == 0
     return jax.shard_map(
-        body,
+        plane_body if fits else general_body,
         mesh=mesh,
         in_specs=(
             P(("grp", "seq"), None),

time: 168 us -> 89.3 us (0.53)
  waiting for transfers between devices: 66.3 us -> 25.4 us
  matrix products: 33.5 us -> 0 us
  Pallas kernels: 0 us -> 16.5 us
  other arithmetic: 14.5 us -> 0.07 us
  local copies, waits for them, and re-layouts: 21.4 us -> 7 us
  starting transfers between devices: 31.1 us -> 39.1 us
    all_to_all x4 -> x0, waiting for transfers between devices: 66.3 us -> none  [the longest x1 30.5 us: body(): lax.all_to_all(replicate_slots(keys), 'seq', split_axis=1, concat_axis=0,...]
    ppermute x0 -> x27, starting transfers between devices: none -> 39.1 us  [swap(): return lax.ppermute(array, 'seq', [(i, i ^ distance) for i in range(size)])]
    dot_general x5 -> x0, matrix products: 33.5 us -> none  [the longest x2 13.4 us: compute_scores(): jnp.einsum('qgp,ugp->gqu', reshaped_queries, current_key_block, preferred...]
    all_to_all x4 -> x0, starting transfers between devices: 31.1 us -> none  [the longest x1 9.11 us: body(): lax.all_to_all(replicate_slots(values), 'seq', split_axis=1, concat_axis=...]
    ppermute x0 -> x27, waiting for transfers between devices: none -> 25.4 us  [swap(): return lax.ppermute(array, 'seq', [(i, i ^ distance) for i in range(size)])]
    pallas_call x0 -> x17, Pallas kernels: none -> 16.5 us  [the longest x3 12.7 us: attend_pair(): pl.pallas_call(functools.partial(attend_kernel, n_q, n_kv, q_block * HEAD...]
    reduce_sum x2 -> x0, other arithmetic: 11.6 us -> none  [the longest x1 10.9 us: advance(): jnp.sum(block_exp, axis=-1)]
    all_to_all x4 -> x0, local copies, waits for them, and re-layouts: 5.77 us -> none  [the longest x2 2.59 us: body(): lax.all_to_all(queries.reshape(tok_rows // query_pieces, query_pieces * f...]
  transfers between devices with their start and end apart: 4 -> 27, of which waited for: 4 -> 8; matrix products, arithmetic and copies ran while one was open for 20% -> 0% of each run, Pallas kernels for 0% -> 17%
where the time goes in v3:
time: 89.3 us; the launch traced here: 89 us
  starting transfers between devices  39.1 us (44%)
  waiting for transfers between devices  25.4 us (28%)
  Pallas kernels  16.5 us (18%)
  local copies, waits for them, and re-layouts  7 us (8%)
    ppermute x27, starting transfers between devices, swap(): return lax.ppermute(array, 'seq', [(i, i ^ distance) for i in range(size)])  39.1 us
    ppermute x27, waiting for transfers between devices, swap(): return lax.ppermute(array, 'seq', [(i, i ^ distance) for i in range(size)])  25.4 us
    pallas_call x3, Pallas kernels, attend_pair(): pl.pallas_call(functools.partial(attend_kernel, n_q, n_kv, q_block * HEAD...  12.7 us
    unnamed x18, local copies, waits for them, and re-layouts  7 us
    pallas_call x1, Pallas kernels, sum_deltas(): pl.pallas_call(deltas_kernel, grid=(4,), in_specs=[pl.BlockSpec(memory_sp...  1.88 us
  transfers between devices with their start and end apart: 27, of which 8 were waited for; matrix products, arithmetic and copies ran while one was open for 0% of the time, Pallas kernels for 17%

profile of v3, /device:TPU:0, one launch (start us, length us, event | category | flops | bytes accessed | tf_op | source)
XLA Modules:
  0.0 89.0 jit_solution(1688065102773423190)
XLA Ops:
  2.4 5.1 %collective-permute-start = (bf16[128,512]{1,0:T(8,128)(2,1)S(1)}, bf16[128,512]{1,0:T(8,128)(2,1)S(1)}, u32[]{:S(2)}, u32[]{:S(2)}) collective-permute-start(bf16[128,512]{1,0:T(8,128)(2,1)S(1)} %get-tuple-element.60.refs_6_), channel_id=1, source_target_pairs={{0,12},{1,13},{2,14},{3,15},{4,8},{5,9},{6,10},{7,11},{8,4},{9,5},... | collective-permute-start | bytes 393224 | tf_op jit(solution)/shard_map/ppermute | solution.py:267
  9.6 1.5 %copy-done.5 = bf16[256,3072]{1,0:T(8,128)(2,1)S(1)} copy-done((bf16[256,3072]{1,0:T(8,128)(2,1)S(1)}, bf16[256,3072]{1,0:T(8,128)(2,1)}, u32[]{:S(2)}) %copy-start.5) | copy-done | bytes 1572888
  11.1 1.5 %copy-done.6 = bf16[256,3072]{1,0:T(8,128)(2,1)S(1)} copy-done((bf16[256,3072]{1,0:T(8,128)(2,1)S(1)}, bf16[256,3072]{1,0:T(8,128)(2,1)}, u32[]{:S(2)}) %copy-start.6) | copy-done | bytes 1572888
  13.3 1.9 %deltas.2.refs_1_.added = f32[128,3072]{1,0:T(8,128)S(1)} custom-call(s32[6]{0:T(128)S(1)} %copy-done.8, bf16[6,128,3072]{2,1,0:T(8,128)(2,1)S(1)} %copy-done, bf16[256,768]{1,0:T(8,128)(2,1)S(1)} %get-tuple-element.62.refs_0_.refs_6_), custom_call_target="tpu_custom_call" | custom-call | flops 1 | bytes 1 | tf_op jit(solution)/shard_map/deltas/pallas_call | solution.py:215
  15.2 3.8 %collective-permute-start.1 = (bf16[128,512]{1,0:T(8,128)(2,1)S(1)}, bf16[128,512]{1,0:T(8,128)(2,1)S(1)}, u32[]{:S(2)}, u32[]{:S(2)}) collective-permute-start(bf16[128,512]{1,0:T(8,128)(2,1)S(1)} %tick.9.refs_0_), channel_id=1, source_target_pairs={{0,12},{1,13},{2,14},{3,15},{4,8},{5,9},{6,10},{7,11},{8,4},{9,5},... | collective-permute-start | bytes 393224 | tf_op jit(solution)/shard_map/ppermute | solution.py:267
  20.6 1.6 %collective-permute-start.4 = (bf16[512,512]{1,0:T(8,128)(2,1)S(1)}, bf16[512,512]{1,0:T(8,128)(2,1)S(1)}, u32[]{:S(2)}, u32[]{:S(2)}) collective-permute-start(bf16[512,512]{1,0:T(8,128)(2,1)S(1)} %get-tuple-element.66.refs_1_.refs_2_), channel_id=1, source_target_pairs={{0,2},{1,3},{2,0},{3,1},{4,6},{5,7},{6,4},{7,5},{8,10},{9,11},{10,... | collective-permute-start | bytes 1572872 | tf_op jit(solution)/shard_map/ppermute | solution.py:267
  22.2 1.7 %collective-permute-start.6 = (bf16[128,512]{1,0:T(8,128)(2,1)S(1)}, bf16[128,512]{1,0:T(8,128)(2,1)S(1)}, u32[]{:S(2)}, u32[]{:S(2)}) collective-permute-start(bf16[128,512]{1,0:T(8,128)(2,1)S(1)} %get-tuple-element.70), channel_id=1, source_target_pairs={{0,8},{1,9},{2,10},{3,11},{4,12},{5,13},{6,14},{7,15},{8,0},{9,1},... | collective-permute-start | bytes 393224 | tf_op jit(solution)/shard_map/ppermute | solution.py:267
  24.0 3.2 %collective-permute-start.9 = (bf16[128,768]{1,0:T(8,128)(2,1)S(1)}, bf16[128,768]{1,0:T(8,128)(2,1)S(1)}, u32[]{:S(2)}, u32[]{:S(2)}) collective-permute-start(bf16[128,768]{1,0:T(8,128)(2,1)S(1)} %tick.11.refs_0_), channel_id=1, source_target_pairs={{0,12},{1,13},{2,14},{3,15},{4,8},{5,9},{6,10},{7,11},{8,4},{9,5},... | collective-permute-start | bytes 589832 | tf_op jit(solution)/shard_map/ppermute | solution.py:267
  27.2 2.8 %collective-permute-done.5.refs_4_ = bf16[128,512]{1,0:T(8,128)(2,1)S(1)} collective-permute-done((bf16[128,512]{1,0:T(8,128)(2,1)S(1)}, bf16[128,512]{1,0:T(8,128)(2,1)S(1)}, u32[]{:S(2)}, u32[]{:S(2)}) %collective-permute-start.5) | collective-permute-done | bytes 131104 | tf_op jit(solution)/shard_map/ppermute | solution.py:267
  30.0 5.3 %collective-permute-done.6.refs_5_ = bf16[128,512]{1,0:T(8,128)(2,1)S(1)} collective-permute-done((bf16[128,512]{1,0:T(8,128)(2,1)S(1)}, bf16[128,512]{1,0:T(8,128)(2,1)S(1)}, u32[]{:S(2)}, u32[]{:S(2)}) %collective-permute-start.6) | collective-permute-done | bytes 131104 | tf_op jit(solution)/shard_map/ppermute | solution.py:267
  36.4 3.4 %collective-permute-start.8 = (bf16[128,768]{1,0:T(8,128)(2,1)S(1)}, bf16[128,768]{1,0:T(8,128)(2,1)S(1)}, u32[]{:S(2)}, u32[]{:S(2)}) collective-permute-start(bf16[128,768]{1,0:T(8,128)(2,1)S(1)} %get-tuple-element.74), channel_id=1, source_target_pairs={{0,8},{1,9},{2,10},{3,11},{4,12},{5,13},{6,14},{7,15},{8,0},{9,1},... | collective-permute-start | bytes 589832 | tf_op jit(solution)/shard_map/ppermute | solution.py:267
  40.8 4.0 %collective-permute-done.7.refs_0_.refs_6_.refs_1_ = bf16[128,768]{1,0:T(8,128)(2,1)S(1)} collective-permute-done((bf16[128,768]{1,0:T(8,128)(2,1)S(1)}, bf16[128,768]{1,0:T(8,128)(2,1)S(1)}, u32[]{:S(2)}, u32[]{:S(2)}) %collective-permute-start.7) | collective-permute-done | bytes 196640 | tf_op jit(solution)/shard_map/ppermute | solution.py:267
  44.9 4.3 %collective-permute-done.8.refs_1_.refs_7_.refs_2_ = bf16[128,768]{1,0:T(8,128)(2,1)S(1)} collective-permute-done((bf16[128,768]{1,0:T(8,128)(2,1)S(1)}, bf16[128,768]{1,0:T(8,128)(2,1)S(1)}, u32[]{:S(2)}, u32[]{:S(2)}) %collective-permute-start.8) | collective-permute-done | bytes 196640 | tf_op jit(solution)/shard_map/ppermute | solution.py:267
  49.4 2.7 %collective-permute-start.12 = (bf16[128,256]{1,0:T(8,128)(2,1)S(1)}, bf16[128,256]{1,0:T(8,128)(2,1)S(1)}, u32[]{:S(2)}, u32[]{:S(2)}) collective-permute-start(bf16[128,256]{1,0:T(8,128)(2,1)S(1)} %get-tuple-element.81), channel_id=1, source_target_pairs={{0,8},{1,9},{2,10},{3,11},{4,12},{5,13},{6,14},{7,15},{8,0},{9,1},... | collective-permute-start | bytes 196616 | tf_op jit(solution)/shard_map/ppermute | solution.py:267
  53.5 4.2 %attend.3 = (bf16[128,256]{1,0:T(8,128)(2,1)S(1)}, bf16[128,256]{1,0:T(8,128)(2,1)S(1)}, bf16[128,256]{1,0:T(8,128)(2,1)S(1)}, bf16[128,256]{1,0:T(8,128)(2,1)S(1)}) custom-call(s32[2]{0:T(128)S(1)} %pad_add_fusion.scalars, bf16[128,768]{1,0:T(8,128)(2,1)S(1)} %get-tuple-element.77.refs_5_.refs_0_, ...), custom_call_target="tpu_custom_call" | custom-call | flops 1 | bytes 1 | tf_op jit(solution)/shard_map/attend/pallas_call | solution.py:167
  57.9 1.9 %collective-permute-start.16 = (bf16[128,256]{1,0:T(8,128)(2,1)S(1)}, bf16[128,256]{1,0:T(8,128)(2,1)S(1)}, u32[]{:S(2)}, u32[]{:S(2)}) collective-permute-start(bf16[128,256]{1,0:T(8,128)(2,1)S(1)} %get-tuple-element.90), channel_id=1, source_target_pairs={{0,8},{1,9},{2,10},{3,11},{4,12},{5,13},{6,14},{7,15},{8,0},{9,1},... | collective-permute-start | bytes 196616 | tf_op jit(solution)/shard_map/ppermute | solution.py:267
  59.8 2.4 %collective-permute-start.17 = (bf16[128,256]{1,0:T(8,128)(2,1)S(1)}, bf16[128,256]{1,0:T(8,128)(2,1)S(1)}, u32[]{:S(2)}, u32[]{:S(2)}) collective-permute-start(bf16[128,256]{1,0:T(8,128)(2,1)S(1)} %tick.15.refs_2_), channel_id=1, source_target_pairs={{0,12},{1,13},{2,14},{3,15},{4,8},{5,9},{6,10},{7,11},{8,4},{9,5},... | collective-permute-start | bytes 196616 | tf_op jit(solution)/shard_map/ppermute | solution.py:267
  62.2 4.2 %attend.4 = (bf16[128,256]{1,0:T(8,128)(2,1)S(1)}, bf16[128,256]{1,0:T(8,128)(2,1)S(1)}, bf16[128,256]{1,0:T(8,128)(2,1)S(1)}, bf16[128,256]{1,0:T(8,128)(2,1)S(1)}) custom-call(s32[2]{0:T(128)S(1)} %pad_add_fusion.scalars, bf16[128,256]{1,0:T(8,128)(2,1)S(1)} %get-tuple-element.91.refs_0_, bf16[128,256]{1,0:T(8,128)(2,1)S(1)} %collective-permute-done.11.refs_0_.refs_1_, ...), custom_call_target="tpu_custom_call" | custom-call | flops 1 | bytes 1 | tf_op jit(solution)/shard_map/attend/pallas_call | solution.py:167
  69.2 2.0 %collective-permute-start.22 = (bf16[128,512]{1,0:T(8,128)(2,1)S(1)}, bf16[128,512]{1,0:T(8,128)(2,1)S(1)}, u32[]{:S(2)}, u32[]{:S(2)}) collective-permute-start(bf16[128,512]{1,0:T(8,128)(2,1)S(1)} %get-tuple-element.103), channel_id=1, source_target_pairs={{0,12},{1,13},{2,14},{3,15},{4,8},{5,9},{6,10},{7,11},{8,4},{9,5},... | collective-permute-start | bytes 393224 | tf_op jit(solution)/shard_map/ppermute | solution.py:267
  71.2 4.3 %attend.5 = (bf16[128,256]{1,0:T(8,128)(2,1)S(1)}, bf16[128,256]{1,0:T(8,128)(2,1)S(1)}, bf16[128,256]{1,0:T(8,128)(2,1)S(1)}, bf16[128,256]{1,0:T(8,128)(2,1)S(1)}) custom-call(s32[2]{0:T(128)S(1)} %pad_add_fusion.scalars, bf16[128,256]{1,0:T(8,128)(2,1)S(1)} %get-tuple-element.61.refs_0_, bf16[128,256]{1,0:T(8,128)(2,1)S(1)} %collective-permute-done.15.refs_0_.refs_1_, ...), custom_call_target="tpu_custom_call" | custom-call | flops 1 | bytes 1 | tf_op jit(solution)/shard_map/attend/pallas_call | solution.py:167
  75.9 2.0 %collective-permute-start.25 = (bf16[128,256]{1,0:T(8,128)(2,1)S(1)}, bf16[128,256]{1,0:T(8,128)(2,1)S(1)}, u32[]{:S(2)}, u32[]{:S(2)}) collective-permute-start(bf16[128,256]{1,0:T(8,128)(2,1)S(1)} %get-tuple-element.107), channel_id=1, source_target_pairs={{0,8},{1,9},{2,10},{3,11},{4,12},{5,13},{6,14},{7,15},{8,0},{9,1},... | collective-permute-start | bytes 196616 | tf_op jit(solution)/shard_map/ppermute | solution.py:267
  77.9 2.0 %collective-permute-start.26 = (bf16[128,256]{1,0:T(8,128)(2,1)S(1)}, bf16[128,256]{1,0:T(8,128)(2,1)S(1)}, u32[]{:S(2)}, u32[]{:S(2)}) collective-permute-start(bf16[128,256]{1,0:T(8,128)(2,1)S(1)} %get-tuple-element.108), channel_id=1, source_target_pairs={{0,12},{1,13},{2,14},{3,15},{4,8},{5,9},{6,10},{7,11},{8,4},{9,5},... | collective-permute-start | bytes 196616 | tf_op jit(solution)/shard_map/ppermute | solution.py:267
  79.9 3.2 %collective-permute-done.21.refs_2_ = bf16[128,512]{1,0:T(8,128)(2,1)S(1)} collective-permute-done((bf16[128,512]{1,0:T(8,128)(2,1)S(1)}, bf16[128,512]{1,0:T(8,128)(2,1)S(1)}, u32[]{:S(2)}, u32[]{:S(2)}) %collective-permute-start.21) | collective-permute-done | bytes 131104 | tf_op jit(solution)/shard_map/ppermute | solution.py:267
  83.1 4.8 %collective-permute-done.25.refs_6_ = bf16[128,256]{1,0:T(8,128)(2,1)S(1)} collective-permute-done((bf16[128,256]{1,0:T(8,128)(2,1)S(1)}, bf16[128,256]{1,0:T(8,128)(2,1)S(1)}, u32[]{:S(2)}, u32[]{:S(2)}) %collective-permute-start.25) | collective-permute-done | bytes 65568 | tf_op jit(solution)/shard_map/ppermute | solution.py:267
  (66 shorter events, 14.3 us)
Async XLA Ops:
  2.4 12.7 %collective-permute-start = (bf16[128,512]{1,0:T(8,128)(2,1)S(1)}, bf16[128,512]{1,0:T(8,128)(2,1)S(1)}, u32[]{:S(2)}, u32[]{:S(2)}) collective-permute-start(bf16[128,512]{1,0:T(8,128)(2,1)S(1)} %get-tuple-element.60.refs_6_), channel_id=1, source_target_pairs={{0,12},{1,13},{2,14},{3,15},{4,8},{5,9},{6,10},{7,11},{8,4},{9,5},... | collective-permute-start | bytes 393224 | tf_op jit(solution)/shard_map/ppermute | solution.py:267
  7.5 12.1 %collective-permute-start.2 = (bf16[128,512]{1,0:T(8,128)(2,1)S(1)}, bf16[128,512]{1,0:T(8,128)(2,1)S(1)}, u32[]{:S(2)}, u32[]{:S(2)}) collective-permute-start(bf16[128,512]{1,0:T(8,128)(2,1)S(1)} %get-tuple-element.58.refs_4_), channel_id=1, source_target_pairs={{0,4},{1,5},{2,6},{3,7},{4,0},{5,1},{6,2},{7,3},{8,12},{9,13},{10,... | collective-permute-start | bytes 393224 | tf_op jit(solution)/shard_map/ppermute | solution.py:267
  7.5 13.1 %collective-permute-start.3 = (bf16[128,512]{1,0:T(8,128)(2,1)S(1)}, bf16[128,512]{1,0:T(8,128)(2,1)S(1)}, u32[]{:S(2)}, u32[]{:S(2)}) collective-permute-start(bf16[128,512]{1,0:T(8,128)(2,1)S(1)} %get-tuple-element.59.refs_5_), channel_id=1, source_target_pairs={{0,8},{1,9},{2,10},{3,11},{4,12},{5,13},{6,14},{7,15},{8,0},{9,1},... | collective-permute-start | bytes 393224 | tf_op jit(solution)/shard_map/ppermute | solution.py:267
  15.2 8.8 %collective-permute-start.1 = (bf16[128,512]{1,0:T(8,128)(2,1)S(1)}, bf16[128,512]{1,0:T(8,128)(2,1)S(1)}, u32[]{:S(2)}, u32[]{:S(2)}) collective-permute-start(bf16[128,512]{1,0:T(8,128)(2,1)S(1)} %tick.9.refs_0_), channel_id=1, source_target_pairs={{0,12},{1,13},{2,14},{3,15},{4,8},{5,9},{6,10},{7,11},{8,4},{9,5},... | collective-permute-start | bytes 393224 | tf_op jit(solution)/shard_map/ppermute | solution.py:267
  20.6 14.6 %collective-permute-start.4 = (bf16[512,512]{1,0:T(8,128)(2,1)S(1)}, bf16[512,512]{1,0:T(8,128)(2,1)S(1)}, u32[]{:S(2)}, u32[]{:S(2)}) collective-permute-start(bf16[512,512]{1,0:T(8,128)(2,1)S(1)} %get-tuple-element.66.refs_1_.refs_2_), channel_id=1, source_target_pairs={{0,2},{1,3},{2,0},{3,1},{4,6},{5,7},{6,4},{7,5},{8,10},{9,11},{10,... | collective-permute-start | bytes 1572872 | tf_op jit(solution)/shard_map/ppermute | solution.py:267
  22.2 7.8 %collective-permute-start.5 = (bf16[128,512]{1,0:T(8,128)(2,1)S(1)}, bf16[128,512]{1,0:T(8,128)(2,1)S(1)}, u32[]{:S(2)}, u32[]{:S(2)}) collective-permute-start(bf16[128,512]{1,0:T(8,128)(2,1)S(1)} %get-tuple-element.69), channel_id=1, source_target_pairs={{0,4},{1,5},{2,6},{3,7},{4,0},{5,1},{6,2},{7,3},{8,12},{9,13},{10,... | collective-permute-start | bytes 393224 | tf_op jit(solution)/shard_map/ppermute | solution.py:267
  22.2 13.0 %collective-permute-start.6 = (bf16[128,512]{1,0:T(8,128)(2,1)S(1)}, bf16[128,512]{1,0:T(8,128)(2,1)S(1)}, u32[]{:S(2)}, u32[]{:S(2)}) collective-permute-start(bf16[128,512]{1,0:T(8,128)(2,1)S(1)} %get-tuple-element.70), channel_id=1, source_target_pairs={{0,8},{1,9},{2,10},{3,11},{4,12},{5,13},{6,14},{7,15},{8,0},{9,1},... | collective-permute-start | bytes 393224 | tf_op jit(solution)/shard_map/ppermute | solution.py:267
  24.0 15.8 %collective-permute-start.9 = (bf16[128,768]{1,0:T(8,128)(2,1)S(1)}, bf16[128,768]{1,0:T(8,128)(2,1)S(1)}, u32[]{:S(2)}, u32[]{:S(2)}) collective-permute-start(bf16[128,768]{1,0:T(8,128)(2,1)S(1)} %tick.11.refs_0_), channel_id=1, source_target_pairs={{0,12},{1,13},{2,14},{3,15},{4,8},{5,9},{6,10},{7,11},{8,4},{9,5},... | collective-permute-start | bytes 589832 | tf_op jit(solution)/shard_map/ppermute | solution.py:267
  35.4 13.8 %collective-permute-start.10 = (bf16[512,512]{1,0:T(8,128)(2,1)S(1)}, bf16[512,512]{1,0:T(8,128)(2,1)S(1)}, u32[]{:S(2)}, u32[]{:S(2)}) collective-permute-start(bf16[512,512]{1,0:T(8,128)(2,1)S(1)} %get-tuple-element.75.refs_0_.refs_4_), channel_id=1, source_target_pairs={{0,2},{1,3},{2,0},{3,1},{4,6},{5,7},{6,4},{7,5},{8,10},{9,11},{10,... | collective-permute-start | bytes 1572872 | tf_op jit(solution)/shard_map/ppermute | solution.py:267
  36.4 8.5 %collective-permute-start.7 = (bf16[128,768]{1,0:T(8,128)(2,1)S(1)}, bf16[128,768]{1,0:T(8,128)(2,1)S(1)}, u32[]{:S(2)}, u32[]{:S(2)}) collective-permute-start(bf16[128,768]{1,0:T(8,128)(2,1)S(1)} %get-tuple-element.73), channel_id=1, source_target_pairs={{0,4},{1,5},{2,6},{3,7},{4,0},{5,1},{6,2},{7,3},{8,12},{9,13},{10,... | collective-permute-start | bytes 589832 | tf_op jit(solution)/shard_map/ppermute | solution.py:267
  36.4 12.8 %collective-permute-start.8 = (bf16[128,768]{1,0:T(8,128)(2,1)S(1)}, bf16[128,768]{1,0:T(8,128)(2,1)S(1)}, u32[]{:S(2)}, u32[]{:S(2)}) collective-permute-start(bf16[128,768]{1,0:T(8,128)(2,1)S(1)} %get-tuple-element.74), channel_id=1, source_target_pairs={{0,8},{1,9},{2,10},{3,11},{4,12},{5,13},{6,14},{7,15},{8,0},{9,1},... | collective-permute-start | bytes 589832 | tf_op jit(solution)/shard_map/ppermute | solution.py:267
  39.8 12.3 %collective-permute-start.13 = (bf16[1024,512]{1,0:T(8,128)(2,1)S(1)}, bf16[1024,512]{1,0:T(8,128)(2,1)S(1)}, u32[]{:S(2)}, u32[]{:S(2)}) collective-permute-start(bf16[1024,512]{1,0:T(8,128)(2,1)S(1)} %get-tuple-element.82.refs_4_), channel_id=1, source_target_pairs={{0,1},{1,0},{2,3},{3,2},{4,5},{5,4},{6,7},{7,6},{8,9},{9,8},{10,11... | collective-permute-start | bytes 3145736 | tf_op jit(solution)/shard_map/ppermute | solution.py:267
  39.8 17.9 %collective-permute-start.14 = (bf16[128,256]{1,0:T(8,128)(2,1)S(1)}, bf16[128,256]{1,0:T(8,128)(2,1)S(1)}, u32[]{:S(2)}, u32[]{:S(2)}) collective-permute-start(bf16[128,256]{1,0:T(8,128)(2,1)S(1)} %tick.13.refs_2_), channel_id=1, source_target_pairs={{0,12},{1,13},{2,14},{3,15},{4,8},{5,9},{6,10},{7,11},{8,4},{9,5},... | collective-permute-start | bytes 196616 | tf_op jit(solution)/shard_map/ppermute | solution.py:267
  49.3 8.4 %collective-permute-start.11 = (bf16[128,256]{1,0:T(8,128)(2,1)S(1)}, bf16[128,256]{1,0:T(8,128)(2,1)S(1)}, u32[]{:S(2)}, u32[]{:S(2)}) collective-permute-start(bf16[128,256]{1,0:T(8,128)(2,1)S(1)} %get-tuple-element.80), channel_id=1, source_target_pairs={{0,4},{1,5},{2,6},{3,7},{4,0},{5,1},{6,2},{7,3},{8,12},{9,13},{10,... | collective-permute-start | bytes 196616 | tf_op jit(solution)/shard_map/ppermute | solution.py:267
  49.4 8.4 %collective-permute-start.12 = (bf16[128,256]{1,0:T(8,128)(2,1)S(1)}, bf16[128,256]{1,0:T(8,128)(2,1)S(1)}, u32[]{:S(2)}, u32[]{:S(2)}) collective-permute-start(bf16[128,256]{1,0:T(8,128)(2,1)S(1)} %get-tuple-element.81), channel_id=1, source_target_pairs={{0,8},{1,9},{2,10},{3,11},{4,12},{5,13},{6,14},{7,15},{8,0},{9,1},... | collective-permute-start | bytes 196616 | tf_op jit(solution)/shard_map/ppermute | solution.py:267
  52.1 10.1 %collective-permute-start.19 = (bf16[1024,512]{1,0:T(8,128)(2,1)S(1)}, bf16[1024,512]{1,0:T(8,128)(2,1)S(1)}, u32[]{:S(2)}, u32[]{:S(2)}) collective-permute-start(bf16[1024,512]{1,0:T(8,128)(2,1)S(1)} %get-tuple-element.92.refs_4_), channel_id=1, source_target_pairs={{0,1},{1,0},{2,3},{3,2},{4,5},{5,4},{6,7},{7,6},{8,9},{9,8},{10,11... | collective-permute-start | bytes 3145736 | tf_op jit(solution)/shard_map/ppermute | solution.py:267
  52.1 14.4 %collective-permute-start.18 = (bf16[512,512]{1,0:T(8,128)(2,1)S(1)}, bf16[512,512]{1,0:T(8,128)(2,1)S(1)}, u32[]{:S(2)}, u32[]{:S(2)}) collective-permute-start(bf16[512,512]{1,0:T(8,128)(2,1)S(1)} %get-tuple-element.84.refs_8_.refs_4_), channel_id=1, source_target_pairs={{0,2},{1,3},{2,0},{3,1},{4,6},{5,7},{6,4},{7,5},{8,10},{9,11},{10,... | collective-permute-start | bytes 1572872 | tf_op jit(solution)/shard_map/ppermute | solution.py:267
  57.8 8.7 %collective-permute-start.15 = (bf16[128,256]{1,0:T(8,128)(2,1)S(1)}, bf16[128,256]{1,0:T(8,128)(2,1)S(1)}, u32[]{:S(2)}, u32[]{:S(2)}) collective-permute-start(bf16[128,256]{1,0:T(8,128)(2,1)S(1)} %get-tuple-element.89.refs_8_), channel_id=1, source_target_pairs={{0,4},{1,5},{2,6},{3,7},{4,0},{5,1},{6,2},{7,3},{8,12},{9,13},{10,... | collective-permute-start | bytes 196616 | tf_op jit(solution)/shard_map/ppermute | solution.py:267
  57.9 8.6 %collective-permute-start.16 = (bf16[128,256]{1,0:T(8,128)(2,1)S(1)}, bf16[128,256]{1,0:T(8,128)(2,1)S(1)}, u32[]{:S(2)}, u32[]{:S(2)}) collective-permute-start(bf16[128,256]{1,0:T(8,128)(2,1)S(1)} %get-tuple-element.90), channel_id=1, source_target_pairs={{0,8},{1,9},{2,10},{3,11},{4,12},{5,13},{6,14},{7,15},{8,0},{9,1},... | collective-permute-start | bytes 196616 | tf_op jit(solution)/shard_map/ppermute | solution.py:267
  66.7 11.2 %collective-permute-start.20 = (bf16[128,512]{1,0:T(8,128)(2,1)S(1)}, bf16[128,512]{1,0:T(8,128)(2,1)S(1)}, u32[]{:S(2)}, u32[]{:S(2)}) collective-permute-start(bf16[128,512]{1,0:T(8,128)(2,1)S(1)} %get-tuple-element.101), channel_id=1, source_target_pairs={{0,4},{1,5},{2,6},{3,7},{4,0},{5,1},{6,2},{7,3},{8,12},{9,13},{10,... | collective-permute-start | bytes 393224 | tf_op jit(solution)/shard_map/ppermute | solution.py:267
  68.1 15.0 %collective-permute-start.21 = (bf16[128,512]{1,0:T(8,128)(2,1)S(1)}, bf16[128,512]{1,0:T(8,128)(2,1)S(1)}, u32[]{:S(2)}, u32[]{:S(2)}) collective-permute-start(bf16[128,512]{1,0:T(8,128)(2,1)S(1)} %get-tuple-element.102), channel_id=1, source_target_pairs={{0,8},{1,9},{2,10},{3,11},{4,12},{5,13},{6,14},{7,15},{8,0},{9,1},... | collective-permute-start | bytes 393224 | tf_op jit(solution)/shard_map/ppermute | solution.py:267
  69.2 13.9 %collective-permute-start.22 = (bf16[128,512]{1,0:T(8,128)(2,1)S(1)}, bf16[128,512]{1,0:T(8,128)(2,1)S(1)}, u32[]{:S(2)}, u32[]{:S(2)}) collective-permute-start(bf16[128,512]{1,0:T(8,128)(2,1)S(1)} %get-tuple-element.103), channel_id=1, source_target_pairs={{0,12},{1,13},{2,14},{3,15},{4,8},{5,9},{6,10},{7,11},{8,4},{9,5},... | collective-permute-start | bytes 393224 | tf_op jit(solution)/shard_map/ppermute | solution.py:267
  75.9 12.0 %collective-permute-start.25 = (bf16[128,256]{1,0:T(8,128)(2,1)S(1)}, bf16[128,256]{1,0:T(8,128)(2,1)S(1)}, u32[]{:S(2)}, u32[]{:S(2)}) collective-permute-start(bf16[128,256]{1,0:T(8,128)(2,1)S(1)} %get-tuple-element.107), channel_id=1, source_target_pairs={{0,8},{1,9},{2,10},{3,11},{4,12},{5,13},{6,14},{7,15},{8,0},{9,1},... | collective-permute-start | bytes 196616 | tf_op jit(solution)/shard_map/ppermute | solution.py:267
  77.9 10.0 %collective-permute-start.26 = (bf16[128,256]{1,0:T(8,128)(2,1)S(1)}, bf16[128,256]{1,0:T(8,128)(2,1)S(1)}, u32[]{:S(2)}, u32[]{:S(2)}) collective-permute-start(bf16[128,256]{1,0:T(8,128)(2,1)S(1)} %get-tuple-element.108), channel_id=1, source_target_pairs={{0,12},{1,13},{2,14},{3,15},{4,8},{5,9},{6,10},{7,11},{8,4},{9,5},... | collective-permute-start | bytes 196616 | tf_op jit(solution)/shard_map/ppermute | solution.py:267
  (12 other events, 41.3 us)

commit v4 on v3

--- a/solution.py
+++ b/solution.py
@@ -17,44 +17,38 @@
 
 
 SMALL = pl.CostEstimate(flops=1, bytes_accessed=1, transcendentals=0)
-LARGE = pl.CostEstimate(flops=20000000000, bytes_accessed=1, transcendentals=0)
-MID = pl.CostEstimate(flops=1000000000, bytes_accessed=1, transcendentals=0)
-
-
-def first_pack_kernel(spans, planes, where, *refs):
-    sources, outs = refs[: len(spans)], refs[len(spans) : len(spans) + planes]
-    slabs, sems = refs[-2:]
-    copies = [
-        pltpu.make_async_copy(source.at[:, pl.ds(phase * planes * PAIR, planes * PAIR)], slabs.at[slot], sems.at[slot])
-        for slot, (source, phase) in enumerate(zip(sources, spans))
-    ]
-    for copy in copies:
-        copy.start()
-    for copy in copies:
-        copy.wait()
-    for relative, out in enumerate(outs):
-        plane = jnp.bitwise_xor(where[0], relative)
-        columns = pl.ds(pl.multiple_of(plane * PAIR, PAIR), PAIR)
-        for slot in range(len(spans)):
-            out[:, slot * PAIR : (slot + 1) * PAIR] = slabs[slot, :, columns]
-
-
-def first_pack(where, phase, planes, *sources):
-    rows = sources[0].shape[0]
-    vmem = pl.BlockSpec(memory_space=pltpu.VMEM)
-    return pl.pallas_call(
-        functools.partial(first_pack_kernel, [phase] * len(sources), planes),
-        out_shape=[jax.ShapeDtypeStruct((rows, len(sources) * PAIR), sources[0].dtype)] * planes,
-        in_specs=[pl.BlockSpec(memory_space=pltpu.SMEM)] + [pl.BlockSpec(memory_space=pltpu.HBM)] * len(sources),
-        out_specs=[vmem] * planes,
-        scratch_shapes=[
-            pltpu.VMEM((len(sources), rows, planes * PAIR), sources[0].dtype),
-            pltpu.SemaphoreType.DMA((len(sources),)),
-        ],
-        compiler_params=pltpu.CompilerParams(vmem_limit_bytes=4 * 2**20),
+MID = pl.CostEstimate(flops=10**9, bytes_accessed=1, transcendentals=0)
+BIG = pl.CostEstimate(flops=2 * 10**10, bytes_accessed=1, transcendentals=0)
+
+
+def first_pack_kernel(planes, where, keys, values, *refs):
+    outs, own = refs[:planes], refs[planes]
+    slab = planes * PAIR
+    for slot, source in enumerate((keys, values)):
+        here = slice(slot * PAIR, (slot + 1) * PAIR)
+        for relative, out in enumerate(outs):
+            plane = jnp.bitwise_xor(where[0], relative)
+            out[:, here] = source[:, pl.ds(pl.multiple_of(plane * PAIR, PAIR), PAIR)]
+        for phase in range(keys.shape[1] // slab):
+            start = pl.multiple_of(phase * slab + where[0] * PAIR, PAIR)
+            at = (2 * phase + slot) * PAIR
+            own[:, at : at + PAIR] = source[:, pl.ds(start, PAIR)]
+
+
+def first_pack(where, planes, keys, values):
+    rows, width = keys.shape
+    vmem = pl.BlockSpec(memory_space=pltpu.VMEM)
+    shapes = [jax.ShapeDtypeStruct((rows, 2 * PAIR), keys.dtype)] * planes
+    shapes.append(jax.ShapeDtypeStruct((rows, 2 * width // planes), keys.dtype))
+    return pl.pallas_call(
+        functools.partial(first_pack_kernel, planes),
+        out_shape=shapes,
+        in_specs=[pl.BlockSpec(memory_space=pltpu.SMEM), vmem, vmem],
+        out_specs=[vmem] * len(shapes),
+        compiler_params=pltpu.CompilerParams(vmem_limit_bytes=6 * 2**20),
         cost_estimate=SMALL,
         name="first_pack",
-    )(where, *sources)
+    )(where, keys, values)
 
 
 def pack_kernel(groups, planes, n_out, where, *refs):
@@ -126,24 +120,30 @@
     )(*earlier, *[a for _, arrays, _ in jobs for a in arrays])
 
 
-def attend_kernel(n_q, n_kv, q_column, text_column, scalars, *refs):
-    queries, kvs = refs[:n_q], refs[n_q : n_q + n_kv]
-    text_keys, text_values = refs[n_q + n_kv : n_q + n_kv + 2]
-    outs = refs[len(refs) - n_q :]
+def attend_kernel(n_q, q_column, groups, scalars, *refs):
+    queries, outs = refs[:n_q], refs[len(refs) - n_q :]
+    arrays = refs[n_q:]
     rows = outs[0].shape[0]
     contract_last = (((1,), (1,)), ((), ()))
+
+    def columns(group, head, which):
+        parts = []
+        for index, key_column, value_column in group:
+            start = (value_column if which else key_column) + head * HEAD_DIM
+            parts.append(arrays[index][:, start : start + HEAD_DIM])
+        return parts[0] if len(parts) == 1 else jnp.concatenate(parts, axis=0)
+
     for head in range(2):
         here = slice(head * HEAD_DIM, (head + 1) * HEAD_DIM)
-        over = slice(PAIR + head * HEAD_DIM, PAIR + (head + 1) * HEAD_DIM)
-        text = slice(text_column + head * HEAD_DIM, text_column + (head + 1) * HEAD_DIM)
         q_here = slice(q_column + head * HEAD_DIM, q_column + (head + 1) * HEAD_DIM)
         q = jnp.concatenate([piece[:, q_here] for piece in queries], axis=0)
-        blocks = [(kv[:, here], kv[:, over]) for kv in kvs] + [(text_keys[:, text], text_values[:, text])]
         top = None
-        for index, (keys, values) in enumerate(blocks):
+        for number, group in enumerate(groups):
+            keys, values = columns(group, head, False), columns(group, head, True)
             scores = lax.dot_general(q, keys, contract_last, preferred_element_type=jnp.float32)
-            if index == n_kv:
-                usable = lax.broadcasted_iota(jnp.int32, scores.shape, 1) < scalars[1]
+            if number == len(groups) - 1:
+                text_at = keys.shape[0] - arrays[group[-1][0]].shape[0]
+                usable = lax.broadcasted_iota(jnp.int32, scores.shape, 1) < scalars[1] + text_at
                 scores = jnp.where(usable, scores, -jnp.inf)
             block_top = jnp.max(scores, axis=1, keepdims=True)
             new_top = block_top if top is None else jnp.maximum(top, block_top)
@@ -161,40 +161,46 @@
             out[:, here] = context[index * rows : (index + 1) * rows]
 
 
-def attend_pair(scalars, queries, q_block, kvs, text_keys, text_values, text_block, earlier):
-    n_q, n_kv = len(queries), len(kvs)
-    vmem = pl.BlockSpec(memory_space=pltpu.VMEM)
-    return pl.pallas_call(
-        functools.partial(attend_kernel, n_q, n_kv, q_block * HEAD_DIM, text_block * HEAD_DIM),
+def attend_pair(scalars, queries, q_block, groups, earlier):
+    n_q = len(queries)
+    arrays, numbered = [], []
+    for group in groups:
+        numbered.append([])
+        for array, key_column, value_column in group:
+            numbered[-1].append((len(arrays), key_column, value_column))
+            arrays.append(array)
+    vmem = pl.BlockSpec(memory_space=pltpu.VMEM)
+    return pl.pallas_call(
+        functools.partial(attend_kernel, n_q, q_block * HEAD_DIM, numbered),
         in_specs=[pl.BlockSpec(memory_space=pltpu.SMEM)]
-        + [vmem] * (n_q + n_kv + 2)
+        + [vmem] * (n_q + len(arrays))
         + [pl.BlockSpec(memory_space=pl.ANY)] * len(earlier),
         out_specs=[vmem] * n_q,
         out_shape=[jax.ShapeDtypeStruct((queries[0].shape[0], PAIR), jnp.bfloat16)] * n_q,
         compiler_params=pltpu.CompilerParams(vmem_limit_bytes=24 * 2**20),
-        cost_estimate=SMALL,
+        cost_estimate=BIG,
         name="attend",
-    )(scalars, *queries, *kvs, text_keys, text_values, *earlier)
+    )(scalars, *queries, *arrays, *earlier)
 
 
 def text_kernel(planes, where, keys, values, *refs):
-    keys_out, values_out = refs[-2:]
+    out = refs[-1]
     slab = planes * PAIR
     for phase in range(keys.shape[1] // slab):
         columns = pl.ds(pl.multiple_of(phase * slab + where[0] * PAIR, PAIR), PAIR)
-        keys_out[:, phase * PAIR : (phase + 1) * PAIR] = keys[:, columns]
-        values_out[:, phase * PAIR : (phase + 1) * PAIR] = values[:, columns]
+        out[:, 2 * phase * PAIR : (2 * phase + 1) * PAIR] = keys[:, columns]
+        out[:, (2 * phase + 1) * PAIR : (2 * phase + 2) * PAIR] = values[:, columns]
 
 
 def own_text(where, planes, text_keys, text_values, earlier):
     vmem = pl.BlockSpec(memory_space=pltpu.VMEM)
-    shape = jax.ShapeDtypeStruct((text_keys.shape[0], text_keys.shape[1] // planes), text_keys.dtype)
+    shape = jax.ShapeDtypeStruct((text_keys.shape[0], 2 * text_keys.shape[1] // planes), text_keys.dtype)
     return pl.pallas_call(
         functools.partial(text_kernel, planes),
         in_specs=[pl.BlockSpec(memory_space=pltpu.SMEM), vmem, vmem]
         + [pl.BlockSpec(memory_space=pl.ANY)] * len(earlier),
-        out_specs=[vmem] * 2,
-        out_shape=[shape] * 2,
+        out_specs=vmem,
+        out_shape=shape,
         compiler_params=pltpu.CompilerParams(vmem_limit_bytes=6 * 2**20),
         cost_estimate=SMALL,
         name="own_text",
@@ -269,60 +275,62 @@
     def send(piece, r):
         return swap(piece, PLANE * r)
 
-    def heads(p, pieces, block, gathered, earlier):
-        return attend_pair(
-            scalars, pieces, block, gathered, text_keys, text_values, 2 * p, earlier
-        )
-
-    fast, slow = (3,), (1, 2)
-    z1 = first_pack(where, 0, planes, keys, values)
-    groups = [((1, 1), (2, 1)), ((1, 2), (2, 2), (0, 0)), ((0, 1),), ((0, 2),)]
-    z2, z3, z4, z5 = pack(where, groups, planes, (queries, keys, values), z1)
-    text_keys, text_values = own_text(where, planes, text_keys, text_values, [z5[0]])
-    added = sum_deltas(plan, deltas, [text_keys])
-
     def release(batch, lanes):
         return [(0, [batch[r]], None) for r in lanes]
 
-    in1 = {r: send(z1[r], r) for r in range(1, planes)}
-    out = tick(release(z2, fast), [in1[r] for r in fast] + [added], LARGE)
-    in2 = {r: send(piece, r) for r, piece in zip(fast, out)}
-    out = tick([(0, [z1[0]] + [in1[r] for r in range(1, planes)], 2 * PAIR)] + release(z2, slow), [out[0]], MID)
-    own1, sent = out[0], out[1:]
-    other1 = swap(own1, 2)
-    in2.update({r: send(piece, r) for r, piece in zip(slow, sent)})
-    out = tick(release(z3, fast), [in2[r] for r in fast] + [own1], LARGE)
-    in3 = {r: send(piece, r) for r, piece in zip(fast, out)}
-    out = tick(
-        [(0, [other1, own1], None), (0, [z2[0]] + [in2[r] for r in range(1, planes)], 2 * PAIR)] + release(z3, slow),
-        [out[0]],
-        MID,
-    )
-    pair1, own2, sent = out[0], out[1], out[2:]
-    other2, core1 = swap(own2, 2), swap(pair1, 1)
-    in3.update({r: send(piece, r) for r, piece in zip(slow, sent)})
-    out = tick(release(z4, fast), [own2] + [in3[r] for r in fast], LARGE)
-    in4 = {r: send(piece, r) for r, piece in zip(fast, out)}
-    out = tick(
-        [(0, [other2, own2], None), (0, [z3[0]] + [in3[r] for r in range(1, planes)], 2 * PAIR)] + release(z4, slow),
-        [in3[r] for r in slow] + [out[0]],
-        MID,
-    )
-    pair2, own3, sent = out[0], out[1], out[2:]
-    other3, core2 = swap(own3, 2), swap(pair2, 1)
-    in4.update({r: send(piece, r) for r, piece in zip(slow, sent)})
-    context1 = heads(0, [z3[0]] + [in3[r] for r in range(1, planes)], 4, [pair1, core1], [own3])
-    out = tick(release(z5, fast), [context1[0]] + [in4[r] for r in fast], LARGE)
-    in5 = {r: send(piece, r) for r, piece in zip(fast, out)}
-    out = tick(release(z5, slow), [in4[r] for r in slow] + [out[0]], MID)
-    in5.update({r: send(piece, r) for r, piece in zip(slow, out)})
-    context2 = heads(1, [z4[0]] + [in4[r] for r in range(1, planes)], 0, [pair2, core2], [out[0]])
-    out = tick([(0, [other3, own3], None)] + [(1, [context1[r], context2[r]], None) for r in range(planes)], [in5[r] for r in range(1, planes)], MID)
-    pair3, contexts = out[0], out[1:]
+    def sent(lanes, pieces):
+        return {r: send(piece, r) for r, piece in zip(lanes, pieces)}
+
+    def whole(batch, arrived):
+        return [batch[0]] + [arrived[r] for r in range(1, planes)]
+
+    def received_kv(arrived):
+        return (0, [arrived[r] for r in range(1, planes)], 2 * PAIR)
+
+    every = tuple(range(1, planes))
+    fast, slow = every[-1:], every[:-1]
+    *z1, own_all = first_pack(where, planes, keys, values)
+    groups = [((1, 1), (2, 1)), ((1, 2), (2, 2), (0, 0)), ((0, 1), (0, 2))]
+    z2, z3, z4 = pack(where, groups, planes, (queries, keys, values), z1)
+    text = own_text(where, planes, text_keys, text_values, [z2[0]])
+    added = sum_deltas(plan, deltas, [text])
+
+    in1 = {r: send(z1[r], r) for r in every}
+    own_other = swap(own_all, 2)
+    out = tick(release(z2, fast), [added] + [in1[r] for r in fast], BIG)
+    in2 = sent(fast, out)
+    received1, *out = tick([received_kv(in1)] + release(z2, slow), [out[0]], MID)
+    in2.update(sent(slow, out))
+    other1 = swap(received1, 2)
+    (own_pair,) = tick([(0, [own_all, own_other], None)], [received1], SMALL)
+    own_core = swap(own_pair, 1)
+    out = tick(release(z3, fast), [received1] + [in2[r] for r in fast], BIG)
+    in3 = sent(fast, out)
+    received2, *out = tick([received_kv(in2)] + release(z3, slow), [out[0]], MID)
+    in3.update(sent(slow, out))
+    (pair1,) = tick([(0, [other1, received1], None)], [received2], MID)
+    other2, core1 = swap(received2, 2), swap(pair1, 1)
+    out = tick(release(z4, fast), [received2] + [in3[r] for r in fast], BIG)
+    in4 = sent(fast, out)
+    received3, *out = tick([received_kv(in3)] + release(z4, slow), [out[0], core1, own_core], MID)
+    in4.update(sent(slow, out))
+    (pair2,) = tick([(0, [other2, received2], None)], [received3], MID)
+    other3, core2 = swap(received3, 2), swap(pair2, 1)
+
+    def heads(phase, pieces, block, pair, core, earlier):
+        at = 2 * PAIR * phase
+        mine = [(array, at, at + PAIR) for array in (own_all, own_other, own_core, text)]
+        return attend_pair(scalars, pieces, block, [[(pair, 0, PAIR)], [(core, 0, PAIR)], mine], earlier)
+
+    context1 = heads(0, whole(z3, in3), 4, pair1, core1, [received3, pair2] + [in4[r] for r in fast])
+    context2 = heads(1, whole(z4, in4), 0, pair2, core2, [context1[0]])
+    pair3, *contexts = tick(
+        [(0, [other3, received3], None)] + [(1, [context1[r], context2[r]], None) for r in range(planes)], [], MID
+    )
     core3 = swap(pair3, 1)
-    returned = [contexts[0]] + [send(contexts[r], r) for r in range(1, planes)]
-    context3 = heads(2, [z5[0]] + [in5[r] for r in range(1, planes)], 0, [pair3, core3], [])
-    returned += [context3[0]] + [send(context3[r], r) for r in range(1, planes)]
+    returned = [contexts[0]] + [send(contexts[r], r) for r in every]
+    context3 = heads(2, whole(z4, in4), 2, pair3, core3, [])
+    returned += [context3[0]] + [send(context3[r], r) for r in every]
     return mix(where, planes, added, returned)
 
 
@@ -417,7 +425,7 @@
 def solution(mesh):
     size = mesh.shape["seq"]
     planes = size // PLANE
-    fits = planes in (2, 4) and planes * PLANE == size and HEADS % (2 * planes) == 0
+    fits = planes * PLANE == size and planes * 6 == HEADS
     return jax.shard_map(
         plane_body if fits else general_body,
         mesh=mesh,

time: 89.3 us -> 85 us (0.952)
  waiting for transfers between devices: 25.4 us -> 23.4 us
  local copies, waits for them, and re-layouts: 7 us -> 5.85 us
    ppermute x27 -> x26, waiting for transfers between devices: 25.4 us -> 23.4 us  [swap(): return lax.ppermute(array, 'seq', [(i, i ^ distance) for i in range(size)])]
    unnamed x18, local copies, waits for them, and re-layouts: 7 us -> 5.85 us
    ppermute x27 -> x26, starting transfers between devices: 39.1 us -> 38.4 us  [swap(): return lax.ppermute(array, 'seq', [(i, i ^ distance) for i in range(size)])]
  transfers between devices with their start and end apart: 27 -> 26, of which waited for: 8 -> 7; matrix products, arithmetic and copies ran while one was open for 0% -> 0% of each run, Pallas kernels for 17% -> 17%
where the time goes in v4:
time: 85 us; the launch traced here: 84.7 us
  starting transfers between devices  38.4 us (45%)
  waiting for transfers between devices  23.4 us (28%)
  Pallas kernels  16.1 us (19%)
  local copies, waits for them, and re-layouts  5.85 us (7%)
  between operations  0.91 us (1%)
    ppermute x26, starting transfers between devices, swap(): return lax.ppermute(array, 'seq', [(i, i ^ distance) for i in range(size)])  38.4 us
    ppermute x26, waiting for transfers between devices, swap(): return lax.ppermute(array, 'seq', [(i, i ^ distance) for i in range(size)])  23.4 us
    pallas_call x3, Pallas kernels, attend_pair(): pl.pallas_call(functools.partial(attend_kernel, n_q, q_block * HEAD_DIM,...  12.3 us
    unnamed x18, local copies, waits for them, and re-layouts  5.85 us
    pallas_call x1, Pallas kernels, sum_deltas(): pl.pallas_call(deltas_kernel, grid=(4,), in_specs=[pl.BlockSpec(memory_sp...  1.88 us
  transfers between devices with their start and end apart: 26, of which 7 were waited for; matrix products, arithmetic and copies ran while one was open for 0% of the time, Pallas kernels for 17%

profile of v4, /device:TPU:0, one launch (start us, length us, event | category | flops | bytes accessed | tf_op | source)
XLA Modules:
  0.0 84.7 jit_solution(15436724469437443110)
XLA Ops:
  2.4 5.1 %collective-permute-start = (bf16[128,512]{1,0:T(8,128)(2,1)S(1)}, bf16[128,512]{1,0:T(8,128)(2,1)S(1)}, u32[]{:S(2)}, u32[]{:S(2)}) collective-permute-start(bf16[128,512]{1,0:T(8,128)(2,1)S(1)} %get-tuple-element.51.refs_6_), channel_id=1, source_target_pairs={{0,12},{1,13},{2,14},{3,15},{4,8},{5,9},{6,10},{7,11},{8,4},{9,5},... | collective-permute-start | bytes 393224 | tf_op jit(solution)/shard_map/ppermute | solution.py:273
  9.6 1.5 %copy-done.6 = bf16[256,3072]{1,0:T(8,128)(2,1)S(1)} copy-done((bf16[256,3072]{1,0:T(8,128)(2,1)S(1)}, bf16[256,3072]{1,0:T(8,128)(2,1)}, u32[]{:S(2)}) %copy-start.6) | copy-done | bytes 1572888
  12.1 1.9 %deltas.2.refs_0_.added = f32[128,3072]{1,0:T(8,128)S(1)} custom-call(s32[6]{0:T(128)S(1)} %copy-done.8, bf16[6,128,3072]{2,1,0:T(8,128)(2,1)S(1)} %copy-done, bf16[256,1536]{1,0:T(8,128)(2,1)S(1)} %own_text.1.refs_0_.refs_9_), custom_call_target="tpu_custom_call" | custom-call | flops 1 | bytes 1 | tf_op jit(solution)/shard_map/deltas/pallas_call | solution.py:221
  14.0 3.8 %collective-permute-start.3 = (bf16[128,512]{1,0:T(8,128)(2,1)S(1)}, bf16[128,512]{1,0:T(8,128)(2,1)S(1)}, u32[]{:S(2)}, u32[]{:S(2)}) collective-permute-start(bf16[128,512]{1,0:T(8,128)(2,1)S(1)} %tick.10.refs_0_), channel_id=1, source_target_pairs={{0,12},{1,13},{2,14},{3,15},{4,8},{5,9},{6,10},{7,11},{8,4},{9,5},... | collective-permute-start | bytes 393224 | tf_op jit(solution)/shard_map/ppermute | solution.py:273
  17.8 1.5 %collective-permute-start.9 = (bf16[128,1536]{1,0:T(8,128)(2,1)S(1)}, bf16[128,1536]{1,0:T(8,128)(2,1)S(1)}, u32[]{:S(2)}, u32[]{:S(2)}) collective-permute-start(bf16[128,1536]{1,0:T(8,128)(2,1)S(1)} %get-tuple-element.64.refs_1_.refs_6_), channel_id=1, source_target_pairs={{0,2},{1,3},{2,0},{3,1},{4,6},{5,7},{6,4},{7,5},{8,10},{9,11},{10,... | collective-permute-start | bytes 1179656 | tf_op jit(solution)/shard_map/ppermute | solution.py:273
  20.0 2.3 %collective-permute-done.2.refs_2_ = bf16[128,512]{1,0:T(8,128)(2,1)S(1)} collective-permute-done((bf16[128,512]{1,0:T(8,128)(2,1)S(1)}, bf16[128,512]{1,0:T(8,128)(2,1)S(1)}, u32[]{:S(2)}, u32[]{:S(2)}) %collective-permute-start.2) | collective-permute-done | bytes 131104 | tf_op jit(solution)/shard_map/ppermute | solution.py:273
  22.5 1.3 %collective-permute-start.5 = (bf16[128,512]{1,0:T(8,128)(2,1)S(1)}, bf16[128,512]{1,0:T(8,128)(2,1)S(1)}, u32[]{:S(2)}, u32[]{:S(2)}) collective-permute-start(bf16[128,512]{1,0:T(8,128)(2,1)S(1)} %get-tuple-element.59), channel_id=1, source_target_pairs={{0,8},{1,9},{2,10},{3,11},{4,12},{5,13},{6,14},{7,15},{8,0},{9,1},... | collective-permute-start | bytes 393224 | tf_op jit(solution)/shard_map/ppermute | solution.py:273
  23.8 1.5 %collective-permute-start.7 = (bf16[384,512]{1,0:T(8,128)(2,1)S(1)}, bf16[384,512]{1,0:T(8,128)(2,1)S(1)}, u32[]{:S(2)}, u32[]{:S(2)}) collective-permute-start(bf16[384,512]{1,0:T(8,128)(2,1)S(1)} %get-tuple-element.56.refs_0_.refs_2_), channel_id=1, source_target_pairs={{0,2},{1,3},{2,0},{3,1},{4,6},{5,7},{6,4},{7,5},{8,10},{9,11},{10,... | collective-permute-start | bytes 1179656 | tf_op jit(solution)/shard_map/ppermute | solution.py:273
  25.4 3.1 %collective-permute-start.6 = (bf16[128,768]{1,0:T(8,128)(2,1)S(1)}, bf16[128,768]{1,0:T(8,128)(2,1)S(1)}, u32[]{:S(2)}, u32[]{:S(2)}) collective-permute-start(bf16[128,768]{1,0:T(8,128)(2,1)S(1)} %tick.12.refs_0_), channel_id=1, source_target_pairs={{0,12},{1,13},{2,14},{3,15},{4,8},{5,9},{6,10},{7,11},{8,4},{9,5},... | collective-permute-start | bytes 589832 | tf_op jit(solution)/shard_map/ppermute | solution.py:273
  29.2 5.7 %collective-permute-done.5.refs_2_ = bf16[128,512]{1,0:T(8,128)(2,1)S(1)} collective-permute-done((bf16[128,512]{1,0:T(8,128)(2,1)S(1)}, bf16[128,512]{1,0:T(8,128)(2,1)S(1)}, u32[]{:S(2)}, u32[]{:S(2)}) %collective-permute-start.5) | collective-permute-done | bytes 131104 | tf_op jit(solution)/shard_map/ppermute | solution.py:273
  35.1 2.8 %collective-permute-start.12 = (bf16[128,768]{1,0:T(8,128)(2,1)S(1)}, bf16[128,768]{1,0:T(8,128)(2,1)S(1)}, u32[]{:S(2)}, u32[]{:S(2)}) collective-permute-start(bf16[128,768]{1,0:T(8,128)(2,1)S(1)} %get-tuple-element.66), channel_id=1, source_target_pairs={{0,8},{1,9},{2,10},{3,11},{4,12},{5,13},{6,14},{7,15},{8,0},{9,1},... | collective-permute-start | bytes 589832 | tf_op jit(solution)/shard_map/ppermute | solution.py:273
  37.9 1.5 %collective-permute-start.14 = (bf16[384,512]{1,0:T(8,128)(2,1)S(1)}, bf16[384,512]{1,0:T(8,128)(2,1)S(1)}, u32[]{:S(2)}, u32[]{:S(2)}) collective-permute-start(bf16[384,512]{1,0:T(8,128)(2,1)S(1)} %get-tuple-element.62.refs_0_.refs_2_), channel_id=1, source_target_pairs={{0,2},{1,3},{2,0},{3,1},{4,6},{5,7},{6,4},{7,5},{8,10},{9,11},{10,... | collective-permute-start | bytes 1179656 | tf_op jit(solution)/shard_map/ppermute | solution.py:273
  41.4 2.5 %collective-permute-start.15 = (bf16[128,512]{1,0:T(8,128)(2,1)S(1)}, bf16[128,512]{1,0:T(8,128)(2,1)S(1)}, u32[]{:S(2)}, u32[]{:S(2)}) collective-permute-start(bf16[128,512]{1,0:T(8,128)(2,1)S(1)} %tick.14.refs_0_), channel_id=1, source_target_pairs={{0,12},{1,13},{2,14},{3,15},{4,8},{5,9},{6,10},{7,11},{8,4},{9,5},... | collective-permute-start | bytes 393224 | tf_op jit(solution)/shard_map/ppermute | solution.py:273
  43.9 6.5 %collective-permute-done.12.refs_4_.refs_2_ = bf16[128,768]{1,0:T(8,128)(2,1)S(1)} collective-permute-done((bf16[128,768]{1,0:T(8,128)(2,1)S(1)}, bf16[128,768]{1,0:T(8,128)(2,1)S(1)}, u32[]{:S(2)}, u32[]{:S(2)}) %collective-permute-start.12) | collective-permute-done | bytes 196640 | tf_op jit(solution)/shard_map/ppermute | solution.py:273
  50.6 2.8 %collective-permute-start.17 = (bf16[128,512]{1,0:T(8,128)(2,1)S(1)}, bf16[128,512]{1,0:T(8,128)(2,1)S(1)}, u32[]{:S(2)}, u32[]{:S(2)}) collective-permute-start(bf16[128,512]{1,0:T(8,128)(2,1)S(1)} %get-tuple-element.74), channel_id=1, source_target_pairs={{0,8},{1,9},{2,10},{3,11},{4,12},{5,13},{6,14},{7,15},{8,0},{9,1},... | collective-permute-start | bytes 393224 | tf_op jit(solution)/shard_map/ppermute | solution.py:273
  53.3 1.5 %collective-permute-start.13 = (bf16[384,512]{1,0:T(8,128)(2,1)S(1)}, bf16[384,512]{1,0:T(8,128)(2,1)S(1)}, u32[]{:S(2)}, u32[]{:S(2)}) collective-permute-start(bf16[384,512]{1,0:T(8,128)(2,1)S(1)} %get-tuple-element.69.refs_0_.refs_10_.refs_1_), channel_id=1, source_target_pairs={{0,2},{1,3},{2,0},{3,1},{4,6},{5,7},{6,4},{7,5},{8,10},{9,11},{10,... | collective-permute-start | bytes 1179656 | tf_op jit(solution)/shard_map/ppermute | solution.py:273
  55.0 4.0 %attend.3 = (bf16[128,256]{1,0:T(8,128)(2,1)S(1)}, bf16[128,256]{1,0:T(8,128)(2,1)S(1)}, bf16[128,256]{1,0:T(8,128)(2,1)S(1)}, bf16[128,256]{1,0:T(8,128)(2,1)S(1)}) custom-call(s32[2]{0:T(128)S(1)} %pad_add_fusion.scalars, bf16[128,768]{1,0:T(8,128)(2,1)S(1)} %get-tuple-element.70.refs_0_, bf16[128,768]{1,0:T(8,128)(2,1)S(1)} %collective-permute-done.11.refs_3_.refs_1_, ...), custom_call_target="tpu_custom_call" | custom-call | flops 20000000000 | bytes 1 | tf_op jit(solution)/shard_map/attend/pallas_call | solution.py:173
  59.1 4.1 %attend.4 = (bf16[128,256]{1,0:T(8,128)(2,1)S(1)}, bf16[128,256]{1,0:T(8,128)(2,1)S(1)}, bf16[128,256]{1,0:T(8,128)(2,1)S(1)}, bf16[128,256]{1,0:T(8,128)(2,1)S(1)}) custom-call(s32[2]{0:T(128)S(1)} %pad_add_fusion.scalars, bf16[128,512]{1,0:T(8,128)(2,1)S(1)} %get-tuple-element.72.refs_0_, bf16[128,512]{1,0:T(8,128)(2,1)S(1)} %collective-permute-done.16.refs_1_, ...), custom_call_target="tpu_custom_call" | custom-call | flops 20000000000 | bytes 1 | tf_op jit(solution)/shard_map/attend/pallas_call | solution.py:173
  63.9 2.3 %collective-permute-start.20 = (bf16[128,512]{1,0:T(8,128)(2,1)S(1)}, bf16[128,512]{1,0:T(8,128)(2,1)S(1)}, u32[]{:S(2)}, u32[]{:S(2)}) collective-permute-start(bf16[128,512]{1,0:T(8,128)(2,1)S(1)} %get-tuple-element.84), channel_id=1, source_target_pairs={{0,8},{1,9},{2,10},{3,11},{4,12},{5,13},{6,14},{7,15},{8,0},{9,1},... | collective-permute-start | bytes 393224 | tf_op jit(solution)/shard_map/ppermute | solution.py:273
  66.2 2.0 %collective-permute-start.21 = (bf16[128,512]{1,0:T(8,128)(2,1)S(1)}, bf16[128,512]{1,0:T(8,128)(2,1)S(1)}, u32[]{:S(2)}, u32[]{:S(2)}) collective-permute-start(bf16[128,512]{1,0:T(8,128)(2,1)S(1)} %get-tuple-element.85), channel_id=1, source_target_pairs={{0,12},{1,13},{2,14},{3,15},{4,8},{5,9},{6,10},{7,11},{8,4},{9,5},... | collective-permute-start | bytes 393224 | tf_op jit(solution)/shard_map/ppermute | solution.py:273
  68.2 4.1 %attend.5 = (bf16[128,256]{1,0:T(8,128)(2,1)S(1)}, bf16[128,256]{1,0:T(8,128)(2,1)S(1)}, bf16[128,256]{1,0:T(8,128)(2,1)S(1)}, bf16[128,256]{1,0:T(8,128)(2,1)S(1)}) custom-call(s32[2]{0:T(128)S(1)} %pad_add_fusion.scalars, bf16[128,512]{1,0:T(8,128)(2,1)S(1)} %get-tuple-element.72.refs_0_, bf16[128,512]{1,0:T(8,128)(2,1)S(1)} %collective-permute-done.16.refs_1_, ...), custom_call_target="tpu_custom_call" | custom-call | flops 20000000000 | bytes 1 | tf_op jit(solution)/shard_map/attend/pallas_call | solution.py:173
  72.4 2.4 %collective-permute-start.24 = (bf16[128,256]{1,0:T(8,128)(2,1)S(1)}, bf16[128,256]{1,0:T(8,128)(2,1)S(1)}, u32[]{:S(2)}, u32[]{:S(2)}) collective-permute-start(bf16[128,256]{1,0:T(8,128)(2,1)S(1)} %get-tuple-element.89), channel_id=1, source_target_pairs={{0,8},{1,9},{2,10},{3,11},{4,12},{5,13},{6,14},{7,15},{8,0},{9,1},... | collective-permute-start | bytes 196616 | tf_op jit(solution)/shard_map/ppermute | solution.py:273
  74.8 2.0 %collective-permute-start.25 = (bf16[128,256]{1,0:T(8,128)(2,1)S(1)}, bf16[128,256]{1,0:T(8,128)(2,1)S(1)}, u32[]{:S(2)}, u32[]{:S(2)}) collective-permute-start(bf16[128,256]{1,0:T(8,128)(2,1)S(1)} %get-tuple-element.90), channel_id=1, source_target_pairs={{0,12},{1,13},{2,14},{3,15},{4,8},{5,9},{6,10},{7,11},{8,4},{9,5},... | collective-permute-start | bytes 196616 | tf_op jit(solution)/shard_map/ppermute | solution.py:273
  77.5 6.1 %collective-permute-done.24.refs_6_ = bf16[128,256]{1,0:T(8,128)(2,1)S(1)} collective-permute-done((bf16[128,256]{1,0:T(8,128)(2,1)S(1)}, bf16[128,256]{1,0:T(8,128)(2,1)S(1)}, u32[]{:S(2)}, u32[]{:S(2)}) %collective-permute-start.24) | collective-permute-done | bytes 65568 | tf_op jit(solution)/shard_map/ppermute | solution.py:273
  (65 shorter events, 11.2 us)
Async XLA Ops:
  2.4 11.6 %collective-permute-start = (bf16[128,512]{1,0:T(8,128)(2,1)S(1)}, bf16[128,512]{1,0:T(8,128)(2,1)S(1)}, u32[]{:S(2)}, u32[]{:S(2)}) collective-permute-start(bf16[128,512]{1,0:T(8,128)(2,1)S(1)} %get-tuple-element.51.refs_6_), channel_id=1, source_target_pairs={{0,12},{1,13},{2,14},{3,15},{4,8},{5,9},{6,10},{7,11},{8,4},{9,5},... | collective-permute-start | bytes 393224 | tf_op jit(solution)/shard_map/ppermute | solution.py:273
  7.5 12.5 %collective-permute-start.1 = (bf16[128,512]{1,0:T(8,128)(2,1)S(1)}, bf16[128,512]{1,0:T(8,128)(2,1)S(1)}, u32[]{:S(2)}, u32[]{:S(2)}) collective-permute-start(bf16[128,512]{1,0:T(8,128)(2,1)S(1)} %get-tuple-element.49.refs_4_), channel_id=1, source_target_pairs={{0,4},{1,5},{2,6},{3,7},{4,0},{5,1},{6,2},{7,3},{8,12},{9,13},{10,... | collective-permute-start | bytes 393224 | tf_op jit(solution)/shard_map/ppermute | solution.py:273
  7.5 14.8 %collective-permute-start.2 = (bf16[128,512]{1,0:T(8,128)(2,1)S(1)}, bf16[128,512]{1,0:T(8,128)(2,1)S(1)}, u32[]{:S(2)}, u32[]{:S(2)}) collective-permute-start(bf16[128,512]{1,0:T(8,128)(2,1)S(1)} %get-tuple-element.50.refs_5_), channel_id=1, source_target_pairs={{0,8},{1,9},{2,10},{3,11},{4,12},{5,13},{6,14},{7,15},{8,0},{9,1},... | collective-permute-start | bytes 393224 | tf_op jit(solution)/shard_map/ppermute | solution.py:273
  14.0 11.3 %collective-permute-start.3 = (bf16[128,512]{1,0:T(8,128)(2,1)S(1)}, bf16[128,512]{1,0:T(8,128)(2,1)S(1)}, u32[]{:S(2)}, u32[]{:S(2)}) collective-permute-start(bf16[128,512]{1,0:T(8,128)(2,1)S(1)} %tick.10.refs_0_), channel_id=1, source_target_pairs={{0,12},{1,13},{2,14},{3,15},{4,8},{5,9},{6,10},{7,11},{8,4},{9,5},... | collective-permute-start | bytes 393224 | tf_op jit(solution)/shard_map/ppermute | solution.py:273
  17.8 20.1 %collective-permute-start.9 = (bf16[128,1536]{1,0:T(8,128)(2,1)S(1)}, bf16[128,1536]{1,0:T(8,128)(2,1)S(1)}, u32[]{:S(2)}, u32[]{:S(2)}) collective-permute-start(bf16[128,1536]{1,0:T(8,128)(2,1)S(1)} %get-tuple-element.64.refs_1_.refs_6_), channel_id=1, source_target_pairs={{0,2},{1,3},{2,0},{3,1},{4,6},{5,7},{6,4},{7,5},{8,10},{9,11},{10,... | collective-permute-start | bytes 1179656 | tf_op jit(solution)/shard_map/ppermute | solution.py:273
  22.4 6.8 %collective-permute-start.4 = (bf16[128,512]{1,0:T(8,128)(2,1)S(1)}, bf16[128,512]{1,0:T(8,128)(2,1)S(1)}, u32[]{:S(2)}, u32[]{:S(2)}) collective-permute-start(bf16[128,512]{1,0:T(8,128)(2,1)S(1)} %get-tuple-element.58), channel_id=1, source_target_pairs={{0,4},{1,5},{2,6},{3,7},{4,0},{5,1},{6,2},{7,3},{8,12},{9,13},{10,... | collective-permute-start | bytes 393224 | tf_op jit(solution)/shard_map/ppermute | solution.py:273
  22.5 12.5 %collective-permute-start.5 = (bf16[128,512]{1,0:T(8,128)(2,1)S(1)}, bf16[128,512]{1,0:T(8,128)(2,1)S(1)}, u32[]{:S(2)}, u32[]{:S(2)}) collective-permute-start(bf16[128,512]{1,0:T(8,128)(2,1)S(1)} %get-tuple-element.59), channel_id=1, source_target_pairs={{0,8},{1,9},{2,10},{3,11},{4,12},{5,13},{6,14},{7,15},{8,0},{9,1},... | collective-permute-start | bytes 393224 | tf_op jit(solution)/shard_map/ppermute | solution.py:273
  23.8 15.6 %collective-permute-start.7 = (bf16[384,512]{1,0:T(8,128)(2,1)S(1)}, bf16[384,512]{1,0:T(8,128)(2,1)S(1)}, u32[]{:S(2)}, u32[]{:S(2)}) collective-permute-start(bf16[384,512]{1,0:T(8,128)(2,1)S(1)} %get-tuple-element.56.refs_0_.refs_2_), channel_id=1, source_target_pairs={{0,2},{1,3},{2,0},{3,1},{4,6},{5,7},{6,4},{7,5},{8,10},{9,11},{10,... | collective-permute-start | bytes 1179656 | tf_op jit(solution)/shard_map/ppermute | solution.py:273
  25.4 14.2 %collective-permute-start.6 = (bf16[128,768]{1,0:T(8,128)(2,1)S(1)}, bf16[128,768]{1,0:T(8,128)(2,1)S(1)}, u32[]{:S(2)}, u32[]{:S(2)}) collective-permute-start(bf16[128,768]{1,0:T(8,128)(2,1)S(1)} %tick.12.refs_0_), channel_id=1, source_target_pairs={{0,12},{1,13},{2,14},{3,15},{4,8},{5,9},{6,10},{7,11},{8,4},{9,5},... | collective-permute-start | bytes 589832 | tf_op jit(solution)/shard_map/ppermute | solution.py:273
  35.0 6.3 %collective-permute-start.11 = (bf16[128,768]{1,0:T(8,128)(2,1)S(1)}, bf16[128,768]{1,0:T(8,128)(2,1)S(1)}, u32[]{:S(2)}, u32[]{:S(2)}) collective-permute-start(bf16[128,768]{1,0:T(8,128)(2,1)S(1)} %get-tuple-element.65), channel_id=1, source_target_pairs={{0,4},{1,5},{2,6},{3,7},{4,0},{5,1},{6,2},{7,3},{8,12},{9,13},{10,... | collective-permute-start | bytes 589832 | tf_op jit(solution)/shard_map/ppermute | solution.py:273
  35.1 15.3 %collective-permute-start.12 = (bf16[128,768]{1,0:T(8,128)(2,1)S(1)}, bf16[128,768]{1,0:T(8,128)(2,1)S(1)}, u32[]{:S(2)}, u32[]{:S(2)}) collective-permute-start(bf16[128,768]{1,0:T(8,128)(2,1)S(1)} %get-tuple-element.66), channel_id=1, source_target_pairs={{0,8},{1,9},{2,10},{3,11},{4,12},{5,13},{6,14},{7,15},{8,0},{9,1},... | collective-permute-start | bytes 589832 | tf_op jit(solution)/shard_map/ppermute | solution.py:273
  37.9 17.0 %collective-permute-start.14 = (bf16[384,512]{1,0:T(8,128)(2,1)S(1)}, bf16[384,512]{1,0:T(8,128)(2,1)S(1)}, u32[]{:S(2)}, u32[]{:S(2)}) collective-permute-start(bf16[384,512]{1,0:T(8,128)(2,1)S(1)} %get-tuple-element.62.refs_0_.refs_2_), channel_id=1, source_target_pairs={{0,2},{1,3},{2,0},{3,1},{4,6},{5,7},{6,4},{7,5},{8,10},{9,11},{10,... | collective-permute-start | bytes 1179656 | tf_op jit(solution)/shard_map/ppermute | solution.py:273
  39.5 11.0 %collective-permute-start.10 = (bf16[256,1536]{1,0:T(8,128)(2,1)S(1)}, bf16[256,1536]{1,0:T(8,128)(2,1)S(1)}, u32[]{:S(2)}, u32[]{:S(2)}) collective-permute-start(bf16[256,1536]{1,0:T(8,128)(2,1)S(1)} %tick.16), channel_id=1, source_target_pairs={{0,1},{1,0},{2,3},{3,2},{4,5},{5,4},{6,7},{7,6},{8,9},{9,8},{10,11... | collective-permute-start | bytes 2359304 | tf_op jit(solution)/shard_map/ppermute | solution.py:273
  39.6 10.8 %collective-permute-start.8 = (bf16[768,512]{1,0:T(8,128)(2,1)S(1)}, bf16[768,512]{1,0:T(8,128)(2,1)S(1)}, u32[]{:S(2)}, u32[]{:S(2)}) collective-permute-start(bf16[768,512]{1,0:T(8,128)(2,1)S(1)} %tick.15.refs_4_), channel_id=1, source_target_pairs={{0,1},{1,0},{2,3},{3,2},{4,5},{5,4},{6,7},{7,6},{8,9},{9,8},{10,11... | collective-permute-start | bytes 2359304 | tf_op jit(solution)/shard_map/ppermute | solution.py:273
  41.4 13.6 %collective-permute-start.15 = (bf16[128,512]{1,0:T(8,128)(2,1)S(1)}, bf16[128,512]{1,0:T(8,128)(2,1)S(1)}, u32[]{:S(2)}, u32[]{:S(2)}) collective-permute-start(bf16[128,512]{1,0:T(8,128)(2,1)S(1)} %tick.14.refs_0_), channel_id=1, source_target_pairs={{0,12},{1,13},{2,14},{3,15},{4,8},{5,9},{6,10},{7,11},{8,4},{9,5},... | collective-permute-start | bytes 393224 | tf_op jit(solution)/shard_map/ppermute | solution.py:273
  50.5 8.5 %collective-permute-start.16 = (bf16[128,512]{1,0:T(8,128)(2,1)S(1)}, bf16[128,512]{1,0:T(8,128)(2,1)S(1)}, u32[]{:S(2)}, u32[]{:S(2)}) collective-permute-start(bf16[128,512]{1,0:T(8,128)(2,1)S(1)} %get-tuple-element.73), channel_id=1, source_target_pairs={{0,4},{1,5},{2,6},{3,7},{4,0},{5,1},{6,2},{7,3},{8,12},{9,13},{10,... | collective-permute-start | bytes 393224 | tf_op jit(solution)/shard_map/ppermute | solution.py:273
  50.6 8.5 %collective-permute-start.17 = (bf16[128,512]{1,0:T(8,128)(2,1)S(1)}, bf16[128,512]{1,0:T(8,128)(2,1)S(1)}, u32[]{:S(2)}, u32[]{:S(2)}) collective-permute-start(bf16[128,512]{1,0:T(8,128)(2,1)S(1)} %get-tuple-element.74), channel_id=1, source_target_pairs={{0,8},{1,9},{2,10},{3,11},{4,12},{5,13},{6,14},{7,15},{8,0},{9,1},... | collective-permute-start | bytes 393224 | tf_op jit(solution)/shard_map/ppermute | solution.py:273
  53.3 9.8 %collective-permute-start.13 = (bf16[384,512]{1,0:T(8,128)(2,1)S(1)}, bf16[384,512]{1,0:T(8,128)(2,1)S(1)}, u32[]{:S(2)}, u32[]{:S(2)}) collective-permute-start(bf16[384,512]{1,0:T(8,128)(2,1)S(1)} %get-tuple-element.69.refs_0_.refs_10_.refs_1_), channel_id=1, source_target_pairs={{0,2},{1,3},{2,0},{3,1},{4,6},{5,7},{6,4},{7,5},{8,10},{9,11},{10,... | collective-permute-start | bytes 1179656 | tf_op jit(solution)/shard_map/ppermute | solution.py:273
  63.8 11.0 %collective-permute-start.19 = (bf16[128,512]{1,0:T(8,128)(2,1)S(1)}, bf16[128,512]{1,0:T(8,128)(2,1)S(1)}, u32[]{:S(2)}, u32[]{:S(2)}) collective-permute-start(bf16[128,512]{1,0:T(8,128)(2,1)S(1)} %get-tuple-element.83), channel_id=1, source_target_pairs={{0,4},{1,5},{2,6},{3,7},{4,0},{5,1},{6,2},{7,3},{8,12},{9,13},{10,... | collective-permute-start | bytes 393224 | tf_op jit(solution)/shard_map/ppermute | solution.py:273
  63.9 13.6 %collective-permute-start.20 = (bf16[128,512]{1,0:T(8,128)(2,1)S(1)}, bf16[128,512]{1,0:T(8,128)(2,1)S(1)}, u32[]{:S(2)}, u32[]{:S(2)}) collective-permute-start(bf16[128,512]{1,0:T(8,128)(2,1)S(1)} %get-tuple-element.84), channel_id=1, source_target_pairs={{0,8},{1,9},{2,10},{3,11},{4,12},{5,13},{6,14},{7,15},{8,0},{9,1},... | collective-permute-start | bytes 393224 | tf_op jit(solution)/shard_map/ppermute | solution.py:273
  66.2 11.3 %collective-permute-start.21 = (bf16[128,512]{1,0:T(8,128)(2,1)S(1)}, bf16[128,512]{1,0:T(8,128)(2,1)S(1)}, u32[]{:S(2)}, u32[]{:S(2)}) collective-permute-start(bf16[128,512]{1,0:T(8,128)(2,1)S(1)} %get-tuple-element.85), channel_id=1, source_target_pairs={{0,12},{1,13},{2,14},{3,15},{4,8},{5,9},{6,10},{7,11},{8,4},{9,5},... | collective-permute-start | bytes 393224 | tf_op jit(solution)/shard_map/ppermute | solution.py:273
  72.4 5.2 %collective-permute-start.23 = (bf16[128,256]{1,0:T(8,128)(2,1)S(1)}, bf16[128,256]{1,0:T(8,128)(2,1)S(1)}, u32[]{:S(2)}, u32[]{:S(2)}) collective-permute-start(bf16[128,256]{1,0:T(8,128)(2,1)S(1)} %get-tuple-element.88), channel_id=1, source_target_pairs={{0,4},{1,5},{2,6},{3,7},{4,0},{5,1},{6,2},{7,3},{8,12},{9,13},{10,... | collective-permute-start | bytes 196616 | tf_op jit(solution)/shard_map/ppermute | solution.py:273
  72.4 11.2 %collective-permute-start.24 = (bf16[128,256]{1,0:T(8,128)(2,1)S(1)}, bf16[128,256]{1,0:T(8,128)(2,1)S(1)}, u32[]{:S(2)}, u32[]{:S(2)}) collective-permute-start(bf16[128,256]{1,0:T(8,128)(2,1)S(1)} %get-tuple-element.89), channel_id=1, source_target_pairs={{0,8},{1,9},{2,10},{3,11},{4,12},{5,13},{6,14},{7,15},{8,0},{9,1},... | collective-permute-start | bytes 196616 | tf_op jit(solution)/shard_map/ppermute | solution.py:273
  74.8 8.8 %collective-permute-start.25 = (bf16[128,256]{1,0:T(8,128)(2,1)S(1)}, bf16[128,256]{1,0:T(8,128)(2,1)S(1)}, u32[]{:S(2)}, u32[]{:S(2)}) collective-permute-start(bf16[128,256]{1,0:T(8,128)(2,1)S(1)} %get-tuple-element.90), channel_id=1, source_target_pairs={{0,12},{1,13},{2,14},{3,15},{4,8},{5,9},{6,10},{7,11},{8,4},{9,5},... | collective-permute-start | bytes 196616 | tf_op jit(solution)/shard_map/ppermute | solution.py:273
  (11 other events, 36.8 us)

commit v5 on v4

--- a/solution.py
+++ b/solution.py
@@ -147,16 +147,12 @@
                 scores = jnp.where(usable, scores, -jnp.inf)
             block_top = jnp.max(scores, axis=1, keepdims=True)
             new_top = block_top if top is None else jnp.maximum(top, block_top)
-            weights = jnp.exp2((scores - new_top) * EXP_SCALE)
-            block_total = jnp.sum(weights, axis=1, keepdims=True)
-            block_weighted = jnp.dot(weights.astype(jnp.bfloat16), values, preferred_element_type=jnp.float32)
-            if top is None:
-                total, weighted = block_total, block_weighted
-            else:
-                rescale = jnp.exp2((top - new_top) * EXP_SCALE)
-                total, weighted = total * rescale + block_total, weighted * rescale + block_weighted
+            weights = jnp.exp2((scores - new_top) * EXP_SCALE).astype(jnp.bfloat16)
+            extended = jnp.concatenate([values, jnp.ones_like(values)], axis=1)
+            block_sums = jnp.dot(weights, extended, preferred_element_type=jnp.float32)
+            sums = block_sums if top is None else sums * jnp.exp2((top - new_top) * EXP_SCALE) + block_sums
             top = new_top
-        context = (weighted / total).astype(jnp.bfloat16)
+        context = (sums[:, :HEAD_DIM] / sums[:, HEAD_DIM:]).astype(jnp.bfloat16)
         for index, out in enumerate(outs):
             out[:, here] = context[index * rows : (index + 1) * rows]
 
@@ -234,24 +230,22 @@
     )(plan, deltas, *earlier)
 
 
-def mix_kernel(planes, where, added, *refs):
-    pieces, out = refs[:-1], refs[-1]
-    slab = planes * PAIR
-    phase = 0
-    for first in range(0, len(pieces), planes):
-        for part in range(pieces[first].shape[1] // PAIR):
-            for relative in range(planes):
-                plane = jnp.bitwise_xor(where[0], relative)
-                columns = pl.ds(pl.multiple_of(phase * slab + plane * PAIR, PAIR), PAIR)
-                piece = pieces[first + relative][:, part * PAIR : (part + 1) * PAIR]
-                out[:, columns] = (piece.astype(jnp.float32) + added[:, columns]).astype(out.dtype)
-            phase += 1
-
-
-def mix(where, planes, added, pieces):
-    vmem = pl.BlockSpec(memory_space=pltpu.VMEM)
-    return pl.pallas_call(
-        functools.partial(mix_kernel, planes),
+def mix_kernel(planes, places, where, added, *refs):
+    out = refs[-1]
+    for index, relative, phases in places:
+        plane = jnp.bitwise_xor(where[0], relative)
+        for part, phase in enumerate(phases):
+            columns = pl.ds(pl.multiple_of((phase * planes + plane) * PAIR, PAIR), PAIR)
+            piece = refs[index][:, part * PAIR : (part + 1) * PAIR]
+            out[:, columns] = (piece.astype(jnp.float32) + added[:, columns]).astype(out.dtype)
+
+
+def mix(where, planes, added, returned):
+    places = [(index, relative, phases) for index, (_, relative, phases) in enumerate(returned)]
+    pieces = [array for array, _, _ in returned]
+    vmem = pl.BlockSpec(memory_space=pltpu.VMEM)
+    return pl.pallas_call(
+        functools.partial(mix_kernel, planes, places),
         in_specs=[pl.BlockSpec(memory_space=pltpu.SMEM)] + [vmem] * (1 + len(pieces)),
         out_specs=vmem,
         out_shape=jax.ShapeDtypeStruct(added.shape, jnp.bfloat16),
@@ -319,18 +313,29 @@
 
     def heads(phase, pieces, block, pair, core, earlier):
         at = 2 * PAIR * phase
-        mine = [(array, at, at + PAIR) for array in (own_all, own_other, own_core, text)]
-        return attend_pair(scalars, pieces, block, [[(pair, 0, PAIR)], [(core, 0, PAIR)], mine], earlier)
+        near = [(pair, 0, PAIR), (own_all, at, at + PAIR), (own_other, at, at + PAIR)]
+        far = [(core, 0, PAIR), (own_core, at, at + PAIR)]
+        return attend_pair(scalars, pieces, block, [near, far, [(text, at, at + PAIR)]], earlier)
 
     context1 = heads(0, whole(z3, in3), 4, pair1, core1, [received3, pair2] + [in4[r] for r in fast])
+    early = (3,)
+    returned = [(send(context1[r], r), r, (0,)) for r in early]
     context2 = heads(1, whole(z4, in4), 0, pair2, core2, [context1[0]])
+    late = [r for r in range(planes) if r not in early]
     pair3, *contexts = tick(
-        [(0, [other3, received3], None)] + [(1, [context1[r], context2[r]], None) for r in range(planes)], [], MID
+        [(0, [other3, received3], None)]
+        + [(1, [context1[r], context2[r]], None) for r in late]
+        + [(0, [context2[r]], None) for r in early],
+        [array for array, _, _ in returned],
+        MID,
     )
     core3 = swap(pair3, 1)
-    returned = [contexts[0]] + [send(contexts[r], r) for r in every]
+    for r, both in zip(late, contexts):
+        returned.append((send(both, r) if r else both, r, (0, 1)))
+    for r, one in zip(early, contexts[len(late) :]):
+        returned.append((send(one, r), r, (1,)))
     context3 = heads(2, whole(z4, in4), 2, pair3, core3, [])
-    returned += [context3[0]] + [send(context3[r], r) for r in every]
+    returned += [(send(context3[r], r) if r else context3[r], r, (2,)) for r in range(planes)]
     return mix(where, planes, added, returned)
 
 

time: 85 us -> 83.5 us (0.982)
  waiting for transfers between devices: 23.4 us -> 21.3 us
  starting transfers between devices: 38.4 us -> 39.9 us
  Pallas kernels: 16.1 us -> 15.1 us
    ppermute x26 -> x27, waiting for transfers between devices: 23.4 us -> 21.3 us  [swap(): return lax.ppermute(array, 'seq', [(i, i ^ distance) for i in range(size)])]
    ppermute x26 -> x27, starting transfers between devices: 38.4 us -> 39.9 us  [swap(): return lax.ppermute(array, 'seq', [(i, i ^ distance) for i in range(size)])]
    pallas_call x3, Pallas kernels: 12.3 us -> 11.4 us  [attend_pair(): pl.pallas_call(functools.partial(attend_kernel, n_q, q_block * HEAD_DIM,...]
  transfers between devices with their start and end apart: 26 -> 27, of which waited for: 7 -> 9; matrix products, arithmetic and copies ran while one was open for 0% -> 0% of each run, Pallas kernels for 17% -> 17%
where the time goes in v5:
time: 83.5 us; the launch traced here: 83.2 us
  starting transfers between devices  39.9 us (48%)
  waiting for transfers between devices  21.3 us (26%)
  Pallas kernels  15.1 us (18%)
  local copies, waits for them, and re-layouts  5.85 us (7%)
  between operations  0.89 us (1%)
    ppermute x27, starting transfers between devices, swap(): return lax.ppermute(array, 'seq', [(i, i ^ distance) for i in range(size)])  39.9 us
    ppermute x27, waiting for transfers between devices, swap(): return lax.ppermute(array, 'seq', [(i, i ^ distance) for i in range(size)])  21.3 us
    pallas_call x3, Pallas kernels, attend_pair(): pl.pallas_call(functools.partial(attend_kernel, n_q, q_block * HEAD_DIM,...  11.4 us
    unnamed x18, local copies, waits for them, and re-layouts  5.85 us
    pallas_call x1, Pallas kernels, sum_deltas(): pl.pallas_call(deltas_kernel, grid=(4,), in_specs=[pl.BlockSpec(memory_sp...  1.88 us
  transfers between devices with their start and end apart: 27, of which 9 were waited for; matrix products, arithmetic and copies ran while one was open for 0% of the time, Pallas kernels for 17%

profile of v5, /device:TPU:0, one launch (start us, length us, event | category | flops | bytes accessed | tf_op | source)
XLA Modules:
  0.0 83.2 jit_solution(15873236623284902014)
XLA Ops:
  2.4 5.1 %collective-permute-start = (bf16[128,512]{1,0:T(8,128)(2,1)S(1)}, bf16[128,512]{1,0:T(8,128)(2,1)S(1)}, u32[]{:S(2)}, u32[]{:S(2)}) collective-permute-start(bf16[128,512]{1,0:T(8,128)(2,1)S(1)} %get-tuple-element.51.refs_6_), channel_id=1, source_target_pairs={{0,12},{1,13},{2,14},{3,15},{4,8},{5,9},{6,10},{7,11},{8,4},{9,5},... | collective-permute-start | bytes 393224 | tf_op jit(solution)/shard_map/ppermute | solution.py:267
  9.6 1.5 %copy-done.6 = bf16[256,3072]{1,0:T(8,128)(2,1)S(1)} copy-done((bf16[256,3072]{1,0:T(8,128)(2,1)S(1)}, bf16[256,3072]{1,0:T(8,128)(2,1)}, u32[]{:S(2)}) %copy-start.6) | copy-done | bytes 1572888
  12.1 1.9 %deltas.2.refs_0_.added = f32[128,3072]{1,0:T(8,128)S(1)} custom-call(s32[6]{0:T(128)S(1)} %copy-done.8, bf16[6,128,3072]{2,1,0:T(8,128)(2,1)S(1)} %copy-done, bf16[256,1536]{1,0:T(8,128)(2,1)S(1)} %own_text.1.refs_0_.refs_9_), custom_call_target="tpu_custom_call" | custom-call | flops 1 | bytes 1 | tf_op jit(solution)/shard_map/deltas/pallas_call | solution.py:217
  14.0 3.8 %collective-permute-start.3 = (bf16[128,512]{1,0:T(8,128)(2,1)S(1)}, bf16[128,512]{1,0:T(8,128)(2,1)S(1)}, u32[]{:S(2)}, u32[]{:S(2)}) collective-permute-start(bf16[128,512]{1,0:T(8,128)(2,1)S(1)} %tick.10.refs_0_), channel_id=1, source_target_pairs={{0,12},{1,13},{2,14},{3,15},{4,8},{5,9},{6,10},{7,11},{8,4},{9,5},... | collective-permute-start | bytes 393224 | tf_op jit(solution)/shard_map/ppermute | solution.py:267
  17.8 1.5 %collective-permute-start.10 = (bf16[128,1536]{1,0:T(8,128)(2,1)S(1)}, bf16[128,1536]{1,0:T(8,128)(2,1)S(1)}, u32[]{:S(2)}, u32[]{:S(2)}) collective-permute-start(bf16[128,1536]{1,0:T(8,128)(2,1)S(1)} %get-tuple-element.66.refs_1_.refs_5_), channel_id=1, source_target_pairs={{0,2},{1,3},{2,0},{3,1},{4,6},{5,7},{6,4},{7,5},{8,10},{9,11},{10,... | collective-permute-start | bytes 1179656 | tf_op jit(solution)/shard_map/ppermute | solution.py:267
  20.0 2.3 %collective-permute-done.2.refs_2_ = bf16[128,512]{1,0:T(8,128)(2,1)S(1)} collective-permute-done((bf16[128,512]{1,0:T(8,128)(2,1)S(1)}, bf16[128,512]{1,0:T(8,128)(2,1)S(1)}, u32[]{:S(2)}, u32[]{:S(2)}) %collective-permute-start.2) | collective-permute-done | bytes 131104 | tf_op jit(solution)/shard_map/ppermute | solution.py:267
  23.8 1.5 %collective-permute-start.9 = (bf16[384,512]{1,0:T(8,128)(2,1)S(1)}, bf16[384,512]{1,0:T(8,128)(2,1)S(1)}, u32[]{:S(2)}, u32[]{:S(2)}) collective-permute-start(bf16[384,512]{1,0:T(8,128)(2,1)S(1)} %get-tuple-element.57.refs_0_.refs_2_), channel_id=1, source_target_pairs={{0,2},{1,3},{2,0},{3,1},{4,6},{5,7},{6,4},{7,5},{8,10},{9,11},{10,... | collective-permute-start | bytes 1179656 | tf_op jit(solution)/shard_map/ppermute | solution.py:267
  25.4 3.1 %collective-permute-start.8 = (bf16[128,768]{1,0:T(8,128)(2,1)S(1)}, bf16[128,768]{1,0:T(8,128)(2,1)S(1)}, u32[]{:S(2)}, u32[]{:S(2)}) collective-permute-start(bf16[128,768]{1,0:T(8,128)(2,1)S(1)} %tick.12.refs_0_), channel_id=1, source_target_pairs={{0,12},{1,13},{2,14},{3,15},{4,8},{5,9},{6,10},{7,11},{8,4},{9,5},... | collective-permute-start | bytes 589832 | tf_op jit(solution)/shard_map/ppermute | solution.py:267
  29.2 5.7 %collective-permute-done.5.refs_2_ = bf16[128,512]{1,0:T(8,128)(2,1)S(1)} collective-permute-done((bf16[128,512]{1,0:T(8,128)(2,1)S(1)}, bf16[128,512]{1,0:T(8,128)(2,1)S(1)}, u32[]{:S(2)}, u32[]{:S(2)}) %collective-permute-start.5) | collective-permute-done | bytes 131104 | tf_op jit(solution)/shard_map/ppermute | solution.py:267
  35.1 2.8 %collective-permute-start.7 = (bf16[128,768]{1,0:T(8,128)(2,1)S(1)}, bf16[128,768]{1,0:T(8,128)(2,1)S(1)}, u32[]{:S(2)}, u32[]{:S(2)}) collective-permute-start(bf16[128,768]{1,0:T(8,128)(2,1)S(1)} %get-tuple-element.64), channel_id=1, source_target_pairs={{0,8},{1,9},{2,10},{3,11},{4,12},{5,13},{6,14},{7,15},{8,0},{9,1},... | collective-permute-start | bytes 589832 | tf_op jit(solution)/shard_map/ppermute | solution.py:267
  37.9 1.5 %collective-permute-start.13 = (bf16[384,512]{1,0:T(8,128)(2,1)S(1)}, bf16[384,512]{1,0:T(8,128)(2,1)S(1)}, u32[]{:S(2)}, u32[]{:S(2)}) collective-permute-start(bf16[384,512]{1,0:T(8,128)(2,1)S(1)} %get-tuple-element.65.refs_0_.refs_2_), channel_id=1, source_target_pairs={{0,2},{1,3},{2,0},{3,1},{4,6},{5,7},{6,4},{7,5},{8,10},{9,11},{10,... | collective-permute-start | bytes 1179656 | tf_op jit(solution)/shard_map/ppermute | solution.py:267
  41.4 2.5 %collective-permute-start.14 = (bf16[128,512]{1,0:T(8,128)(2,1)S(1)}, bf16[128,512]{1,0:T(8,128)(2,1)S(1)}, u32[]{:S(2)}, u32[]{:S(2)}) collective-permute-start(bf16[128,512]{1,0:T(8,128)(2,1)S(1)} %tick.16.refs_0_), channel_id=1, source_target_pairs={{0,12},{1,13},{2,14},{3,15},{4,8},{5,9},{6,10},{7,11},{8,4},{9,5},... | collective-permute-start | bytes 393224 | tf_op jit(solution)/shard_map/ppermute | solution.py:267
  43.9 6.5 %collective-permute-done.7.refs_4_.refs_2_ = bf16[128,768]{1,0:T(8,128)(2,1)S(1)} collective-permute-done((bf16[128,768]{1,0:T(8,128)(2,1)S(1)}, bf16[128,768]{1,0:T(8,128)(2,1)S(1)}, u32[]{:S(2)}, u32[]{:S(2)}) %collective-permute-start.7) | collective-permute-done | bytes 196640 | tf_op jit(solution)/shard_map/ppermute | solution.py:267
  50.6 2.8 %collective-permute-start.18 = (bf16[128,512]{1,0:T(8,128)(2,1)S(1)}, bf16[128,512]{1,0:T(8,128)(2,1)S(1)}, u32[]{:S(2)}, u32[]{:S(2)}) collective-permute-start(bf16[128,512]{1,0:T(8,128)(2,1)S(1)} %get-tuple-element.75), channel_id=1, source_target_pairs={{0,8},{1,9},{2,10},{3,11},{4,12},{5,13},{6,14},{7,15},{8,0},{9,1},... | collective-permute-start | bytes 393224 | tf_op jit(solution)/shard_map/ppermute | solution.py:267
  53.3 1.5 %collective-permute-start.16 = (bf16[384,512]{1,0:T(8,128)(2,1)S(1)}, bf16[384,512]{1,0:T(8,128)(2,1)S(1)}, u32[]{:S(2)}, u32[]{:S(2)}) collective-permute-start(bf16[384,512]{1,0:T(8,128)(2,1)S(1)} %get-tuple-element.70.refs_0_.refs_10_.refs_2_), channel_id=1, source_target_pairs={{0,2},{1,3},{2,0},{3,1},{4,6},{5,7},{6,4},{7,5},{8,10},{9,11},{10,... | collective-permute-start | bytes 1179656 | tf_op jit(solution)/shard_map/ppermute | solution.py:267
  55.0 3.7 %attend.3 = (bf16[128,256]{1,0:T(8,128)(2,1)S(1)}, bf16[128,256]{1,0:T(8,128)(2,1)S(1)}, bf16[128,256]{1,0:T(8,128)(2,1)S(1)}, bf16[128,256]{1,0:T(8,128)(2,1)S(1)}) custom-call(s32[2]{0:T(128)S(1)} %pad_add_fusion.scalars, bf16[128,768]{1,0:T(8,128)(2,1)S(1)} %get-tuple-element.53.refs_0_, bf16[128,768]{1,0:T(8,128)(2,1)S(1)} %collective-permute-done.6.refs_3_.refs_1_, ...), custom_call_target="tpu_custom_call" | custom-call | flops 20000000000 | bytes 1 | tf_op jit(solution)/shard_map/attend/pallas_call | solution.py:169
  58.7 1.9 %collective-permute-start.15 = (bf16[128,256]{1,0:T(8,128)(2,1)S(1)}, bf16[128,256]{1,0:T(8,128)(2,1)S(1)}, u32[]{:S(2)}, u32[]{:S(2)}) collective-permute-start(bf16[128,256]{1,0:T(8,128)(2,1)S(1)} %get-tuple-element.71), channel_id=1, source_target_pairs={{0,12},{1,13},{2,14},{3,15},{4,8},{5,9},{6,10},{7,11},{8,4},{9,5},... | collective-permute-start | bytes 196616 | tf_op jit(solution)/shard_map/ppermute | solution.py:267
  60.7 3.8 %attend.4 = (bf16[128,256]{1,0:T(8,128)(2,1)S(1)}, bf16[128,256]{1,0:T(8,128)(2,1)S(1)}, bf16[128,256]{1,0:T(8,128)(2,1)S(1)}, bf16[128,256]{1,0:T(8,128)(2,1)S(1)}) custom-call(s32[2]{0:T(128)S(1)} %pad_add_fusion.scalars, bf16[128,512]{1,0:T(8,128)(2,1)S(1)} %get-tuple-element.73.refs_0_, bf16[128,512]{1,0:T(8,128)(2,1)S(1)} %collective-permute-done.17.refs_1_, ...), custom_call_target="tpu_custom_call" | custom-call | flops 20000000000 | bytes 1 | tf_op jit(solution)/shard_map/attend/pallas_call | solution.py:169
  65.2 1.9 %collective-permute-start.22 = (bf16[128,256]{1,0:T(8,128)(2,1)S(1)}, bf16[128,256]{1,0:T(8,128)(2,1)S(1)}, u32[]{:S(2)}, u32[]{:S(2)}) collective-permute-start(bf16[128,256]{1,0:T(8,128)(2,1)S(1)} %get-tuple-element.85), channel_id=1, source_target_pairs={{0,12},{1,13},{2,14},{3,15},{4,8},{5,9},{6,10},{7,11},{8,4},{9,5},... | collective-permute-start | bytes 196616 | tf_op jit(solution)/shard_map/ppermute | solution.py:267
  67.2 2.5 %collective-permute-start.21 = (bf16[128,512]{1,0:T(8,128)(2,1)S(1)}, bf16[128,512]{1,0:T(8,128)(2,1)S(1)}, u32[]{:S(2)}, u32[]{:S(2)}) collective-permute-start(bf16[128,512]{1,0:T(8,128)(2,1)S(1)} %get-tuple-element.84), channel_id=1, source_target_pairs={{0,8},{1,9},{2,10},{3,11},{4,12},{5,13},{6,14},{7,15},{8,0},{9,1},... | collective-permute-start | bytes 393224 | tf_op jit(solution)/shard_map/ppermute | solution.py:267
  69.7 3.8 %attend.5 = (bf16[128,256]{1,0:T(8,128)(2,1)S(1)}, bf16[128,256]{1,0:T(8,128)(2,1)S(1)}, bf16[128,256]{1,0:T(8,128)(2,1)S(1)}, bf16[128,256]{1,0:T(8,128)(2,1)S(1)}) custom-call(s32[2]{0:T(128)S(1)} %pad_add_fusion.scalars, bf16[128,512]{1,0:T(8,128)(2,1)S(1)} %get-tuple-element.73.refs_0_, bf16[128,512]{1,0:T(8,128)(2,1)S(1)} %collective-permute-done.17.refs_1_, ...), custom_call_target="tpu_custom_call" | custom-call | flops 20000000000 | bytes 1 | tf_op jit(solution)/shard_map/attend/pallas_call | solution.py:169
  73.6 2.4 %collective-permute-start.25 = (bf16[128,256]{1,0:T(8,128)(2,1)S(1)}, bf16[128,256]{1,0:T(8,128)(2,1)S(1)}, u32[]{:S(2)}, u32[]{:S(2)}) collective-permute-start(bf16[128,256]{1,0:T(8,128)(2,1)S(1)} %get-tuple-element.89), channel_id=1, source_target_pairs={{0,8},{1,9},{2,10},{3,11},{4,12},{5,13},{6,14},{7,15},{8,0},{9,1},... | collective-permute-start | bytes 196616 | tf_op jit(solution)/shard_map/ppermute | solution.py:267
  76.0 2.0 %collective-permute-start.26 = (bf16[128,256]{1,0:T(8,128)(2,1)S(1)}, bf16[128,256]{1,0:T(8,128)(2,1)S(1)}, u32[]{:S(2)}, u32[]{:S(2)}) collective-permute-start(bf16[128,256]{1,0:T(8,128)(2,1)S(1)} %get-tuple-element.90), channel_id=1, source_target_pairs={{0,12},{1,13},{2,14},{3,15},{4,8},{5,9},{6,10},{7,11},{8,4},{9,5},... | collective-permute-start | bytes 196616 | tf_op jit(solution)/shard_map/ppermute | solution.py:267
  79.3 2.1 %collective-permute-done.25.refs_7_ = bf16[128,256]{1,0:T(8,128)(2,1)S(1)} collective-permute-done((bf16[128,256]{1,0:T(8,128)(2,1)S(1)}, bf16[128,256]{1,0:T(8,128)(2,1)S(1)}, u32[]{:S(2)}, u32[]{:S(2)}) %collective-permute-start.25) | collective-permute-done | bytes 65568 | tf_op jit(solution)/shard_map/ppermute | solution.py:267
  (67 shorter events, 13.9 us)
Async XLA Ops:
  2.4 11.6 %collective-permute-start = (bf16[128,512]{1,0:T(8,128)(2,1)S(1)}, bf16[128,512]{1,0:T(8,128)(2,1)S(1)}, u32[]{:S(2)}, u32[]{:S(2)}) collective-permute-start(bf16[128,512]{1,0:T(8,128)(2,1)S(1)} %get-tuple-element.51.refs_6_), channel_id=1, source_target_pairs={{0,12},{1,13},{2,14},{3,15},{4,8},{5,9},{6,10},{7,11},{8,4},{9,5},... | collective-permute-start | bytes 393224 | tf_op jit(solution)/shard_map/ppermute | solution.py:267
  7.5 12.5 %collective-permute-start.1 = (bf16[128,512]{1,0:T(8,128)(2,1)S(1)}, bf16[128,512]{1,0:T(8,128)(2,1)S(1)}, u32[]{:S(2)}, u32[]{:S(2)}) collective-permute-start(bf16[128,512]{1,0:T(8,128)(2,1)S(1)} %get-tuple-element.49.refs_4_), channel_id=1, source_target_pairs={{0,4},{1,5},{2,6},{3,7},{4,0},{5,1},{6,2},{7,3},{8,12},{9,13},{10,... | collective-permute-start | bytes 393224 | tf_op jit(solution)/shard_map/ppermute | solution.py:267
  7.5 14.8 %collective-permute-start.2 = (bf16[128,512]{1,0:T(8,128)(2,1)S(1)}, bf16[128,512]{1,0:T(8,128)(2,1)S(1)}, u32[]{:S(2)}, u32[]{:S(2)}) collective-permute-start(bf16[128,512]{1,0:T(8,128)(2,1)S(1)} %get-tuple-element.50.refs_5_), channel_id=1, source_target_pairs={{0,8},{1,9},{2,10},{3,11},{4,12},{5,13},{6,14},{7,15},{8,0},{9,1},... | collective-permute-start | bytes 393224 | tf_op jit(solution)/shard_map/ppermute | solution.py:267
  14.0 11.3 %collective-permute-start.3 = (bf16[128,512]{1,0:T(8,128)(2,1)S(1)}, bf16[128,512]{1,0:T(8,128)(2,1)S(1)}, u32[]{:S(2)}, u32[]{:S(2)}) collective-permute-start(bf16[128,512]{1,0:T(8,128)(2,1)S(1)} %tick.10.refs_0_), channel_id=1, source_target_pairs={{0,12},{1,13},{2,14},{3,15},{4,8},{5,9},{6,10},{7,11},{8,4},{9,5},... | collective-permute-start | bytes 393224 | tf_op jit(solution)/shard_map/ppermute | solution.py:267
  17.8 20.1 %collective-permute-start.10 = (bf16[128,1536]{1,0:T(8,128)(2,1)S(1)}, bf16[128,1536]{1,0:T(8,128)(2,1)S(1)}, u32[]{:S(2)}, u32[]{:S(2)}) collective-permute-start(bf16[128,1536]{1,0:T(8,128)(2,1)S(1)} %get-tuple-element.66.refs_1_.refs_5_), channel_id=1, source_target_pairs={{0,2},{1,3},{2,0},{3,1},{4,6},{5,7},{6,4},{7,5},{8,10},{9,11},{10,... | collective-permute-start | bytes 1179656 | tf_op jit(solution)/shard_map/ppermute | solution.py:267
  22.4 6.8 %collective-permute-start.4 = (bf16[128,512]{1,0:T(8,128)(2,1)S(1)}, bf16[128,512]{1,0:T(8,128)(2,1)S(1)}, u32[]{:S(2)}, u32[]{:S(2)}) collective-permute-start(bf16[128,512]{1,0:T(8,128)(2,1)S(1)} %get-tuple-element.59), channel_id=1, source_target_pairs={{0,4},{1,5},{2,6},{3,7},{4,0},{5,1},{6,2},{7,3},{8,12},{9,13},{10,... | collective-permute-start | bytes 393224 | tf_op jit(solution)/shard_map/ppermute | solution.py:267
  22.5 12.5 %collective-permute-start.5 = (bf16[128,512]{1,0:T(8,128)(2,1)S(1)}, bf16[128,512]{1,0:T(8,128)(2,1)S(1)}, u32[]{:S(2)}, u32[]{:S(2)}) collective-permute-start(bf16[128,512]{1,0:T(8,128)(2,1)S(1)} %get-tuple-element.60), channel_id=1, source_target_pairs={{0,8},{1,9},{2,10},{3,11},{4,12},{5,13},{6,14},{7,15},{8,0},{9,1},... | collective-permute-start | bytes 393224 | tf_op jit(solution)/shard_map/ppermute | solution.py:267
  23.8 15.6 %collective-permute-start.9 = (bf16[384,512]{1,0:T(8,128)(2,1)S(1)}, bf16[384,512]{1,0:T(8,128)(2,1)S(1)}, u32[]{:S(2)}, u32[]{:S(2)}) collective-permute-start(bf16[384,512]{1,0:T(8,128)(2,1)S(1)} %get-tuple-element.57.refs_0_.refs_2_), channel_id=1, source_target_pairs={{0,2},{1,3},{2,0},{3,1},{4,6},{5,7},{6,4},{7,5},{8,10},{9,11},{10,... | collective-permute-start | bytes 1179656 | tf_op jit(solution)/shard_map/ppermute | solution.py:267
  25.4 14.2 %collective-permute-start.8 = (bf16[128,768]{1,0:T(8,128)(2,1)S(1)}, bf16[128,768]{1,0:T(8,128)(2,1)S(1)}, u32[]{:S(2)}, u32[]{:S(2)}) collective-permute-start(bf16[128,768]{1,0:T(8,128)(2,1)S(1)} %tick.12.refs_0_), channel_id=1, source_target_pairs={{0,12},{1,13},{2,14},{3,15},{4,8},{5,9},{6,10},{7,11},{8,4},{9,5},... | collective-permute-start | bytes 589832 | tf_op jit(solution)/shard_map/ppermute | solution.py:267
  35.0 6.3 %collective-permute-start.6 = (bf16[128,768]{1,0:T(8,128)(2,1)S(1)}, bf16[128,768]{1,0:T(8,128)(2,1)S(1)}, u32[]{:S(2)}, u32[]{:S(2)}) collective-permute-start(bf16[128,768]{1,0:T(8,128)(2,1)S(1)} %get-tuple-element.63), channel_id=1, source_target_pairs={{0,4},{1,5},{2,6},{3,7},{4,0},{5,1},{6,2},{7,3},{8,12},{9,13},{10,... | collective-permute-start | bytes 589832 | tf_op jit(solution)/shard_map/ppermute | solution.py:267
  35.1 15.3 %collective-permute-start.7 = (bf16[128,768]{1,0:T(8,128)(2,1)S(1)}, bf16[128,768]{1,0:T(8,128)(2,1)S(1)}, u32[]{:S(2)}, u32[]{:S(2)}) collective-permute-start(bf16[128,768]{1,0:T(8,128)(2,1)S(1)} %get-tuple-element.64), channel_id=1, source_target_pairs={{0,8},{1,9},{2,10},{3,11},{4,12},{5,13},{6,14},{7,15},{8,0},{9,1},... | collective-permute-start | bytes 589832 | tf_op jit(solution)/shard_map/ppermute | solution.py:267
  37.9 17.0 %collective-permute-start.13 = (bf16[384,512]{1,0:T(8,128)(2,1)S(1)}, bf16[384,512]{1,0:T(8,128)(2,1)S(1)}, u32[]{:S(2)}, u32[]{:S(2)}) collective-permute-start(bf16[384,512]{1,0:T(8,128)(2,1)S(1)} %get-tuple-element.65.refs_0_.refs_2_), channel_id=1, source_target_pairs={{0,2},{1,3},{2,0},{3,1},{4,6},{5,7},{6,4},{7,5},{8,10},{9,11},{10,... | collective-permute-start | bytes 1179656 | tf_op jit(solution)/shard_map/ppermute | solution.py:267
  39.5 11.0 %collective-permute-start.12 = (bf16[256,1536]{1,0:T(8,128)(2,1)S(1)}, bf16[256,1536]{1,0:T(8,128)(2,1)S(1)}, u32[]{:S(2)}, u32[]{:S(2)}) collective-permute-start(bf16[256,1536]{1,0:T(8,128)(2,1)S(1)} %tick.15), channel_id=1, source_target_pairs={{0,1},{1,0},{2,3},{3,2},{4,5},{5,4},{6,7},{7,6},{8,9},{9,8},{10,11... | collective-permute-start | bytes 2359304 | tf_op jit(solution)/shard_map/ppermute | solution.py:267
  39.6 10.8 %collective-permute-start.11 = (bf16[768,512]{1,0:T(8,128)(2,1)S(1)}, bf16[768,512]{1,0:T(8,128)(2,1)S(1)}, u32[]{:S(2)}, u32[]{:S(2)}) collective-permute-start(bf16[768,512]{1,0:T(8,128)(2,1)S(1)} %tick.14.refs_4_), channel_id=1, source_target_pairs={{0,1},{1,0},{2,3},{3,2},{4,5},{5,4},{6,7},{7,6},{8,9},{9,8},{10,11... | collective-permute-start | bytes 2359304 | tf_op jit(solution)/shard_map/ppermute | solution.py:267
  41.4 13.6 %collective-permute-start.14 = (bf16[128,512]{1,0:T(8,128)(2,1)S(1)}, bf16[128,512]{1,0:T(8,128)(2,1)S(1)}, u32[]{:S(2)}, u32[]{:S(2)}) collective-permute-start(bf16[128,512]{1,0:T(8,128)(2,1)S(1)} %tick.16.refs_0_), channel_id=1, source_target_pairs={{0,12},{1,13},{2,14},{3,15},{4,8},{5,9},{6,10},{7,11},{8,4},{9,5},... | collective-permute-start | bytes 393224 | tf_op jit(solution)/shard_map/ppermute | solution.py:267
  50.5 10.2 %collective-permute-start.17 = (bf16[128,512]{1,0:T(8,128)(2,1)S(1)}, bf16[128,512]{1,0:T(8,128)(2,1)S(1)}, u32[]{:S(2)}, u32[]{:S(2)}) collective-permute-start(bf16[128,512]{1,0:T(8,128)(2,1)S(1)} %get-tuple-element.74), channel_id=1, source_target_pairs={{0,4},{1,5},{2,6},{3,7},{4,0},{5,1},{6,2},{7,3},{8,12},{9,13},{10,... | collective-permute-start | bytes 393224 | tf_op jit(solution)/shard_map/ppermute | solution.py:267
  50.6 10.1 %collective-permute-start.18 = (bf16[128,512]{1,0:T(8,128)(2,1)S(1)}, bf16[128,512]{1,0:T(8,128)(2,1)S(1)}, u32[]{:S(2)}, u32[]{:S(2)}) collective-permute-start(bf16[128,512]{1,0:T(8,128)(2,1)S(1)} %get-tuple-element.75), channel_id=1, source_target_pairs={{0,8},{1,9},{2,10},{3,11},{4,12},{5,13},{6,14},{7,15},{8,0},{9,1},... | collective-permute-start | bytes 393224 | tf_op jit(solution)/shard_map/ppermute | solution.py:267
  53.3 11.7 %collective-permute-start.16 = (bf16[384,512]{1,0:T(8,128)(2,1)S(1)}, bf16[384,512]{1,0:T(8,128)(2,1)S(1)}, u32[]{:S(2)}, u32[]{:S(2)}) collective-permute-start(bf16[384,512]{1,0:T(8,128)(2,1)S(1)} %get-tuple-element.70.refs_0_.refs_10_.refs_2_), channel_id=1, source_target_pairs={{0,2},{1,3},{2,0},{3,1},{4,6},{5,7},{6,4},{7,5},{8,10},{9,11},{10,... | collective-permute-start | bytes 1179656 | tf_op jit(solution)/shard_map/ppermute | solution.py:267
  58.7 6.3 %collective-permute-start.15 = (bf16[128,256]{1,0:T(8,128)(2,1)S(1)}, bf16[128,256]{1,0:T(8,128)(2,1)S(1)}, u32[]{:S(2)}, u32[]{:S(2)}) collective-permute-start(bf16[128,256]{1,0:T(8,128)(2,1)S(1)} %get-tuple-element.71), channel_id=1, source_target_pairs={{0,12},{1,13},{2,14},{3,15},{4,8},{5,9},{6,10},{7,11},{8,4},{9,5},... | collective-permute-start | bytes 196616 | tf_op jit(solution)/shard_map/ppermute | solution.py:267
  65.2 10.8 %collective-permute-start.22 = (bf16[128,256]{1,0:T(8,128)(2,1)S(1)}, bf16[128,256]{1,0:T(8,128)(2,1)S(1)}, u32[]{:S(2)}, u32[]{:S(2)}) collective-permute-start(bf16[128,256]{1,0:T(8,128)(2,1)S(1)} %get-tuple-element.85), channel_id=1, source_target_pairs={{0,12},{1,13},{2,14},{3,15},{4,8},{5,9},{6,10},{7,11},{8,4},{9,5},... | collective-permute-start | bytes 196616 | tf_op jit(solution)/shard_map/ppermute | solution.py:267
  67.2 10.8 %collective-permute-start.20 = (bf16[128,512]{1,0:T(8,128)(2,1)S(1)}, bf16[128,512]{1,0:T(8,128)(2,1)S(1)}, u32[]{:S(2)}, u32[]{:S(2)}) collective-permute-start(bf16[128,512]{1,0:T(8,128)(2,1)S(1)} %get-tuple-element.83), channel_id=1, source_target_pairs={{0,4},{1,5},{2,6},{3,7},{4,0},{5,1},{6,2},{7,3},{8,12},{9,13},{10,... | collective-permute-start | bytes 393224 | tf_op jit(solution)/shard_map/ppermute | solution.py:267
  67.2 10.8 %collective-permute-start.21 = (bf16[128,512]{1,0:T(8,128)(2,1)S(1)}, bf16[128,512]{1,0:T(8,128)(2,1)S(1)}, u32[]{:S(2)}, u32[]{:S(2)}) collective-permute-start(bf16[128,512]{1,0:T(8,128)(2,1)S(1)} %get-tuple-element.84), channel_id=1, source_target_pairs={{0,8},{1,9},{2,10},{3,11},{4,12},{5,13},{6,14},{7,15},{8,0},{9,1},... | collective-permute-start | bytes 393224 | tf_op jit(solution)/shard_map/ppermute | solution.py:267
  73.6 7.8 %collective-permute-start.25 = (bf16[128,256]{1,0:T(8,128)(2,1)S(1)}, bf16[128,256]{1,0:T(8,128)(2,1)S(1)}, u32[]{:S(2)}, u32[]{:S(2)}) collective-permute-start(bf16[128,256]{1,0:T(8,128)(2,1)S(1)} %get-tuple-element.89), channel_id=1, source_target_pairs={{0,8},{1,9},{2,10},{3,11},{4,12},{5,13},{6,14},{7,15},{8,0},{9,1},... | collective-permute-start | bytes 196616 | tf_op jit(solution)/shard_map/ppermute | solution.py:267
  76.0 6.2 %collective-permute-start.26 = (bf16[128,256]{1,0:T(8,128)(2,1)S(1)}, bf16[128,256]{1,0:T(8,128)(2,1)S(1)}, u32[]{:S(2)}, u32[]{:S(2)}) collective-permute-start(bf16[128,256]{1,0:T(8,128)(2,1)S(1)} %get-tuple-element.90), channel_id=1, source_target_pairs={{0,12},{1,13},{2,14},{3,15},{4,8},{5,9},{6,10},{7,11},{8,4},{9,5},... | collective-permute-start | bytes 196616 | tf_op jit(solution)/shard_map/ppermute | solution.py:267
  (12 other events, 43.7 us)

commit v6 on v5

--- a/solution.py
+++ b/solution.py
@@ -17,7 +17,7 @@
 
 
 SMALL = pl.CostEstimate(flops=1, bytes_accessed=1, transcendentals=0)
-MID = pl.CostEstimate(flops=10**9, bytes_accessed=1, transcendentals=0)
+MID = pl.CostEstimate(flops=6 * 10**8, bytes_accessed=1, transcendentals=0)
 BIG = pl.CostEstimate(flops=2 * 10**10, bytes_accessed=1, transcendentals=0)
 
 
@@ -300,7 +300,7 @@
     own_core = swap(own_pair, 1)
     out = tick(release(z3, fast), [received1] + [in2[r] for r in fast], BIG)
     in3 = sent(fast, out)
-    received2, *out = tick([received_kv(in2)] + release(z3, slow), [out[0]], MID)
+    received2, *out = tick([received_kv(in2)] + release(z3, slow), [out[0], own_core], MID)
     in3.update(sent(slow, out))
     (pair1,) = tick([(0, [other1, received1], None)], [received2], MID)
     other2, core1 = swap(received2, 2), swap(pair1, 1)

time: 83.5 us -> 83.4 us (level)
  starting transfers between devices: 39.9 us -> 46.4 us
  waiting for transfers between devices: 21.3 us -> 14.8 us
    ppermute x27, waiting for transfers between devices: 21.3 us -> 14.8 us  [swap(): return lax.ppermute(array, 'seq', [(i, i ^ distance) for i in range(size)])]
    ppermute x27, starting transfers between devices: 39.9 us -> 46.4 us  [swap(): return lax.ppermute(array, 'seq', [(i, i ^ distance) for i in range(size)])]
  transfers between devices with their start and end apart: 27 -> 27, of which waited for: 9 -> 5; matrix products, arithmetic and copies ran while one was open for 0% -> 0% of each run, Pallas kernels for 17% -> 17%
where the time goes in v6:
time: 83.4 us; the launch traced here: 83.2 us
  starting transfers between devices  46.4 us (56%)
  Pallas kernels  15.1 us (18%)
  waiting for transfers between devices  14.8 us (18%)
  local copies, waits for them, and re-layouts  5.85 us (7%)
  between operations  0.89 us (1%)
    ppermute x27, starting transfers between devices, swap(): return lax.ppermute(array, 'seq', [(i, i ^ distance) for i in range(size)])  46.4 us
    ppermute x27, waiting for transfers between devices, swap(): return lax.ppermute(array, 'seq', [(i, i ^ distance) for i in range(size)])  14.8 us
    pallas_call x3, Pallas kernels, attend_pair(): pl.pallas_call(functools.partial(attend_kernel, n_q, q_block * HEAD_DIM,...  11.4 us
    unnamed x18, local copies, waits for them, and re-layouts  5.85 us
    pallas_call x1, Pallas kernels, sum_deltas(): pl.pallas_call(deltas_kernel, grid=(4,), in_specs=[pl.BlockSpec(memory_sp...  1.88 us
  transfers between devices with their start and end apart: 27, of which 5 were waited for; matrix products, arithmetic and copies ran while one was open for 0% of the time, Pallas kernels for 17%

profile of v6, /device:TPU:0, one launch (start us, length us, event | category | flops | bytes accessed | tf_op | source)
XLA Modules:
  0.0 83.2 jit_solution(6781254342872022444)
XLA Ops:
  2.4 5.1 %collective-permute-start = (bf16[128,512]{1,0:T(8,128)(2,1)S(1)}, bf16[128,512]{1,0:T(8,128)(2,1)S(1)}, u32[]{:S(2)}, u32[]{:S(2)}) collective-permute-start(bf16[128,512]{1,0:T(8,128)(2,1)S(1)} %get-tuple-element.51.refs_6_), channel_id=1, source_target_pairs={{0,12},{1,13},{2,14},{3,15},{4,8},{5,9},{6,10},{7,11},{8,4},{9,5},... | collective-permute-start | bytes 393224 | tf_op jit(solution)/shard_map/ppermute | solution.py:267
  8.1 1.7 %collective-permute-start.4 = (bf16[128,1536]{1,0:T(8,128)(2,1)S(1)}, bf16[128,1536]{1,0:T(8,128)(2,1)S(1)}, u32[]{:S(2)}, u32[]{:S(2)}) collective-permute-start(bf16[128,1536]{1,0:T(8,128)(2,1)S(1)} %get-tuple-element.59.refs_1_.refs_5_), channel_id=1, source_target_pairs={{0,2},{1,3},{2,0},{3,1},{4,6},{5,7},{6,4},{7,5},{8,10},{9,11},{10,... | collective-permute-start | bytes 1179656 | tf_op jit(solution)/shard_map/ppermute | solution.py:267
  9.8 1.1 %copy-done.7 = bf16[128,3072]{1,0:T(8,128)(2,1)S(1)} copy-done((bf16[128,3072]{1,0:T(8,128)(2,1)S(1)}, bf16[128,3072]{1,0:T(8,128)(2,1)}, u32[]{:S(2)}) %copy-start.7) | copy-done | bytes 786456
  11.2 1.5 %copy-done.6 = bf16[256,3072]{1,0:T(8,128)(2,1)S(1)} copy-done((bf16[256,3072]{1,0:T(8,128)(2,1)S(1)}, bf16[256,3072]{1,0:T(8,128)(2,1)}, u32[]{:S(2)}) %copy-start.6) | copy-done | bytes 1572888
  13.8 1.9 %deltas.2.refs_0_.added = f32[128,3072]{1,0:T(8,128)S(1)} custom-call(s32[6]{0:T(128)S(1)} %copy-done.8, bf16[6,128,3072]{2,1,0:T(8,128)(2,1)S(1)} %copy-done, bf16[256,1536]{1,0:T(8,128)(2,1)S(1)} %own_text.1.refs_0_.refs_9_), custom_call_target="tpu_custom_call" | custom-call | flops 1 | bytes 1 | tf_op jit(solution)/shard_map/deltas/pallas_call | solution.py:217
  15.7 3.7 %collective-permute-start.3 = (bf16[128,512]{1,0:T(8,128)(2,1)S(1)}, bf16[128,512]{1,0:T(8,128)(2,1)S(1)}, u32[]{:S(2)}, u32[]{:S(2)}) collective-permute-start(bf16[128,512]{1,0:T(8,128)(2,1)S(1)} %tick.10.refs_0_), channel_id=1, source_target_pairs={{0,12},{1,13},{2,14},{3,15},{4,8},{5,9},{6,10},{7,11},{8,4},{9,5},... | collective-permute-start | bytes 393224 | tf_op jit(solution)/shard_map/ppermute | solution.py:267
  19.5 2.9 %collective-permute-start.7 = (bf16[128,512]{1,0:T(8,128)(2,1)S(1)}, bf16[128,512]{1,0:T(8,128)(2,1)S(1)}, u32[]{:S(2)}, u32[]{:S(2)}) collective-permute-start(bf16[128,512]{1,0:T(8,128)(2,1)S(1)} %get-tuple-element.61), channel_id=1, source_target_pairs={{0,8},{1,9},{2,10},{3,11},{4,12},{5,13},{6,14},{7,15},{8,0},{9,1},... | collective-permute-start | bytes 393224 | tf_op jit(solution)/shard_map/ppermute | solution.py:267
  22.3 3.0 %collective-permute-start.11 = (bf16[384,512]{1,0:T(8,128)(2,1)S(1)}, bf16[384,512]{1,0:T(8,128)(2,1)S(1)}, u32[]{:S(2)}, u32[]{:S(2)}) collective-permute-start(bf16[384,512]{1,0:T(8,128)(2,1)S(1)} %get-tuple-element.57.refs_0_.refs_2_), channel_id=1, source_target_pairs={{0,2},{1,3},{2,0},{3,1},{4,6},{5,7},{6,4},{7,5},{8,10},{9,11},{10,... | collective-permute-start | bytes 1179656 | tf_op jit(solution)/shard_map/ppermute | solution.py:267
  25.5 3.1 %collective-permute-start.10 = (bf16[128,768]{1,0:T(8,128)(2,1)S(1)}, bf16[128,768]{1,0:T(8,128)(2,1)S(1)}, u32[]{:S(2)}, u32[]{:S(2)}) collective-permute-start(bf16[128,768]{1,0:T(8,128)(2,1)S(1)} %tick.12.refs_0_), channel_id=1, source_target_pairs={{0,12},{1,13},{2,14},{3,15},{4,8},{5,9},{6,10},{7,11},{8,4},{9,5},... | collective-permute-start | bytes 589832 | tf_op jit(solution)/shard_map/ppermute | solution.py:267
  30.6 3.4 %collective-permute-start.9 = (bf16[128,768]{1,0:T(8,128)(2,1)S(1)}, bf16[128,768]{1,0:T(8,128)(2,1)S(1)}, u32[]{:S(2)}, u32[]{:S(2)}) collective-permute-start(bf16[128,768]{1,0:T(8,128)(2,1)S(1)} %get-tuple-element.65), channel_id=1, source_target_pairs={{0,8},{1,9},{2,10},{3,11},{4,12},{5,13},{6,14},{7,15},{8,0},{9,1},... | collective-permute-start | bytes 589832 | tf_op jit(solution)/shard_map/ppermute | solution.py:267
  34.0 5.4 %collective-permute-start.13 = (bf16[384,512]{1,0:T(8,128)(2,1)S(1)}, bf16[384,512]{1,0:T(8,128)(2,1)S(1)}, u32[]{:S(2)}, u32[]{:S(2)}) collective-permute-start(bf16[384,512]{1,0:T(8,128)(2,1)S(1)} %get-tuple-element.66.refs_0_.refs_2_), channel_id=1, source_target_pairs={{0,2},{1,3},{2,0},{3,1},{4,6},{5,7},{6,4},{7,5},{8,10},{9,11},{10,... | collective-permute-start | bytes 1179656 | tf_op jit(solution)/shard_map/ppermute | solution.py:267
  39.6 1.7 %collective-permute-start.14 = (bf16[128,512]{1,0:T(8,128)(2,1)S(1)}, bf16[128,512]{1,0:T(8,128)(2,1)S(1)}, u32[]{:S(2)}, u32[]{:S(2)}) collective-permute-start(bf16[128,512]{1,0:T(8,128)(2,1)S(1)} %tick.16.refs_0_), channel_id=1, source_target_pairs={{0,12},{1,13},{2,14},{3,15},{4,8},{5,9},{6,10},{7,11},{8,4},{9,5},... | collective-permute-start | bytes 393224 | tf_op jit(solution)/shard_map/ppermute | solution.py:267
  41.3 8.7 %collective-permute-done.9.refs_4_.refs_2_ = bf16[128,768]{1,0:T(8,128)(2,1)S(1)} collective-permute-done((bf16[128,768]{1,0:T(8,128)(2,1)S(1)}, bf16[128,768]{1,0:T(8,128)(2,1)S(1)}, u32[]{:S(2)}, u32[]{:S(2)}) %collective-permute-start.9) | collective-permute-done | bytes 196640 | tf_op jit(solution)/shard_map/ppermute | solution.py:267
  50.3 3.4 %collective-permute-start.18 = (bf16[128,512]{1,0:T(8,128)(2,1)S(1)}, bf16[128,512]{1,0:T(8,128)(2,1)S(1)}, u32[]{:S(2)}, u32[]{:S(2)}) collective-permute-start(bf16[128,512]{1,0:T(8,128)(2,1)S(1)} %get-tuple-element.75), channel_id=1, source_target_pairs={{0,8},{1,9},{2,10},{3,11},{4,12},{5,13},{6,14},{7,15},{8,0},{9,1},... | collective-permute-start | bytes 393224 | tf_op jit(solution)/shard_map/ppermute | solution.py:267
  53.7 1.2 %collective-permute-start.16 = (bf16[384,512]{1,0:T(8,128)(2,1)S(1)}, bf16[384,512]{1,0:T(8,128)(2,1)S(1)}, u32[]{:S(2)}, u32[]{:S(2)}) collective-permute-start(bf16[384,512]{1,0:T(8,128)(2,1)S(1)} %get-tuple-element.70.refs_0_.refs_10_.refs_2_), channel_id=1, source_target_pairs={{0,2},{1,3},{2,0},{3,1},{4,6},{5,7},{6,4},{7,5},{8,10},{9,11},{10,... | collective-permute-start | bytes 1179656 | tf_op jit(solution)/shard_map/ppermute | solution.py:267
  55.0 3.7 %attend.3 = (bf16[128,256]{1,0:T(8,128)(2,1)S(1)}, bf16[128,256]{1,0:T(8,128)(2,1)S(1)}, bf16[128,256]{1,0:T(8,128)(2,1)S(1)}, bf16[128,256]{1,0:T(8,128)(2,1)S(1)}) custom-call(s32[2]{0:T(128)S(1)} %pad_add_fusion.scalars, bf16[128,768]{1,0:T(8,128)(2,1)S(1)} %get-tuple-element.53.refs_0_, bf16[128,768]{1,0:T(8,128)(2,1)S(1)} %collective-permute-done.8.refs_3_.refs_1_, ...), custom_call_target="tpu_custom_call" | custom-call | flops 20000000000 | bytes 1 | tf_op jit(solution)/shard_map/attend/pallas_call | solution.py:169
  58.7 1.7 %collective-permute-start.15 = (bf16[128,256]{1,0:T(8,128)(2,1)S(1)}, bf16[128,256]{1,0:T(8,128)(2,1)S(1)}, u32[]{:S(2)}, u32[]{:S(2)}) collective-permute-start(bf16[128,256]{1,0:T(8,128)(2,1)S(1)} %get-tuple-element.71), channel_id=1, source_target_pairs={{0,12},{1,13},{2,14},{3,15},{4,8},{5,9},{6,10},{7,11},{8,4},{9,5},... | collective-permute-start | bytes 196616 | tf_op jit(solution)/shard_map/ppermute | solution.py:267
  60.4 3.8 %attend.4 = (bf16[128,256]{1,0:T(8,128)(2,1)S(1)}, bf16[128,256]{1,0:T(8,128)(2,1)S(1)}, bf16[128,256]{1,0:T(8,128)(2,1)S(1)}, bf16[128,256]{1,0:T(8,128)(2,1)S(1)}) custom-call(s32[2]{0:T(128)S(1)} %pad_add_fusion.scalars, bf16[128,512]{1,0:T(8,128)(2,1)S(1)} %get-tuple-element.73.refs_0_, bf16[128,512]{1,0:T(8,128)(2,1)S(1)} %collective-permute-done.17.refs_1_, ...), custom_call_target="tpu_custom_call" | custom-call | flops 20000000000 | bytes 1 | tf_op jit(solution)/shard_map/attend/pallas_call | solution.py:169
  65.2 1.7 %collective-permute-start.22 = (bf16[128,256]{1,0:T(8,128)(2,1)S(1)}, bf16[128,256]{1,0:T(8,128)(2,1)S(1)}, u32[]{:S(2)}, u32[]{:S(2)}) collective-permute-start(bf16[128,256]{1,0:T(8,128)(2,1)S(1)} %get-tuple-element.85), channel_id=1, source_target_pairs={{0,12},{1,13},{2,14},{3,15},{4,8},{5,9},{6,10},{7,11},{8,4},{9,5},... | collective-permute-start | bytes 196616 | tf_op jit(solution)/shard_map/ppermute | solution.py:267
  66.9 2.8 %collective-permute-start.21 = (bf16[128,512]{1,0:T(8,128)(2,1)S(1)}, bf16[128,512]{1,0:T(8,128)(2,1)S(1)}, u32[]{:S(2)}, u32[]{:S(2)}) collective-permute-start(bf16[128,512]{1,0:T(8,128)(2,1)S(1)} %get-tuple-element.84), channel_id=1, source_target_pairs={{0,8},{1,9},{2,10},{3,11},{4,12},{5,13},{6,14},{7,15},{8,0},{9,1},... | collective-permute-start | bytes 393224 | tf_op jit(solution)/shard_map/ppermute | solution.py:267
  69.7 3.8 %attend.5 = (bf16[128,256]{1,0:T(8,128)(2,1)S(1)}, bf16[128,256]{1,0:T(8,128)(2,1)S(1)}, bf16[128,256]{1,0:T(8,128)(2,1)S(1)}, bf16[128,256]{1,0:T(8,128)(2,1)S(1)}) custom-call(s32[2]{0:T(128)S(1)} %pad_add_fusion.scalars, bf16[128,512]{1,0:T(8,128)(2,1)S(1)} %get-tuple-element.73.refs_0_, bf16[128,512]{1,0:T(8,128)(2,1)S(1)} %collective-permute-done.17.refs_1_, ...), custom_call_target="tpu_custom_call" | custom-call | flops 20000000000 | bytes 1 | tf_op jit(solution)/shard_map/attend/pallas_call | solution.py:169
  73.6 2.2 %collective-permute-start.25 = (bf16[128,256]{1,0:T(8,128)(2,1)S(1)}, bf16[128,256]{1,0:T(8,128)(2,1)S(1)}, u32[]{:S(2)}, u32[]{:S(2)}) collective-permute-start(bf16[128,256]{1,0:T(8,128)(2,1)S(1)} %get-tuple-element.89), channel_id=1, source_target_pairs={{0,8},{1,9},{2,10},{3,11},{4,12},{5,13},{6,14},{7,15},{8,0},{9,1},... | collective-permute-start | bytes 196616 | tf_op jit(solution)/shard_map/ppermute | solution.py:267
  75.8 2.2 %collective-permute-start.26 = (bf16[128,256]{1,0:T(8,128)(2,1)S(1)}, bf16[128,256]{1,0:T(8,128)(2,1)S(1)}, u32[]{:S(2)}, u32[]{:S(2)}) collective-permute-start(bf16[128,256]{1,0:T(8,128)(2,1)S(1)} %get-tuple-element.90), channel_id=1, source_target_pairs={{0,12},{1,13},{2,14},{3,15},{4,8},{5,9},{6,10},{7,11},{8,4},{9,5},... | collective-permute-start | bytes 196616 | tf_op jit(solution)/shard_map/ppermute | solution.py:267
  79.0 3.1 %collective-permute-done.25.refs_7_ = bf16[128,256]{1,0:T(8,128)(2,1)S(1)} collective-permute-done((bf16[128,256]{1,0:T(8,128)(2,1)S(1)}, bf16[128,256]{1,0:T(8,128)(2,1)S(1)}, u32[]{:S(2)}, u32[]{:S(2)}) %collective-permute-start.25) | collective-permute-done | bytes 65568 | tf_op jit(solution)/shard_map/ppermute | solution.py:267
  (67 shorter events, 9.6 us)
Async XLA Ops:
  2.4 13.3 %collective-permute-start = (bf16[128,512]{1,0:T(8,128)(2,1)S(1)}, bf16[128,512]{1,0:T(8,128)(2,1)S(1)}, u32[]{:S(2)}, u32[]{:S(2)}) collective-permute-start(bf16[128,512]{1,0:T(8,128)(2,1)S(1)} %get-tuple-element.51.refs_6_), channel_id=1, source_target_pairs={{0,12},{1,13},{2,14},{3,15},{4,8},{5,9},{6,10},{7,11},{8,4},{9,5},... | collective-permute-start | bytes 393224 | tf_op jit(solution)/shard_map/ppermute | solution.py:267
  7.5 11.8 %collective-permute-start.1 = (bf16[128,512]{1,0:T(8,128)(2,1)S(1)}, bf16[128,512]{1,0:T(8,128)(2,1)S(1)}, u32[]{:S(2)}, u32[]{:S(2)}) collective-permute-start(bf16[128,512]{1,0:T(8,128)(2,1)S(1)} %get-tuple-element.49.refs_4_), channel_id=1, source_target_pairs={{0,4},{1,5},{2,6},{3,7},{4,0},{5,1},{6,2},{7,3},{8,12},{9,13},{10,... | collective-permute-start | bytes 393224 | tf_op jit(solution)/shard_map/ppermute | solution.py:267
  7.5 11.8 %collective-permute-start.2 = (bf16[128,512]{1,0:T(8,128)(2,1)S(1)}, bf16[128,512]{1,0:T(8,128)(2,1)S(1)}, u32[]{:S(2)}, u32[]{:S(2)}) collective-permute-start(bf16[128,512]{1,0:T(8,128)(2,1)S(1)} %get-tuple-element.50.refs_5_), channel_id=1, source_target_pairs={{0,8},{1,9},{2,10},{3,11},{4,12},{5,13},{6,14},{7,15},{8,0},{9,1},... | collective-permute-start | bytes 393224 | tf_op jit(solution)/shard_map/ppermute | solution.py:267
  8.1 17.2 %collective-permute-start.4 = (bf16[128,1536]{1,0:T(8,128)(2,1)S(1)}, bf16[128,1536]{1,0:T(8,128)(2,1)S(1)}, u32[]{:S(2)}, u32[]{:S(2)}) collective-permute-start(bf16[128,1536]{1,0:T(8,128)(2,1)S(1)} %get-tuple-element.59.refs_1_.refs_5_), channel_id=1, source_target_pairs={{0,2},{1,3},{2,0},{3,1},{4,6},{5,7},{6,4},{7,5},{8,10},{9,11},{10,... | collective-permute-start | bytes 1179656 | tf_op jit(solution)/shard_map/ppermute | solution.py:267
  15.7 9.8 %collective-permute-start.3 = (bf16[128,512]{1,0:T(8,128)(2,1)S(1)}, bf16[128,512]{1,0:T(8,128)(2,1)S(1)}, u32[]{:S(2)}, u32[]{:S(2)}) collective-permute-start(bf16[128,512]{1,0:T(8,128)(2,1)S(1)} %tick.10.refs_0_), channel_id=1, source_target_pairs={{0,12},{1,13},{2,14},{3,15},{4,8},{5,9},{6,10},{7,11},{8,4},{9,5},... | collective-permute-start | bytes 393224 | tf_op jit(solution)/shard_map/ppermute | solution.py:267
  19.4 9.9 %collective-permute-start.6 = (bf16[128,512]{1,0:T(8,128)(2,1)S(1)}, bf16[128,512]{1,0:T(8,128)(2,1)S(1)}, u32[]{:S(2)}, u32[]{:S(2)}) collective-permute-start(bf16[128,512]{1,0:T(8,128)(2,1)S(1)} %get-tuple-element.60), channel_id=1, source_target_pairs={{0,4},{1,5},{2,6},{3,7},{4,0},{5,1},{6,2},{7,3},{8,12},{9,13},{10,... | collective-permute-start | bytes 393224 | tf_op jit(solution)/shard_map/ppermute | solution.py:267
  19.5 10.9 %collective-permute-start.7 = (bf16[128,512]{1,0:T(8,128)(2,1)S(1)}, bf16[128,512]{1,0:T(8,128)(2,1)S(1)}, u32[]{:S(2)}, u32[]{:S(2)}) collective-permute-start(bf16[128,512]{1,0:T(8,128)(2,1)S(1)} %get-tuple-element.61), channel_id=1, source_target_pairs={{0,8},{1,9},{2,10},{3,11},{4,12},{5,13},{6,14},{7,15},{8,0},{9,1},... | collective-permute-start | bytes 393224 | tf_op jit(solution)/shard_map/ppermute | solution.py:267
  22.3 17.1 %collective-permute-start.11 = (bf16[384,512]{1,0:T(8,128)(2,1)S(1)}, bf16[384,512]{1,0:T(8,128)(2,1)S(1)}, u32[]{:S(2)}, u32[]{:S(2)}) collective-permute-start(bf16[384,512]{1,0:T(8,128)(2,1)S(1)} %get-tuple-element.57.refs_0_.refs_2_), channel_id=1, source_target_pairs={{0,2},{1,3},{2,0},{3,1},{4,6},{5,7},{6,4},{7,5},{8,10},{9,11},{10,... | collective-permute-start | bytes 1179656 | tf_op jit(solution)/shard_map/ppermute | solution.py:267
  25.5 14.0 %collective-permute-start.10 = (bf16[128,768]{1,0:T(8,128)(2,1)S(1)}, bf16[128,768]{1,0:T(8,128)(2,1)S(1)}, u32[]{:S(2)}, u32[]{:S(2)}) collective-permute-start(bf16[128,768]{1,0:T(8,128)(2,1)S(1)} %tick.12.refs_0_), channel_id=1, source_target_pairs={{0,12},{1,13},{2,14},{3,15},{4,8},{5,9},{6,10},{7,11},{8,4},{9,5},... | collective-permute-start | bytes 589832 | tf_op jit(solution)/shard_map/ppermute | solution.py:267
  30.4 10.9 %collective-permute-start.8 = (bf16[128,768]{1,0:T(8,128)(2,1)S(1)}, bf16[128,768]{1,0:T(8,128)(2,1)S(1)}, u32[]{:S(2)}, u32[]{:S(2)}) collective-permute-start(bf16[128,768]{1,0:T(8,128)(2,1)S(1)} %get-tuple-element.64), channel_id=1, source_target_pairs={{0,4},{1,5},{2,6},{3,7},{4,0},{5,1},{6,2},{7,3},{8,12},{9,13},{10,... | collective-permute-start | bytes 589832 | tf_op jit(solution)/shard_map/ppermute | solution.py:267
  30.6 19.4 %collective-permute-start.9 = (bf16[128,768]{1,0:T(8,128)(2,1)S(1)}, bf16[128,768]{1,0:T(8,128)(2,1)S(1)}, u32[]{:S(2)}, u32[]{:S(2)}) collective-permute-start(bf16[128,768]{1,0:T(8,128)(2,1)S(1)} %get-tuple-element.65), channel_id=1, source_target_pairs={{0,8},{1,9},{2,10},{3,11},{4,12},{5,13},{6,14},{7,15},{8,0},{9,1},... | collective-permute-start | bytes 589832 | tf_op jit(solution)/shard_map/ppermute | solution.py:267
  34.0 20.8 %collective-permute-start.13 = (bf16[384,512]{1,0:T(8,128)(2,1)S(1)}, bf16[384,512]{1,0:T(8,128)(2,1)S(1)}, u32[]{:S(2)}, u32[]{:S(2)}) collective-permute-start(bf16[384,512]{1,0:T(8,128)(2,1)S(1)} %get-tuple-element.66.refs_0_.refs_2_), channel_id=1, source_target_pairs={{0,2},{1,3},{2,0},{3,1},{4,6},{5,7},{6,4},{7,5},{8,10},{9,11},{10,... | collective-permute-start | bytes 1179656 | tf_op jit(solution)/shard_map/ppermute | solution.py:267
  39.5 10.6 %collective-permute-start.12 = (bf16[768,512]{1,0:T(8,128)(2,1)S(1)}, bf16[768,512]{1,0:T(8,128)(2,1)S(1)}, u32[]{:S(2)}, u32[]{:S(2)}) collective-permute-start(bf16[768,512]{1,0:T(8,128)(2,1)S(1)} %tick.15.refs_4_), channel_id=1, source_target_pairs={{0,1},{1,0},{2,3},{3,2},{4,5},{5,4},{6,7},{7,6},{8,9},{9,8},{10,11... | collective-permute-start | bytes 2359304 | tf_op jit(solution)/shard_map/ppermute | solution.py:267
  39.6 15.4 %collective-permute-start.14 = (bf16[128,512]{1,0:T(8,128)(2,1)S(1)}, bf16[128,512]{1,0:T(8,128)(2,1)S(1)}, u32[]{:S(2)}, u32[]{:S(2)}) collective-permute-start(bf16[128,512]{1,0:T(8,128)(2,1)S(1)} %tick.16.refs_0_), channel_id=1, source_target_pairs={{0,12},{1,13},{2,14},{3,15},{4,8},{5,9},{6,10},{7,11},{8,4},{9,5},... | collective-permute-start | bytes 393224 | tf_op jit(solution)/shard_map/ppermute | solution.py:267
  50.1 10.3 %collective-permute-start.17 = (bf16[128,512]{1,0:T(8,128)(2,1)S(1)}, bf16[128,512]{1,0:T(8,128)(2,1)S(1)}, u32[]{:S(2)}, u32[]{:S(2)}) collective-permute-start(bf16[128,512]{1,0:T(8,128)(2,1)S(1)} %get-tuple-element.74), channel_id=1, source_target_pairs={{0,4},{1,5},{2,6},{3,7},{4,0},{5,1},{6,2},{7,3},{8,12},{9,13},{10,... | collective-permute-start | bytes 393224 | tf_op jit(solution)/shard_map/ppermute | solution.py:267
  50.3 10.1 %collective-permute-start.18 = (bf16[128,512]{1,0:T(8,128)(2,1)S(1)}, bf16[128,512]{1,0:T(8,128)(2,1)S(1)}, u32[]{:S(2)}, u32[]{:S(2)}) collective-permute-start(bf16[128,512]{1,0:T(8,128)(2,1)S(1)} %get-tuple-element.75), channel_id=1, source_target_pairs={{0,8},{1,9},{2,10},{3,11},{4,12},{5,13},{6,14},{7,15},{8,0},{9,1},... | collective-permute-start | bytes 393224 | tf_op jit(solution)/shard_map/ppermute | solution.py:267
  53.7 11.4 %collective-permute-start.16 = (bf16[384,512]{1,0:T(8,128)(2,1)S(1)}, bf16[384,512]{1,0:T(8,128)(2,1)S(1)}, u32[]{:S(2)}, u32[]{:S(2)}) collective-permute-start(bf16[384,512]{1,0:T(8,128)(2,1)S(1)} %get-tuple-element.70.refs_0_.refs_10_.refs_2_), channel_id=1, source_target_pairs={{0,2},{1,3},{2,0},{3,1},{4,6},{5,7},{6,4},{7,5},{8,10},{9,11},{10,... | collective-permute-start | bytes 1179656 | tf_op jit(solution)/shard_map/ppermute | solution.py:267
  54.9 5.5 %collective-permute-start.19 = (bf16[768,512]{1,0:T(8,128)(2,1)S(1)}, bf16[768,512]{1,0:T(8,128)(2,1)S(1)}, u32[]{:S(2)}, u32[]{:S(2)}) collective-permute-start(bf16[768,512]{1,0:T(8,128)(2,1)S(1)} %tick.18.refs_11_.refs_4_), channel_id=1, source_target_pairs={{0,1},{1,0},{2,3},{3,2},{4,5},{5,4},{6,7},{7,6},{8,9},{9,8},{10,11... | collective-permute-start | bytes 2359304 | tf_op jit(solution)/shard_map/ppermute | solution.py:267
  58.7 6.3 %collective-permute-start.15 = (bf16[128,256]{1,0:T(8,128)(2,1)S(1)}, bf16[128,256]{1,0:T(8,128)(2,1)S(1)}, u32[]{:S(2)}, u32[]{:S(2)}) collective-permute-start(bf16[128,256]{1,0:T(8,128)(2,1)S(1)} %get-tuple-element.71), channel_id=1, source_target_pairs={{0,12},{1,13},{2,14},{3,15},{4,8},{5,9},{6,10},{7,11},{8,4},{9,5},... | collective-permute-start | bytes 196616 | tf_op jit(solution)/shard_map/ppermute | solution.py:267
  65.2 10.6 %collective-permute-start.22 = (bf16[128,256]{1,0:T(8,128)(2,1)S(1)}, bf16[128,256]{1,0:T(8,128)(2,1)S(1)}, u32[]{:S(2)}, u32[]{:S(2)}) collective-permute-start(bf16[128,256]{1,0:T(8,128)(2,1)S(1)} %get-tuple-element.85), channel_id=1, source_target_pairs={{0,12},{1,13},{2,14},{3,15},{4,8},{5,9},{6,10},{7,11},{8,4},{9,5},... | collective-permute-start | bytes 196616 | tf_op jit(solution)/shard_map/ppermute | solution.py:267
  66.9 11.1 %collective-permute-start.20 = (bf16[128,512]{1,0:T(8,128)(2,1)S(1)}, bf16[128,512]{1,0:T(8,128)(2,1)S(1)}, u32[]{:S(2)}, u32[]{:S(2)}) collective-permute-start(bf16[128,512]{1,0:T(8,128)(2,1)S(1)} %get-tuple-element.83), channel_id=1, source_target_pairs={{0,4},{1,5},{2,6},{3,7},{4,0},{5,1},{6,2},{7,3},{8,12},{9,13},{10,... | collective-permute-start | bytes 393224 | tf_op jit(solution)/shard_map/ppermute | solution.py:267
  66.9 11.1 %collective-permute-start.21 = (bf16[128,512]{1,0:T(8,128)(2,1)S(1)}, bf16[128,512]{1,0:T(8,128)(2,1)S(1)}, u32[]{:S(2)}, u32[]{:S(2)}) collective-permute-start(bf16[128,512]{1,0:T(8,128)(2,1)S(1)} %get-tuple-element.84), channel_id=1, source_target_pairs={{0,8},{1,9},{2,10},{3,11},{4,12},{5,13},{6,14},{7,15},{8,0},{9,1},... | collective-permute-start | bytes 393224 | tf_op jit(solution)/shard_map/ppermute | solution.py:267
  73.6 8.5 %collective-permute-start.25 = (bf16[128,256]{1,0:T(8,128)(2,1)S(1)}, bf16[128,256]{1,0:T(8,128)(2,1)S(1)}, u32[]{:S(2)}, u32[]{:S(2)}) collective-permute-start(bf16[128,256]{1,0:T(8,128)(2,1)S(1)} %get-tuple-element.89), channel_id=1, source_target_pairs={{0,8},{1,9},{2,10},{3,11},{4,12},{5,13},{6,14},{7,15},{8,0},{9,1},... | collective-permute-start | bytes 196616 | tf_op jit(solution)/shard_map/ppermute | solution.py:267
  75.8 6.3 %collective-permute-start.26 = (bf16[128,256]{1,0:T(8,128)(2,1)S(1)}, bf16[128,256]{1,0:T(8,128)(2,1)S(1)}, u32[]{:S(2)}, u32[]{:S(2)}) collective-permute-start(bf16[128,256]{1,0:T(8,128)(2,1)S(1)} %get-tuple-element.90), channel_id=1, source_target_pairs={{0,12},{1,13},{2,14},{3,15},{4,8},{5,9},{6,10},{7,11},{8,4},{9,5},... | collective-permute-start | bytes 196616 | tf_op jit(solution)/shard_map/ppermute | solution.py:267
  (12 other events, 47.7 us)

commit v7 on v6

--- a/solution.py
+++ b/solution.py
@@ -318,7 +318,7 @@
         return attend_pair(scalars, pieces, block, [near, far, [(text, at, at + PAIR)]], earlier)
 
     context1 = heads(0, whole(z3, in3), 4, pair1, core1, [received3, pair2] + [in4[r] for r in fast])
-    early = (3,)
+    early = (2,)
     returned = [(send(context1[r], r), r, (0,)) for r in early]
     context2 = heads(1, whole(z4, in4), 0, pair2, core2, [context1[0]])
     late = [r for r in range(planes) if r not in early]
@@ -326,7 +326,7 @@
         [(0, [other3, received3], None)]
         + [(1, [context1[r], context2[r]], None) for r in late]
         + [(0, [context2[r]], None) for r in early],
-        [array for array, _, _ in returned],
+        [],
         MID,
     )
     core3 = swap(pair3, 1)

time: 83.4 us -> 83.2 us (level)
  no operation moved by 1% of the time
where the time goes in v7:
time: 83.2 us; the launch traced here: 83 us
  starting transfers between devices  45.6 us (55%)
  waiting for transfers between devices  15.4 us (19%)
  Pallas kernels  15.1 us (18%)
  local copies, waits for them, and re-layouts  5.85 us (7%)
  between operations  0.91 us (1%)
    ppermute x27, starting transfers between devices, swap(): return lax.ppermute(array, 'seq', [(i, i ^ distance) for i in range(size)])  45.6 us
    ppermute x27, waiting for transfers between devices, swap(): return lax.ppermute(array, 'seq', [(i, i ^ distance) for i in range(size)])  15.4 us
    pallas_call x3, Pallas kernels, attend_pair(): pl.pallas_call(functools.partial(attend_kernel, n_q, q_block * HEAD_DIM,...  11.4 us
    unnamed x18, local copies, waits for them, and re-layouts  5.85 us
    pallas_call x1, Pallas kernels, sum_deltas(): pl.pallas_call(deltas_kernel, grid=(4,), in_specs=[pl.BlockSpec(memory_sp...  1.88 us
  transfers between devices with their start and end apart: 27, of which 5 were waited for; matrix products, arithmetic and copies ran while one was open for 0% of the time, Pallas kernels for 17%

profile of v7, /device:TPU:0, one launch (start us, length us, event | category | flops | bytes accessed | tf_op | source)
XLA Modules:
  0.0 83.0 jit_solution(1656689450745473919)
XLA Ops:
  0.0 1.1 %copy-done.1 = bf16[128,3072]{1,0:T(8,128)(2,1)S(1)} copy-done((bf16[128,3072]{1,0:T(8,128)(2,1)S(1)}, bf16[128,3072]{1,0:T(8,128)(2,1)}, u32[]{:S(2)}) %copy-start.1) | copy-done | bytes 786456
  2.4 5.1 %collective-permute-start = (bf16[128,512]{1,0:T(8,128)(2,1)S(1)}, bf16[128,512]{1,0:T(8,128)(2,1)S(1)}, u32[]{:S(2)}, u32[]{:S(2)}) collective-permute-start(bf16[128,512]{1,0:T(8,128)(2,1)S(1)} %get-tuple-element.51.refs_6_), channel_id=1, source_target_pairs={{0,12},{1,13},{2,14},{3,15},{4,8},{5,9},{6,10},{7,11},{8,4},{9,5},... | collective-permute-start | bytes 393224 | tf_op jit(solution)/shard_map/ppermute | solution.py:267
  8.1 1.7 %collective-permute-start.4 = (bf16[128,1536]{1,0:T(8,128)(2,1)S(1)}, bf16[128,1536]{1,0:T(8,128)(2,1)S(1)}, u32[]{:S(2)}, u32[]{:S(2)}) collective-permute-start(bf16[128,1536]{1,0:T(8,128)(2,1)S(1)} %get-tuple-element.59.refs_1_.refs_5_), channel_id=1, source_target_pairs={{0,2},{1,3},{2,0},{3,1},{4,6},{5,7},{6,4},{7,5},{8,10},{9,11},{10,... | collective-permute-start | bytes 1179656 | tf_op jit(solution)/shard_map/ppermute | solution.py:267
  9.8 1.1 %copy-done.7 = bf16[128,3072]{1,0:T(8,128)(2,1)S(1)} copy-done((bf16[128,3072]{1,0:T(8,128)(2,1)S(1)}, bf16[128,3072]{1,0:T(8,128)(2,1)}, u32[]{:S(2)}) %copy-start.7) | copy-done | bytes 786456
  11.2 1.5 %copy-done.6 = bf16[256,3072]{1,0:T(8,128)(2,1)S(1)} copy-done((bf16[256,3072]{1,0:T(8,128)(2,1)S(1)}, bf16[256,3072]{1,0:T(8,128)(2,1)}, u32[]{:S(2)}) %copy-start.6) | copy-done | bytes 1572888
  13.8 1.9 %deltas.2.refs_0_.added = f32[128,3072]{1,0:T(8,128)S(1)} custom-call(s32[6]{0:T(128)S(1)} %copy-done.8, bf16[6,128,3072]{2,1,0:T(8,128)(2,1)S(1)} %copy-done, bf16[256,1536]{1,0:T(8,128)(2,1)S(1)} %own_text.1.refs_0_.refs_9_), custom_call_target="tpu_custom_call" | custom-call | flops 1 | bytes 1 | tf_op jit(solution)/shard_map/deltas/pallas_call | solution.py:217
  15.7 3.7 %collective-permute-start.3 = (bf16[128,512]{1,0:T(8,128)(2,1)S(1)}, bf16[128,512]{1,0:T(8,128)(2,1)S(1)}, u32[]{:S(2)}, u32[]{:S(2)}) collective-permute-start(bf16[128,512]{1,0:T(8,128)(2,1)S(1)} %tick.10.refs_0_), channel_id=1, source_target_pairs={{0,12},{1,13},{2,14},{3,15},{4,8},{5,9},{6,10},{7,11},{8,4},{9,5},... | collective-permute-start | bytes 393224 | tf_op jit(solution)/shard_map/ppermute | solution.py:267
  19.5 2.9 %collective-permute-start.7 = (bf16[128,512]{1,0:T(8,128)(2,1)S(1)}, bf16[128,512]{1,0:T(8,128)(2,1)S(1)}, u32[]{:S(2)}, u32[]{:S(2)}) collective-permute-start(bf16[128,512]{1,0:T(8,128)(2,1)S(1)} %get-tuple-element.61), channel_id=1, source_target_pairs={{0,8},{1,9},{2,10},{3,11},{4,12},{5,13},{6,14},{7,15},{8,0},{9,1},... | collective-permute-start | bytes 393224 | tf_op jit(solution)/shard_map/ppermute | solution.py:267
  22.3 3.0 %collective-permute-start.11 = (bf16[384,512]{1,0:T(8,128)(2,1)S(1)}, bf16[384,512]{1,0:T(8,128)(2,1)S(1)}, u32[]{:S(2)}, u32[]{:S(2)}) collective-permute-start(bf16[384,512]{1,0:T(8,128)(2,1)S(1)} %get-tuple-element.57.refs_0_.refs_2_), channel_id=1, source_target_pairs={{0,2},{1,3},{2,0},{3,1},{4,6},{5,7},{6,4},{7,5},{8,10},{9,11},{10,... | collective-permute-start | bytes 1179656 | tf_op jit(solution)/shard_map/ppermute | solution.py:267
  25.5 3.1 %collective-permute-start.10 = (bf16[128,768]{1,0:T(8,128)(2,1)S(1)}, bf16[128,768]{1,0:T(8,128)(2,1)S(1)}, u32[]{:S(2)}, u32[]{:S(2)}) collective-permute-start(bf16[128,768]{1,0:T(8,128)(2,1)S(1)} %tick.12.refs_0_), channel_id=1, source_target_pairs={{0,12},{1,13},{2,14},{3,15},{4,8},{5,9},{6,10},{7,11},{8,4},{9,5},... | collective-permute-start | bytes 589832 | tf_op jit(solution)/shard_map/ppermute | solution.py:267
  30.6 3.4 %collective-permute-start.9 = (bf16[128,768]{1,0:T(8,128)(2,1)S(1)}, bf16[128,768]{1,0:T(8,128)(2,1)S(1)}, u32[]{:S(2)}, u32[]{:S(2)}) collective-permute-start(bf16[128,768]{1,0:T(8,128)(2,1)S(1)} %get-tuple-element.65), channel_id=1, source_target_pairs={{0,8},{1,9},{2,10},{3,11},{4,12},{5,13},{6,14},{7,15},{8,0},{9,1},... | collective-permute-start | bytes 589832 | tf_op jit(solution)/shard_map/ppermute | solution.py:267
  34.0 5.4 %collective-permute-start.13 = (bf16[384,512]{1,0:T(8,128)(2,1)S(1)}, bf16[384,512]{1,0:T(8,128)(2,1)S(1)}, u32[]{:S(2)}, u32[]{:S(2)}) collective-permute-start(bf16[384,512]{1,0:T(8,128)(2,1)S(1)} %get-tuple-element.66.refs_0_.refs_2_), channel_id=1, source_target_pairs={{0,2},{1,3},{2,0},{3,1},{4,6},{5,7},{6,4},{7,5},{8,10},{9,11},{10,... | collective-permute-start | bytes 1179656 | tf_op jit(solution)/shard_map/ppermute | solution.py:267
  39.6 1.7 %collective-permute-start.14 = (bf16[128,512]{1,0:T(8,128)(2,1)S(1)}, bf16[128,512]{1,0:T(8,128)(2,1)S(1)}, u32[]{:S(2)}, u32[]{:S(2)}) collective-permute-start(bf16[128,512]{1,0:T(8,128)(2,1)S(1)} %tick.16.refs_0_), channel_id=1, source_target_pairs={{0,12},{1,13},{2,14},{3,15},{4,8},{5,9},{6,10},{7,11},{8,4},{9,5},... | collective-permute-start | bytes 393224 | tf_op jit(solution)/shard_map/ppermute | solution.py:267
  41.3 8.7 %collective-permute-done.9.refs_4_.refs_2_ = bf16[128,768]{1,0:T(8,128)(2,1)S(1)} collective-permute-done((bf16[128,768]{1,0:T(8,128)(2,1)S(1)}, bf16[128,768]{1,0:T(8,128)(2,1)S(1)}, u32[]{:S(2)}, u32[]{:S(2)}) %collective-permute-start.9) | collective-permute-done | bytes 196640 | tf_op jit(solution)/shard_map/ppermute | solution.py:267
  50.3 3.4 %collective-permute-start.18 = (bf16[128,512]{1,0:T(8,128)(2,1)S(1)}, bf16[128,512]{1,0:T(8,128)(2,1)S(1)}, u32[]{:S(2)}, u32[]{:S(2)}) collective-permute-start(bf16[128,512]{1,0:T(8,128)(2,1)S(1)} %get-tuple-element.75), channel_id=1, source_target_pairs={{0,8},{1,9},{2,10},{3,11},{4,12},{5,13},{6,14},{7,15},{8,0},{9,1},... | collective-permute-start | bytes 393224 | tf_op jit(solution)/shard_map/ppermute | solution.py:267
  53.7 1.2 %collective-permute-start.16 = (bf16[384,512]{1,0:T(8,128)(2,1)S(1)}, bf16[384,512]{1,0:T(8,128)(2,1)S(1)}, u32[]{:S(2)}, u32[]{:S(2)}) collective-permute-start(bf16[384,512]{1,0:T(8,128)(2,1)S(1)} %get-tuple-element.70.refs_0_.refs_10_.refs_1_), channel_id=1, source_target_pairs={{0,2},{1,3},{2,0},{3,1},{4,6},{5,7},{6,4},{7,5},{8,10},{9,11},{10,... | collective-permute-start | bytes 1179656 | tf_op jit(solution)/shard_map/ppermute | solution.py:267
  55.0 3.7 %attend.3 = (bf16[128,256]{1,0:T(8,128)(2,1)S(1)}, bf16[128,256]{1,0:T(8,128)(2,1)S(1)}, bf16[128,256]{1,0:T(8,128)(2,1)S(1)}, bf16[128,256]{1,0:T(8,128)(2,1)S(1)}) custom-call(s32[2]{0:T(128)S(1)} %pad_add_fusion.scalars, bf16[128,768]{1,0:T(8,128)(2,1)S(1)} %get-tuple-element.53.refs_0_, bf16[128,768]{1,0:T(8,128)(2,1)S(1)} %collective-permute-done.8.refs_3_.refs_1_, ...), custom_call_target="tpu_custom_call" | custom-call | flops 20000000000 | bytes 1 | tf_op jit(solution)/shard_map/attend/pallas_call | solution.py:169
  58.7 3.8 %attend.4 = (bf16[128,256]{1,0:T(8,128)(2,1)S(1)}, bf16[128,256]{1,0:T(8,128)(2,1)S(1)}, bf16[128,256]{1,0:T(8,128)(2,1)S(1)}, bf16[128,256]{1,0:T(8,128)(2,1)S(1)}) custom-call(s32[2]{0:T(128)S(1)} %pad_add_fusion.scalars, bf16[128,512]{1,0:T(8,128)(2,1)S(1)} %get-tuple-element.73.refs_0_, bf16[128,512]{1,0:T(8,128)(2,1)S(1)} %collective-permute-done.17.refs_1_, ...), custom_call_target="tpu_custom_call" | custom-call | flops 20000000000 | bytes 1 | tf_op jit(solution)/shard_map/attend/pallas_call | solution.py:169
  63.7 2.4 %collective-permute-start.22 = (bf16[128,256]{1,0:T(8,128)(2,1)S(1)}, bf16[128,256]{1,0:T(8,128)(2,1)S(1)}, u32[]{:S(2)}, u32[]{:S(2)}) collective-permute-start(bf16[128,256]{1,0:T(8,128)(2,1)S(1)} %get-tuple-element.85), channel_id=1, source_target_pairs={{0,8},{1,9},{2,10},{3,11},{4,12},{5,13},{6,14},{7,15},{8,0},{9,1},... | collective-permute-start | bytes 196616 | tf_op jit(solution)/shard_map/ppermute | solution.py:267
  66.2 1.9 %collective-permute-start.21 = (bf16[128,512]{1,0:T(8,128)(2,1)S(1)}, bf16[128,512]{1,0:T(8,128)(2,1)S(1)}, u32[]{:S(2)}, u32[]{:S(2)}) collective-permute-start(bf16[128,512]{1,0:T(8,128)(2,1)S(1)} %get-tuple-element.84), channel_id=1, source_target_pairs={{0,12},{1,13},{2,14},{3,15},{4,8},{5,9},{6,10},{7,11},{8,4},{9,5},... | collective-permute-start | bytes 393224 | tf_op jit(solution)/shard_map/ppermute | solution.py:267
  68.1 3.8 %attend.5 = (bf16[128,256]{1,0:T(8,128)(2,1)S(1)}, bf16[128,256]{1,0:T(8,128)(2,1)S(1)}, bf16[128,256]{1,0:T(8,128)(2,1)S(1)}, bf16[128,256]{1,0:T(8,128)(2,1)S(1)}) custom-call(s32[2]{0:T(128)S(1)} %pad_add_fusion.scalars, bf16[128,512]{1,0:T(8,128)(2,1)S(1)} %get-tuple-element.73.refs_0_, bf16[128,512]{1,0:T(8,128)(2,1)S(1)} %collective-permute-done.17.refs_1_, ...), custom_call_target="tpu_custom_call" | custom-call | flops 20000000000 | bytes 1 | tf_op jit(solution)/shard_map/attend/pallas_call | solution.py:169
  73.0 1.5 %collective-permute-start.25 = (bf16[128,256]{1,0:T(8,128)(2,1)S(1)}, bf16[128,256]{1,0:T(8,128)(2,1)S(1)}, u32[]{:S(2)}, u32[]{:S(2)}) collective-permute-start(bf16[128,256]{1,0:T(8,128)(2,1)S(1)} %get-tuple-element.89), channel_id=1, source_target_pairs={{0,8},{1,9},{2,10},{3,11},{4,12},{5,13},{6,14},{7,15},{8,0},{9,1},... | collective-permute-start | bytes 196616 | tf_op jit(solution)/shard_map/ppermute | solution.py:267
  74.5 1.9 %collective-permute-start.26 = (bf16[128,256]{1,0:T(8,128)(2,1)S(1)}, bf16[128,256]{1,0:T(8,128)(2,1)S(1)}, u32[]{:S(2)}, u32[]{:S(2)}) collective-permute-start(bf16[128,256]{1,0:T(8,128)(2,1)S(1)} %get-tuple-element.90), channel_id=1, source_target_pairs={{0,12},{1,13},{2,14},{3,15},{4,8},{5,9},{6,10},{7,11},{8,4},{9,5},... | collective-permute-start | bytes 196616 | tf_op jit(solution)/shard_map/ppermute | solution.py:267
  77.5 4.4 %collective-permute-done.25.refs_7_ = bf16[128,256]{1,0:T(8,128)(2,1)S(1)} collective-permute-done((bf16[128,256]{1,0:T(8,128)(2,1)S(1)}, bf16[128,256]{1,0:T(8,128)(2,1)S(1)}, u32[]{:S(2)}, u32[]{:S(2)}) %collective-permute-start.25) | collective-permute-done | bytes 65568 | tf_op jit(solution)/shard_map/ppermute | solution.py:267
  (67 shorter events, 9.8 us)
Async XLA Ops:
  2.4 13.3 %collective-permute-start = (bf16[128,512]{1,0:T(8,128)(2,1)S(1)}, bf16[128,512]{1,0:T(8,128)(2,1)S(1)}, u32[]{:S(2)}, u32[]{:S(2)}) collective-permute-start(bf16[128,512]{1,0:T(8,128)(2,1)S(1)} %get-tuple-element.51.refs_6_), channel_id=1, source_target_pairs={{0,12},{1,13},{2,14},{3,15},{4,8},{5,9},{6,10},{7,11},{8,4},{9,5},... | collective-permute-start | bytes 393224 | tf_op jit(solution)/shard_map/ppermute | solution.py:267
  7.5 11.8 %collective-permute-start.1 = (bf16[128,512]{1,0:T(8,128)(2,1)S(1)}, bf16[128,512]{1,0:T(8,128)(2,1)S(1)}, u32[]{:S(2)}, u32[]{:S(2)}) collective-permute-start(bf16[128,512]{1,0:T(8,128)(2,1)S(1)} %get-tuple-element.49.refs_4_), channel_id=1, source_target_pairs={{0,4},{1,5},{2,6},{3,7},{4,0},{5,1},{6,2},{7,3},{8,12},{9,13},{10,... | collective-permute-start | bytes 393224 | tf_op jit(solution)/shard_map/ppermute | solution.py:267
  7.5 11.8 %collective-permute-start.2 = (bf16[128,512]{1,0:T(8,128)(2,1)S(1)}, bf16[128,512]{1,0:T(8,128)(2,1)S(1)}, u32[]{:S(2)}, u32[]{:S(2)}) collective-permute-start(bf16[128,512]{1,0:T(8,128)(2,1)S(1)} %get-tuple-element.50.refs_5_), channel_id=1, source_target_pairs={{0,8},{1,9},{2,10},{3,11},{4,12},{5,13},{6,14},{7,15},{8,0},{9,1},... | collective-permute-start | bytes 393224 | tf_op jit(solution)/shard_map/ppermute | solution.py:267
  8.1 17.2 %collective-permute-start.4 = (bf16[128,1536]{1,0:T(8,128)(2,1)S(1)}, bf16[128,1536]{1,0:T(8,128)(2,1)S(1)}, u32[]{:S(2)}, u32[]{:S(2)}) collective-permute-start(bf16[128,1536]{1,0:T(8,128)(2,1)S(1)} %get-tuple-element.59.refs_1_.refs_5_), channel_id=1, source_target_pairs={{0,2},{1,3},{2,0},{3,1},{4,6},{5,7},{6,4},{7,5},{8,10},{9,11},{10,... | collective-permute-start | bytes 1179656 | tf_op jit(solution)/shard_map/ppermute | solution.py:267
  15.7 9.8 %collective-permute-start.3 = (bf16[128,512]{1,0:T(8,128)(2,1)S(1)}, bf16[128,512]{1,0:T(8,128)(2,1)S(1)}, u32[]{:S(2)}, u32[]{:S(2)}) collective-permute-start(bf16[128,512]{1,0:T(8,128)(2,1)S(1)} %tick.10.refs_0_), channel_id=1, source_target_pairs={{0,12},{1,13},{2,14},{3,15},{4,8},{5,9},{6,10},{7,11},{8,4},{9,5},... | collective-permute-start | bytes 393224 | tf_op jit(solution)/shard_map/ppermute | solution.py:267
  19.4 9.9 %collective-permute-start.6 = (bf16[128,512]{1,0:T(8,128)(2,1)S(1)}, bf16[128,512]{1,0:T(8,128)(2,1)S(1)}, u32[]{:S(2)}, u32[]{:S(2)}) collective-permute-start(bf16[128,512]{1,0:T(8,128)(2,1)S(1)} %get-tuple-element.60), channel_id=1, source_target_pairs={{0,4},{1,5},{2,6},{3,7},{4,0},{5,1},{6,2},{7,3},{8,12},{9,13},{10,... | collective-permute-start | bytes 393224 | tf_op jit(solution)/shard_map/ppermute | solution.py:267
  19.5 10.9 %collective-permute-start.7 = (bf16[128,512]{1,0:T(8,128)(2,1)S(1)}, bf16[128,512]{1,0:T(8,128)(2,1)S(1)}, u32[]{:S(2)}, u32[]{:S(2)}) collective-permute-start(bf16[128,512]{1,0:T(8,128)(2,1)S(1)} %get-tuple-element.61), channel_id=1, source_target_pairs={{0,8},{1,9},{2,10},{3,11},{4,12},{5,13},{6,14},{7,15},{8,0},{9,1},... | collective-permute-start | bytes 393224 | tf_op jit(solution)/shard_map/ppermute | solution.py:267
  22.3 17.1 %collective-permute-start.11 = (bf16[384,512]{1,0:T(8,128)(2,1)S(1)}, bf16[384,512]{1,0:T(8,128)(2,1)S(1)}, u32[]{:S(2)}, u32[]{:S(2)}) collective-permute-start(bf16[384,512]{1,0:T(8,128)(2,1)S(1)} %get-tuple-element.57.refs_0_.refs_2_), channel_id=1, source_target_pairs={{0,2},{1,3},{2,0},{3,1},{4,6},{5,7},{6,4},{7,5},{8,10},{9,11},{10,... | collective-permute-start | bytes 1179656 | tf_op jit(solution)/shard_map/ppermute | solution.py:267
  25.5 14.0 %collective-permute-start.10 = (bf16[128,768]{1,0:T(8,128)(2,1)S(1)}, bf16[128,768]{1,0:T(8,128)(2,1)S(1)}, u32[]{:S(2)}, u32[]{:S(2)}) collective-permute-start(bf16[128,768]{1,0:T(8,128)(2,1)S(1)} %tick.12.refs_0_), channel_id=1, source_target_pairs={{0,12},{1,13},{2,14},{3,15},{4,8},{5,9},{6,10},{7,11},{8,4},{9,5},... | collective-permute-start | bytes 589832 | tf_op jit(solution)/shard_map/ppermute | solution.py:267
  30.4 10.9 %collective-permute-start.8 = (bf16[128,768]{1,0:T(8,128)(2,1)S(1)}, bf16[128,768]{1,0:T(8,128)(2,1)S(1)}, u32[]{:S(2)}, u32[]{:S(2)}) collective-permute-start(bf16[128,768]{1,0:T(8,128)(2,1)S(1)} %get-tuple-element.64), channel_id=1, source_target_pairs={{0,4},{1,5},{2,6},{3,7},{4,0},{5,1},{6,2},{7,3},{8,12},{9,13},{10,... | collective-permute-start | bytes 589832 | tf_op jit(solution)/shard_map/ppermute | solution.py:267
  30.6 19.4 %collective-permute-start.9 = (bf16[128,768]{1,0:T(8,128)(2,1)S(1)}, bf16[128,768]{1,0:T(8,128)(2,1)S(1)}, u32[]{:S(2)}, u32[]{:S(2)}) collective-permute-start(bf16[128,768]{1,0:T(8,128)(2,1)S(1)} %get-tuple-element.65), channel_id=1, source_target_pairs={{0,8},{1,9},{2,10},{3,11},{4,12},{5,13},{6,14},{7,15},{8,0},{9,1},... | collective-permute-start | bytes 589832 | tf_op jit(solution)/shard_map/ppermute | solution.py:267
  34.0 20.8 %collective-permute-start.13 = (bf16[384,512]{1,0:T(8,128)(2,1)S(1)}, bf16[384,512]{1,0:T(8,128)(2,1)S(1)}, u32[]{:S(2)}, u32[]{:S(2)}) collective-permute-start(bf16[384,512]{1,0:T(8,128)(2,1)S(1)} %get-tuple-element.66.refs_0_.refs_2_), channel_id=1, source_target_pairs={{0,2},{1,3},{2,0},{3,1},{4,6},{5,7},{6,4},{7,5},{8,10},{9,11},{10,... | collective-permute-start | bytes 1179656 | tf_op jit(solution)/shard_map/ppermute | solution.py:267
  39.5 10.6 %collective-permute-start.12 = (bf16[768,512]{1,0:T(8,128)(2,1)S(1)}, bf16[768,512]{1,0:T(8,128)(2,1)S(1)}, u32[]{:S(2)}, u32[]{:S(2)}) collective-permute-start(bf16[768,512]{1,0:T(8,128)(2,1)S(1)} %tick.15.refs_4_), channel_id=1, source_target_pairs={{0,1},{1,0},{2,3},{3,2},{4,5},{5,4},{6,7},{7,6},{8,9},{9,8},{10,11... | collective-permute-start | bytes 2359304 | tf_op jit(solution)/shard_map/ppermute | solution.py:267
  39.6 15.4 %collective-permute-start.14 = (bf16[128,512]{1,0:T(8,128)(2,1)S(1)}, bf16[128,512]{1,0:T(8,128)(2,1)S(1)}, u32[]{:S(2)}, u32[]{:S(2)}) collective-permute-start(bf16[128,512]{1,0:T(8,128)(2,1)S(1)} %tick.16.refs_0_), channel_id=1, source_target_pairs={{0,12},{1,13},{2,14},{3,15},{4,8},{5,9},{6,10},{7,11},{8,4},{9,5},... | collective-permute-start | bytes 393224 | tf_op jit(solution)/shard_map/ppermute | solution.py:267
  50.1 8.6 %collective-permute-start.17 = (bf16[128,512]{1,0:T(8,128)(2,1)S(1)}, bf16[128,512]{1,0:T(8,128)(2,1)S(1)}, u32[]{:S(2)}, u32[]{:S(2)}) collective-permute-start(bf16[128,512]{1,0:T(8,128)(2,1)S(1)} %get-tuple-element.74), channel_id=1, source_target_pairs={{0,4},{1,5},{2,6},{3,7},{4,0},{5,1},{6,2},{7,3},{8,12},{9,13},{10,... | collective-permute-start | bytes 393224 | tf_op jit(solution)/shard_map/ppermute | solution.py:267
  50.3 8.4 %collective-permute-start.18 = (bf16[128,512]{1,0:T(8,128)(2,1)S(1)}, bf16[128,512]{1,0:T(8,128)(2,1)S(1)}, u32[]{:S(2)}, u32[]{:S(2)}) collective-permute-start(bf16[128,512]{1,0:T(8,128)(2,1)S(1)} %get-tuple-element.75), channel_id=1, source_target_pairs={{0,8},{1,9},{2,10},{3,11},{4,12},{5,13},{6,14},{7,15},{8,0},{9,1},... | collective-permute-start | bytes 393224 | tf_op jit(solution)/shard_map/ppermute | solution.py:267
  53.7 8.9 %collective-permute-start.16 = (bf16[384,512]{1,0:T(8,128)(2,1)S(1)}, bf16[384,512]{1,0:T(8,128)(2,1)S(1)}, u32[]{:S(2)}, u32[]{:S(2)}) collective-permute-start(bf16[384,512]{1,0:T(8,128)(2,1)S(1)} %get-tuple-element.70.refs_0_.refs_10_.refs_1_), channel_id=1, source_target_pairs={{0,2},{1,3},{2,0},{3,1},{4,6},{5,7},{6,4},{7,5},{8,10},{9,11},{10,... | collective-permute-start | bytes 1179656 | tf_op jit(solution)/shard_map/ppermute | solution.py:267
  63.2 9.8 %collective-permute-start.15 = (bf16[128,256]{1,0:T(8,128)(2,1)S(1)}, bf16[128,256]{1,0:T(8,128)(2,1)S(1)}, u32[]{:S(2)}, u32[]{:S(2)}) collective-permute-start(bf16[128,256]{1,0:T(8,128)(2,1)S(1)} %get-tuple-element.71), channel_id=1, source_target_pairs={{0,8},{1,9},{2,10},{3,11},{4,12},{5,13},{6,14},{7,15},{8,0},{9,1},... | collective-permute-start | bytes 196616 | tf_op jit(solution)/shard_map/ppermute | solution.py:267
  63.7 10.8 %collective-permute-start.22 = (bf16[128,256]{1,0:T(8,128)(2,1)S(1)}, bf16[128,256]{1,0:T(8,128)(2,1)S(1)}, u32[]{:S(2)}, u32[]{:S(2)}) collective-permute-start(bf16[128,256]{1,0:T(8,128)(2,1)S(1)} %get-tuple-element.85), channel_id=1, source_target_pairs={{0,8},{1,9},{2,10},{3,11},{4,12},{5,13},{6,14},{7,15},{8,0},{9,1},... | collective-permute-start | bytes 196616 | tf_op jit(solution)/shard_map/ppermute | solution.py:267
  66.1 10.3 %collective-permute-start.20 = (bf16[128,512]{1,0:T(8,128)(2,1)S(1)}, bf16[128,512]{1,0:T(8,128)(2,1)S(1)}, u32[]{:S(2)}, u32[]{:S(2)}) collective-permute-start(bf16[128,512]{1,0:T(8,128)(2,1)S(1)} %get-tuple-element.83), channel_id=1, source_target_pairs={{0,4},{1,5},{2,6},{3,7},{4,0},{5,1},{6,2},{7,3},{8,12},{9,13},{10,... | collective-permute-start | bytes 393224 | tf_op jit(solution)/shard_map/ppermute | solution.py:267
  66.2 10.3 %collective-permute-start.21 = (bf16[128,512]{1,0:T(8,128)(2,1)S(1)}, bf16[128,512]{1,0:T(8,128)(2,1)S(1)}, u32[]{:S(2)}, u32[]{:S(2)}) collective-permute-start(bf16[128,512]{1,0:T(8,128)(2,1)S(1)} %get-tuple-element.84), channel_id=1, source_target_pairs={{0,12},{1,13},{2,14},{3,15},{4,8},{5,9},{6,10},{7,11},{8,4},{9,5},... | collective-permute-start | bytes 393224 | tf_op jit(solution)/shard_map/ppermute | solution.py:267
  71.9 5.6 %collective-permute-start.24 = (bf16[128,256]{1,0:T(8,128)(2,1)S(1)}, bf16[128,256]{1,0:T(8,128)(2,1)S(1)}, u32[]{:S(2)}, u32[]{:S(2)}) collective-permute-start(bf16[128,256]{1,0:T(8,128)(2,1)S(1)} %get-tuple-element.88), channel_id=1, source_target_pairs={{0,4},{1,5},{2,6},{3,7},{4,0},{5,1},{6,2},{7,3},{8,12},{9,13},{10,... | collective-permute-start | bytes 196616 | tf_op jit(solution)/shard_map/ppermute | solution.py:267
  73.0 9.0 %collective-permute-start.25 = (bf16[128,256]{1,0:T(8,128)(2,1)S(1)}, bf16[128,256]{1,0:T(8,128)(2,1)S(1)}, u32[]{:S(2)}, u32[]{:S(2)}) collective-permute-start(bf16[128,256]{1,0:T(8,128)(2,1)S(1)} %get-tuple-element.89), channel_id=1, source_target_pairs={{0,8},{1,9},{2,10},{3,11},{4,12},{5,13},{6,14},{7,15},{8,0},{9,1},... | collective-permute-start | bytes 196616 | tf_op jit(solution)/shard_map/ppermute | solution.py:267
  74.5 7.4 %collective-permute-start.26 = (bf16[128,256]{1,0:T(8,128)(2,1)S(1)}, bf16[128,256]{1,0:T(8,128)(2,1)S(1)}, u32[]{:S(2)}, u32[]{:S(2)}) collective-permute-start(bf16[128,256]{1,0:T(8,128)(2,1)S(1)} %get-tuple-element.90), channel_id=1, source_target_pairs={{0,12},{1,13},{2,14},{3,15},{4,8},{5,9},{6,10},{7,11},{8,4},{9,5},... | collective-permute-start | bytes 196616 | tf_op jit(solution)/shard_map/ppermute | solution.py:267
  (12 other events, 46.9 us)
